TPU v7x, 128 devices: a whole 4x4x4 slice. The times are simulated.
128 devices in a mesh: dp: 64 (over z_hi, x, y, core), expert: 2 (over z_lo).
Axes of the slice: x: 4, y: 4, z: 4 (z_hi: 2, z_lo: 2; z = z_hi * 2 + z_lo), core: 2. Of those that a mesh axis runs over, the one named last changes fastest.
Arguments:
- hidden_in: bfloat16 [32768, 1536], P(('dp', 'expert')), may hold values from -6 to 6
- out_grad: bfloat16 [32768, 1536], P(('dp', 'expert')), may hold values from -6 to 6
- doc_lengths: int32 [128, 4], P(('dp', 'expert')), may hold values from 1 to 192, 256 in all within a row
- expert_ids: int32 [32768, 6], P(('dp', 'expert')), may hold values from 0 to 63, all different within a row; in each aligned block of 256 rows (0 to 255, 256 to 511, ...) at most 32 rows name the same one
- gain_attn: bfloat16 [1536], P(('dp', 'expert')), may hold values from 0.5 to 1.5
- w_query: bfloat16 [1536, 1536], P(('dp', 'expert')), may hold values from -0.15625 to 0.15625
- key_weight_shard: bfloat16 [1536, 512], P(('dp', 'expert')), may hold values from -0.15625 to 0.15625
- value_weight_shard: bfloat16 [1536, 512], P(('dp', 'expert')), may hold values from -0.15625 to 0.15625
- w_out: bfloat16 [1536, 1536], P(('dp', 'expert')), may hold values from -0.875 to 0.875
- gain_ffn: bfloat16 [1536], P(('dp', 'expert')), may hold values from 0.5 to 1.5
- w_router: bfloat16 [1536, 64], P(('dp', 'expert')), may hold values from -0.078125 to 0.078125
- w_shared_gate: bfloat16 [1536, 1024], P(('dp', 'expert')), may hold values from -0.15625 to 0.15625
- w_shared_up: bfloat16 [1536, 1024], P(('dp', 'expert')), may hold values from -0.15625 to 0.15625
- w_shared_down: bfloat16 [1024, 1536], P(('dp', 'expert')), may hold values from -0.1875 to 0.1875
- expert_gate: bfloat16 [64, 1536, 512], P('dp', None, 'expert'), may hold values from -0.15625 to 0.15625
- expert_up: bfloat16 [64, 1536, 512], P('dp', None, 'expert'), may hold values from -0.15625 to 0.15625
- expert_down: bfloat16 [64, 512, 1536], P('dp', 'expert'), may hold values from -0.75 to 0.75
Outputs:
- block_out: bfloat16 [32768, 1536], P(('dp', 'expert'))
- grad_in: float32 [32768, 1536], P(('dp', 'expert'))
- grad_gain_attn: float32 [1536], P(('dp', 'expert'))
- grad_w_query: float32 [1536, 1536], P(('dp', 'expert'))
- grad_w_key: float32 [1536, 512], P(('dp', 'expert'))
- grad_w_value: float32 [1536, 512], P(('dp', 'expert'))
- grad_w_out: float32 [1536, 1536], P(('dp', 'expert'))
- grad_gain_ffn: float32 [1536], P(('dp', 'expert'))
- grad_w_router: float32 [1536, 64], P(('dp', 'expert'))
- grad_w_shared_gate: float32 [1536, 1024], P(('dp', 'expert'))
- grad_w_shared_up: float32 [1536, 1024], P(('dp', 'expert'))
- grad_w_shared_down: float32 [1024, 1536], P(('dp', 'expert'))
- grad_expert_gate: float32 [64, 1536, 512], P('dp', None, 'expert')
- grad_expert_up: float32 [64, 1536, 512], P('dp', None, 'expert')
- grad_expert_down: float32 [64, 512, 1536], P('dp', 'expert')
Inputs may be any that keep to these rules, and one draw needn't show every extreme that they name: `doc_lengths`: each row holds the lengths of the 4 documents of one device's 256 tokens; they sum to 256 and the longest is 192. `expert_ids`: each row names 6 different experts. Among the rows of one device no expert is named more than 32 times, and on some device one expert is named exactly 32 times.
All inputs are finite; a program needn't handle non-finite values.
Results may differ from a plain program's by a relative error of at most 0.02.
Values may be sent and summed in bfloat16 or wider, within the bound.
No kernel may reach another device: no remote copies, remote signals or barrier semaphores. Data moves between devices by JAX's collectives and lax.ppermute only.
A program may use at most 320 MiB of HBM per device.

v0:
```python
import functools

import jax
import jax.numpy as jnp
from jax import lax
from jax.experimental import pallas as pl
from jax.experimental.pallas import tpu as pltpu
from jax.sharding import Mesh, PartitionSpec as P

GROUP = 3
HEAD = 128
EXPERTS = 64
SLOTS = 32
TOKENS = 256
WIDTH = 1536
SHARED = 1024
HALF = 256
ROWS = EXPERTS * SLOTS
WIDE = WIDTH + 128
PACK = 2 * WIDTH + 1024 + 128

EPSILON = 1e-06
NEGATIVE = -1e30
SCALING = HEAD ** (-0.5)
BF = jnp.bfloat16
F32 = jnp.float32

AXES = ("zh", "x", "y", "c", "zl")
DP = ("zh", "x", "y", "c")
PLANE = ("x", "y", "c")
ANY = pl.BlockSpec(memory_space=pl.ANY)


def mm(a, b):
    return jnp.dot(a, b, preferred_element_type=F32)


def mm_l(a, b):
    return lax.dot_general(a, b, (((0,), (0,)), ((), ())), preferred_element_type=F32)


def mm_r(a, b):
    return lax.dot_general(a, b, (((1,), (1,)), ((), ())), preferred_element_type=F32)


def swap(x, axis):
    return lax.ppermute(x, axis, [(0, 1), (1, 0)])


def out(shape, dtype):
    return jax.ShapeDtypeStruct(shape, dtype)


def full(shape):
    return pl.BlockSpec(shape, lambda *i: (0,) * len(shape))


def call(kernel, grid, in_specs, out_specs, out_shape, scratch=(), flops=0):
    return pl.pallas_call(
        kernel,
        grid=grid,
        in_specs=in_specs,
        out_specs=out_specs,
        out_shape=out_shape,
        scratch_shapes=list(scratch),
        compiler_params=pltpu.CompilerParams(vmem_limit_bytes=56 * 1024 * 1024),
        cost_estimate=pl.CostEstimate(flops=flops, bytes_accessed=0, transcendentals=0),
    )


def gather_plane(four):
    _, rows, width = four.shape
    whole = lax.all_gather(four.reshape(2, 2 * rows, width), PLANE, axis=1, tiled=True)
    return whole.reshape(128 * rows, width)


def scatter_plane(grads):
    return lax.psum_scatter(grads, PLANE, scatter_dimension=0, tiled=True)


def scatter_line(plane):
    r, width = plane.shape[0] // 2, plane.shape[1] // 2
    zh = lax.axis_index("zh")
    zl = lax.axis_index("zl")
    low, high = plane[:, :width], plane[:, width:]
    keep = jnp.where(zh == 0, low, high)
    give = jnp.where(zh == 0, high, low)
    pair = keep.astype(F32) + swap(give, "zh").astype(F32)
    keep = jnp.where(zl == 0, pair[:r], pair[r:])
    give = jnp.where(zl == 0, pair[r:], pair[:r]).astype(BF)
    return keep + swap(give, "zl").astype(F32)


def one_hot(rank_ref):
    rank = rank_ref[...]
    slot = lax.broadcasted_iota(jnp.int32, (8, SLOTS, TOKENS), 1).astype(F32)
    hit = jnp.where(rank[:, None, :] == slot, 1.0, 0.0)
    return hit.reshape(8 * SLOTS, TOKENS).astype(BF)


def dispatch_kernel(n, rank_ref, rows_ref, *refs):
    refs[n][...] = mm(one_hot(rank_ref), rows_ref[...]).astype(BF)


def dispatch(rank, rows, *after):
    width = rows.shape[1]
    return call(
        functools.partial(dispatch_kernel, len(after)),
        (8,),
        [pl.BlockSpec((8, TOKENS), lambda i: (i, 0)), full((TOKENS, width))]
        + [ANY] * len(after),
        pl.BlockSpec((8 * SLOTS, width), lambda i: (i, 0)),
        out((ROWS, width), BF),
    )(rank, rows, *after)


def to_experts(rows):
    return lax.all_to_all(
        rows.reshape(EXPERTS, SLOTS, -1), DP, split_axis=0, concat_axis=0, tiled=True
    ).reshape(ROWS, -1)


def result_kernel(rank_ref, rows_ref, base_ref, out_ref, acc):
    step = pl.program_id(0)

    @pl.when(step == 0)
    def _():
        acc[...] = base_ref[...]

    acc[...] += mm_l(one_hot(rank_ref), rows_ref[...])

    @pl.when(step == 7)
    def _():
        out_ref[...] = acc[...].astype(BF)


def add_results(rank, rows, base):
    return call(
        result_kernel,
        (8,),
        [
            pl.BlockSpec((8, TOKENS), lambda i: (i, 0)),
            pl.BlockSpec((8 * SLOTS, WIDTH), lambda i: (i, 0)),
            full((TOKENS, WIDTH)),
        ],
        full((TOKENS, WIDTH)),
        out((TOKENS, WIDTH), BF),
        [pltpu.VMEM((TOKENS, WIDTH), F32)],
    )(rank, rows, base)


def root_scale(values):
    return lax.rsqrt(jnp.mean(values * values, axis=-1, keepdims=True) + EPSILON)


def forward_kernel(
    hidden_ref,
    docs_ref,
    hits_ref,
    wq_ref,
    wo_ref,
    wkv_ref,
    small_ref,
    attn_in_ref,
    q_ref,
    kv_ref,
    probs_ref,
    attended_ref,
    middle_ref,
    ffn_in_ref,
    gates_ref,
    gains_ref,
):
    gains = jnp.transpose(small_ref[...].astype(F32))
    gains_ref[...] = gains[64:72]
    gain_one, gain_two = gains[64:65], gains[65:66]
    tokens = hidden_ref[...].astype(F32)
    attn_in_ref[...] = (tokens * root_scale(tokens) * gain_one).astype(BF)
    for j in range(0, WIDTH, 512):
        q_ref[:, j : j + 512] = mm(attn_in_ref[...], wq_ref[:, j : j + 512]).astype(BF)
    for j in range(0, 1024, 512):
        kv_ref[:, j : j + 512] = mm(attn_in_ref[...], wkv_ref[:, j : j + 512]).astype(BF)
    first = docs_ref[0, 0]
    second = first + docs_ref[0, 1]
    third = second + docs_ref[0, 2]
    row = lax.broadcasted_iota(jnp.int32, (TOKENS, TOKENS), 0)
    col = lax.broadcasted_iota(jnp.int32, (TOKENS, TOKENS), 1)

    def segment(place):
        return (
            (place >= first).astype(jnp.int32)
            + (place >= second).astype(jnp.int32)
            + (place >= third).astype(jnp.int32)
        )

    visible = (segment(row) == segment(col)) & (row >= col)
    for kv_head in range(4):
        key = kv_ref[:, kv_head * HEAD : (kv_head + 1) * HEAD]
        value = kv_ref[:, 512 + kv_head * HEAD : 512 + (kv_head + 1) * HEAD]
        for head in range(kv_head * GROUP, (kv_head + 1) * GROUP):
            at = slice(head * HEAD, (head + 1) * HEAD)
            scores = jnp.where(visible, mm_r(q_ref[:, at], key) * SCALING, NEGATIVE)
            exponent = jnp.exp(scores - jnp.max(scores, axis=-1, keepdims=True))
            probs = exponent / jnp.sum(exponent, axis=-1, keepdims=True)
            probs_ref[head] = probs
            attended_ref[:, at] = mm(probs.astype(BF), value).astype(BF)
    for j in range(0, WIDTH, 512):
        at = slice(j, j + 512)
        middle_ref[:, at] = hidden_ref[:, at].astype(F32) + mm(
            attended_ref[...], wo_ref[:, at]
        )
    middle = middle_ref[...]
    ffn_in_ref[...] = (middle * root_scale(middle) * gain_two).astype(BF)
    logits = mm(ffn_in_ref[...], small_ref[...])
    hits = hits_ref[...] > 0
    top = jnp.max(jnp.where(hits, logits, NEGATIVE), axis=-1, keepdims=True)
    weight = jnp.where(hits, jnp.exp(jnp.where(hits, logits - top, 0.0)), 0.0)
    gates_ref[...] = weight / jnp.sum(weight, axis=-1, keepdims=True)


def pack_specs():
    return [
        pl.BlockSpec((WIDTH, WIDTH), lambda *i: (0, 0)),
        pl.BlockSpec((WIDTH, WIDTH), lambda *i: (0, 1)),
        pl.BlockSpec((WIDTH, 1024), lambda *i: (0, 3)),
        pl.BlockSpec((WIDTH, 128), lambda *i: (0, 32)),
    ]


def forward(hidden, docs, hits, pack):
    wide = (TOKENS, WIDTH)
    shapes = [
        (wide, BF),
        (wide, BF),
        ((TOKENS, 1024), BF),
        ((12, TOKENS, TOKENS), F32),
        (wide, BF),
        (wide, F32),
        (wide, BF),
        ((TOKENS, 128), F32),
        ((8, WIDTH), F32),
    ]
    return call(
        forward_kernel,
        (1,),
        [full(wide), pl.BlockSpec(memory_space=pltpu.SMEM), full((TOKENS, 128))] + pack_specs(),
        [full(s) for s, _ in shapes],
        [out(s, d) for s, d in shapes],
    )(hidden, docs, hits, pack, pack, pack, pack)


def act_cot_kernel(cot_ref, down_ref, other_ref, out_ref):
    out_ref[:, :HALF] = mm_r(cot_ref[...], down_ref[...])
    out_ref[:, HALF:] = mm_r(cot_ref[...], other_ref[...])


def act_cots(cot_rows, down, other):
    return call(
        act_cot_kernel,
        (8,),
        [pl.BlockSpec((256, WIDTH), lambda i: (i, 0)), full((HALF, WIDTH)), full((HALF, WIDTH))],
        pl.BlockSpec((256, 2 * HALF), lambda i: (i, 0)),
        out((ROWS, 2 * HALF), F32),
    )(cot_rows, down, other)


def expert_kernel(
    rows_ref,
    marks_ref,
    act_cot_ref,
    own_ref,
    small_ref,
    gate_ref,
    gate_other_ref,
    up_ref,
    up_other_ref,
    _after_ref,
    back_ref,
    act_ref,
    gate_cot_ref,
    up_cot_ref,
):
    rows = rows_ref[...]
    marks = marks_ref[...] > 0
    logits = mm(rows, small_ref[...])
    top = jnp.max(jnp.where(marks, logits, NEGATIVE), axis=-1, keepdims=True)
    weight = jnp.where(marks, jnp.exp(jnp.where(marks, logits - top, 0.0)), 0.0)
    own = own_ref[...]
    total = jnp.sum(weight, axis=-1, keepdims=True)
    mine = jnp.sum(weight * own, axis=-1, keepdims=True)
    route_gate = mine / jnp.where(total > 0, total, 1.0)
    share = jnp.zeros((256, 1), F32)
    for half, gate_w, up_w in ((0, gate_ref, up_ref), (1, gate_other_ref, up_other_ref)):
        at = slice(half * HALF, (half + 1) * HALF)
        gate = mm(rows, gate_w[...])
        upper = mm(rows, up_w[...])
        sig = 1.0 / (1.0 + jnp.exp(-gate))
        silu = gate * sig
        act_cot = act_cot_ref[:, at]
        act = route_gate * silu * upper
        act_ref[:, at] = act.astype(BF)
        share += jnp.sum(act_cot * act, axis=-1, keepdims=True)
        scaled = route_gate * act_cot
        gate_cot_ref[:, at] = (scaled * upper * (sig * (1.0 + gate * (1.0 - sig)))).astype(BF)
        up_cot_ref[:, at] = (scaled * silu).astype(BF)
    for j in range(0, WIDTH, 512):
        at = slice(j, j + 512)
        total = mm_r(gate_cot_ref[:, :HALF], gate_ref[at, :])
        total += mm_r(gate_cot_ref[:, HALF:], gate_other_ref[at, :])
        total += mm_r(up_cot_ref[:, :HALF], up_ref[at, :])
        total += mm_r(up_cot_ref[:, HALF:], up_other_ref[at, :])
        back_ref[:, at] = total.astype(BF)
    high = share.astype(BF).astype(F32)
    lane = lax.broadcasted_iota(jnp.int32, (1, 128), 1)
    placed = jnp.where(lane < 64, high, share - high) * (own + pltpu.roll(own, 64, 1))
    back_ref[:, WIDTH:] = placed.astype(BF)


def expert_phase(rows, cot_rows, act_cot, own, pack, gate, gate_other, up, up_other, after):
    tile = lambda w, j=0: pl.BlockSpec((256, w), lambda i: (i, j))
    weight = full((WIDTH, HALF))
    return call(
        expert_kernel,
        (8,),
        [tile(WIDTH), tile(128, 12), tile(512), full((1, 128)), pack_specs()[3]]
        + [weight] * 4
        + [ANY],
        [tile(WIDE), tile(512), tile(512), tile(512)],
        [out((ROWS, WIDE), BF)] + [out((ROWS, 512), BF)] * 3,
    )(rows, cot_rows, act_cot, own, pack, gate, gate_other, up, up_other, after)


def expert_out_kernel(act_ref, down_ref, other_ref, _after_ref, out_ref):
    total = mm(act_ref[:, :HALF], down_ref[...]) + mm(act_ref[:, HALF:], other_ref[...])
    out_ref[...] = total.astype(BF)


def expert_outs(act, down, other, after):
    return call(
        expert_out_kernel,
        (8,),
        [
            pl.BlockSpec((256, 512), lambda i: (i, 0)),
            full((HALF, WIDTH)),
            full((HALF, WIDTH)),
            ANY,
        ],
        pl.BlockSpec((256, WIDTH), lambda i: (i, 0)),
        out((ROWS, WIDTH), BF),
    )(act, down, other, after)


def expert_grad_kernel(
    rows_ref, cot_ref, act_ref, gate_cot_ref, up_cot_ref, _after_ref, gate_ref, up_ref, down_ref, gate, up, down
):
    step = pl.program_id(0)

    @pl.when(step == 0)
    def _():
        gate[...] = jnp.zeros_like(gate)
        up[...] = jnp.zeros_like(up)
        down[...] = jnp.zeros_like(down)

    gate[...] += mm_l(rows_ref[...], gate_cot_ref[...])
    up[...] += mm_l(rows_ref[...], up_cot_ref[...])
    down[...] += mm_l(act_ref[...], cot_ref[...])

    @pl.when(step == 7)
    def _():
        gate_ref[...] = gate[...].astype(gate_ref.dtype)
        up_ref[...] = up[...].astype(up_ref.dtype)
        down_ref[...] = down[...].astype(down_ref.dtype)


def expert_grads(half, dtype, rows, cot_rows, act, gate_cot, up_cot, after):
    tile = lambda w, j=0: pl.BlockSpec((256, w), lambda i: (i, j))
    shapes = [(WIDTH, HALF), (WIDTH, HALF), (HALF, WIDTH)]
    return call(
        expert_grad_kernel,
        (8,),
        [tile(WIDTH), tile(WIDTH), tile(HALF, half), tile(HALF, half), tile(HALF, half), ANY],
        [full(s) for s in shapes],
        [out(s, dtype) for s in shapes],
        [pltpu.VMEM(s, F32) for s in shapes],
    )(rows, cot_rows, act, gate_cot, up_cot, after)


def shared_grad_kernel(ffn_in_ref, pair_ref, act_ref, cot_ref, _after_ref, pair_out_ref, down_out_ref):
    for j in range(0, 2 * SHARED, 512):
        at = slice(j, j + 512)
        pair_out_ref[:, at] = mm_l(ffn_in_ref[...], pair_ref[:, at]).astype(BF)
    for j in range(0, WIDTH, 512):
        at = slice(j, j + 512)
        down_out_ref[:, at] = mm_l(act_ref[...], cot_ref[:, at]).astype(BF)


def shared_grads(ffn_in, pair_low, shared_low, out_grad, after):
    return call(
        shared_grad_kernel,
        (2,),
        [
            pl.BlockSpec((TOKENS, 768), lambda h: (0, h)),
            full((TOKENS, 2 * SHARED)),
            pl.BlockSpec((TOKENS, 512), lambda h: (0, h)),
            full((TOKENS, WIDTH)),
            ANY,
        ],
        [
            pl.BlockSpec((768, 2 * SHARED), lambda h: (0, h)),
            pl.BlockSpec((512, WIDTH), lambda h: (0, h)),
        ],
        [out((768, 4 * SHARED), BF), out((512, 2 * WIDTH), BF)],
    )(ffn_in, pair_low, shared_low, out_grad, after)


def norm_back(values, scale, gain, cot):
    weighted = cot * gain
    centre = jnp.mean(weighted * values, axis=-1, keepdims=True)
    return scale * weighted - values * (scale * scale * scale * centre)


def middle_kernel(
    rank_ref,
    back_ref,
    shared_cot_ref,
    gates_ref,
    middle_ref,
    gains_ref,
    out_grad_ref,
    small_ref,
    wo_ref,
    middle_cot_ref,
    middle_low_ref,
    attended_cot_ref,
    logit_ref,
    gain_rows_ref,
    acc,
):
    step = pl.program_id(0)

    @pl.when(step == 0)
    def _():
        acc[...] = jnp.zeros_like(acc)

    acc[...] += mm_l(one_hot(rank_ref), back_ref[...])

    @pl.when(step == 7)
    def _():
        extra = acc[:, WIDTH:]
        lane = lax.broadcasted_iota(jnp.int32, (1, 128), 1)
        shares = jnp.where(lane < 64, extra + pltpu.roll(extra, 64, 1), 0.0)
        logit = shares - gates_ref[...] * jnp.sum(shares, axis=-1, keepdims=True)
        logit_ref[...] = logit.astype(BF)
        cot = acc[:, :WIDTH] + shared_cot_ref[...] + mm_r(logit_ref[...], small_ref[...])
        middle = middle_ref[...]
        scale = root_scale(middle)
        gain_rows_ref[...] = (cot * middle * scale).astype(BF)
        total = out_grad_ref[...].astype(F32) + norm_back(middle, scale, gains_ref[1:2], cot)
        middle_cot_ref[...] = total
        middle_low_ref[...] = total.astype(BF)
        for j in range(0, WIDTH, 512):
            at = slice(j, j + 512)
            attended_cot_ref[:, at] = mm_r(middle_low_ref[...], wo_ref[at, :]).astype(BF)


def middle_back(rank, back, shared_cot, gates, middle, gains, out_grad, pack):
    wide = (TOKENS, WIDTH)
    shapes = [(wide, F32), (wide, BF), (wide, BF), ((TOKENS, 128), BF), (wide, BF)]
    specs = pack_specs()
    return call(
        middle_kernel,
        (8,),
        [
            pl.BlockSpec((8, TOKENS), lambda i: (i, 0)),
            pl.BlockSpec((8 * SLOTS, WIDE), lambda i: (i, 0)),
            full(wide),
            full((TOKENS, 128)),
            full(wide),
            full((8, WIDTH)),
            full(wide),
            specs[3],
            specs[1],
        ],
        [full(s) for s, _ in shapes],
        [out(s, d) for s, d in shapes],
        [pltpu.VMEM((TOKENS, WIDE), F32)],
    )(rank, back, shared_cot, gates, middle, gains, out_grad, pack, pack)


def attention_back_kernel(
    q_ref,
    k_ref,
    v_ref,
    probs_ref,
    cot_ref,
    wq_ref,
    wk_ref,
    wv_ref,
    hidden_ref,
    gains_ref,
    middle_cot_ref,
    dq_ref,
    dk_ref,
    dv_ref,
    grad_in_ref,
    gain_rows_ref,
    acc,
):
    step = pl.program_id(0)
    key, value = k_ref[...], v_ref[...]
    dk = jnp.zeros((TOKENS, HEAD), F32)
    dv = jnp.zeros((TOKENS, HEAD), F32)
    for g in range(GROUP):
        at = slice(g * HEAD, (g + 1) * HEAD)
        probs = probs_ref[g]
        cot = cot_ref[:, at]
        dprobs = mm_r(cot, value)
        dv += mm_l(probs.astype(BF), cot)
        centre = jnp.sum(probs * dprobs, axis=-1, keepdims=True)
        dscores = (probs * (dprobs - centre)).astype(BF)
        dq_ref[:, at] = (mm(dscores, key) * SCALING).astype(BF)
        dk += mm_l(dscores, q_ref[:, at])
    dk_ref[...] = (dk * SCALING).astype(BF)
    dv_ref[...] = dv.astype(BF)

    @pl.when(step == 0)
    def _():
        acc[...] = jnp.zeros_like(acc)

    for j in range(0, WIDTH, 512):
        at = slice(j, j + 512)
        acc[:, at] += (
            mm_r(dq_ref[...], wq_ref[at, :])
            + mm_r(dk_ref[...], wk_ref[at, :])
            + mm_r(dv_ref[...], wv_ref[at, :])
        )

    @pl.when(step == 3)
    def _():
        tokens = hidden_ref[...].astype(F32)
        scale = root_scale(tokens)
        cot = acc[...]
        gain_rows_ref[...] = (cot * tokens * scale).astype(BF)
        grad_in_ref[...] = middle_cot_ref[...] + norm_back(tokens, scale, gains_ref[0:1], cot)


def attention_back(q, kv, probs, attended_cot, pack, hidden, gains, middle_cot):
    wide = (TOKENS, WIDTH)
    col = lambda w, j: pl.BlockSpec((TOKENS, w), lambda h: (0, j + h))
    weight = lambda w, j: pl.BlockSpec((WIDTH, w), lambda h: (0, j + h))
    return call(
        attention_back_kernel,
        (4,),
        [
            col(GROUP * HEAD, 0),
            col(HEAD, 0),
            col(HEAD, 4),
            pl.BlockSpec((GROUP, TOKENS, TOKENS), lambda h: (h, 0, 0)),
            col(GROUP * HEAD, 0),
            weight(GROUP * HEAD, 0),
            weight(HEAD, 24),
            weight(HEAD, 28),
            full(wide),
            full((8, WIDTH)),
            full(wide),
        ],
        [col(GROUP * HEAD, 0), col(HEAD, 0), col(HEAD, 0), full(wide), full(wide)],
        [
            out(wide, BF),
            out((TOKENS, 512), BF),
            out((TOKENS, 512), BF),
            out(wide, F32),
            out(wide, BF),
        ],
        [pltpu.VMEM(wide, F32)],
    )(q, kv, kv, probs, attended_cot, pack, pack, pack, hidden, gains, middle_cot)


def dense_grad_kernel(
    attn_in_ref,
    attended_ref,
    ffn_in_ref,
    gain_one_ref,
    gain_two_ref,
    dq_ref,
    middle_ref,
    dk_ref,
    dv_ref,
    logit_ref,
    out_ref,
):
    for j in range(0, WIDTH, 512):
        at = slice(j, j + 512)
        out_ref[:, at] = mm_l(attn_in_ref[...], dq_ref[:, at]).astype(BF)
        out_ref[:, WIDTH + j : WIDTH + j + 512] = mm_l(
            attended_ref[...], middle_ref[:, at]
        ).astype(BF)
    out_ref[:, 2 * WIDTH : 2 * WIDTH + 512] = mm_l(attn_in_ref[...], dk_ref[...]).astype(BF)
    out_ref[:, 2 * WIDTH + 512 : 2 * WIDTH + 1024] = mm_l(attn_in_ref[...], dv_ref[...]).astype(BF)
    lane = lax.broadcasted_iota(jnp.int32, (TOKENS, 128), 1)
    small = mm_l(ffn_in_ref[...], logit_ref[...])
    small += mm_l(gain_one_ref[...], jnp.where(lane == 64, 1.0, 0.0).astype(BF))
    small += mm_l(gain_two_ref[...], jnp.where(lane == 65, 1.0, 0.0).astype(BF))
    out_ref[:, 2 * WIDTH + 1024 :] = small.astype(BF)


def dense_grads(attn_in, attended, ffn_in, gain_one, gain_two, dq, middle_low, dk, dv, logit):
    left = pl.BlockSpec((TOKENS, 768), lambda h: (0, h))
    wide = full((TOKENS, WIDTH))
    thin = full((TOKENS, 512))
    return call(
        dense_grad_kernel,
        (2,),
        [left] * 5 + [wide, wide, thin, thin, full((TOKENS, 128))],
        pl.BlockSpec((768, PACK), lambda h: (0, h)),
        out((768, 2 * PACK), BF),
    )(attn_in, attended, ffn_in, gain_one, gain_two, dq, middle_low, dk, dv, logit)


def body(
    hidden_in,
    out_grad,
    doc_lengths,
    expert_ids,
    gain_attn,
    w_query,
    w_key,
    w_value,
    w_out,
    gain_ffn,
    w_router,
    w_shared_gate,
    w_shared_up,
    w_shared_down,
    expert_gate,
    expert_up,
    expert_down,
):
    parts = [w_query, w_out, w_key, w_value, w_router, gain_attn[:, None], gain_ffn[:, None]]
    parts += [jnp.zeros((12, 62), BF), w_shared_gate, w_shared_up, w_shared_down.reshape(12, 1024)]
    line = lax.all_gather(jnp.concatenate(parts, axis=1), ("zh", "zl"), axis=0, tiled=False)
    pack = gather_plane(line[:, :, :PACK])
    pair_w = gather_plane(line[:, :, PACK : PACK + 2 * SHARED])
    down_w = gather_plane(line[:, :, PACK + 2 * SHARED :].reshape(4, 8, WIDTH))
    gate, up, down = expert_gate[0], expert_up[0], expert_down[0]
    gate_other, up_other, down_other = swap(gate, "zl"), swap(up, "zl"), swap(down, "zl")

    lanes = jnp.arange(128, dtype=jnp.int32)
    hits = jnp.any(expert_ids[:, :, None] == lanes, axis=1)
    hits_low = hits.astype(BF)
    place = jnp.arange(TOKENS, dtype=jnp.int32)
    earlier = (place[:, None] > place[None, :]).astype(BF)
    rank = jnp.where(hits, mm(earlier, hits_low), -1.0).T[:EXPERTS]
    own = (lanes == lax.axis_index(DP)).astype(F32)[None]

    marked = jnp.concatenate([out_grad, hits_low], axis=1)
    cot_rows = to_experts(dispatch(rank, marked, pack, gate_other, up_other, down_other))

    attn_in, q, kv, probs, attended, middle, ffn_in, gates, gains = forward(
        hidden_in, doc_lengths, hits_low, pack
    )
    rows = to_experts(dispatch(rank, ffn_in))

    pair = mm(ffn_in, pair_w)
    shared_gate, shared_upper = pair[:, :SHARED], pair[:, SHARED:]
    sig = jax.nn.sigmoid(shared_gate)
    silu = shared_gate * sig
    shared_low = (silu * shared_upper).astype(BF)
    shared_sum = middle + mm(shared_low, down_w)
    shared_cot = mm_r(out_grad, down_w)
    slope = sig * (1.0 + shared_gate * (1.0 - sig))
    pair_low = jnp.concatenate(
        [(shared_cot * shared_upper * slope).astype(BF), (shared_cot * silu).astype(BF)], axis=1
    )
    shared_cot = mm_r(pair_low, pair_w)

    act_cot = act_cots(cot_rows, down, down_other)
    back, act, gate_cot, up_cot = expert_phase(
        rows, cot_rows, act_cot, own, pack, gate, gate_other, up, up_other, shared_cot
    )
    pair_grad, down_grad = shared_grads(ffn_in, pair_low, shared_low, out_grad, act)
    pair_grad, down_grad = scatter_plane(pair_grad), scatter_plane(down_grad)
    back = to_experts(back)
    result = to_experts(expert_outs(act, down, down_other, gate_cot))

    middle_cot, middle_low, attended_cot, logit, gain_two_rows = middle_back(
        rank, back, shared_cot, gates, middle, gains, out_grad, pack
    )
    dq, dk, dv, grad_in, gain_one_rows = attention_back(
        q, kv, probs, attended_cot, pack, hidden_in, gains, middle_cot
    )
    dense_grad = dense_grads(
        attn_in, attended, ffn_in, gain_one_rows, gain_two_rows, dq, middle_low, dk, dv, logit
    )
    dense = scatter_line(scatter_plane(dense_grad))
    pair_grad = scatter_line(pair_grad)
    down_grad = scatter_line(down_grad)
    block_out = add_results(rank, result, shared_sum)
    sent = expert_grads(1, BF, rows, cot_rows, act, gate_cot, up_cot, dense_grad)
    kept = expert_grads(0, F32, rows, cot_rows, act, gate_cot, up_cot, back)
    expert = [(k + swap(s, "zl").astype(F32))[None] for k, s in zip(kept, sent)]
    at = 2 * WIDTH
    return (
        block_out,
        grad_in,
        dense[:, at + 1088],
        dense[:, :WIDTH],
        dense[:, at : at + 512],
        dense[:, at + 512 : at + 1024],
        dense[:, WIDTH:at],
        dense[:, at + 1089],
        dense[:, at + 1024 : at + 1088],
        pair_grad[:, :SHARED],
        pair_grad[:, SHARED:],
        down_grad,
        expert[0],
        expert[1],
        expert[2],
    )


def solution(mesh):
    fine = Mesh(mesh.devices.reshape(2, 4, 4, 2, 2), AXES)
    rows, vector = P(AXES, None), P(AXES)
    banks = (P(DP, None, "zl"), P(DP, None, "zl"), P(DP, "zl", None))
    return jax.shard_map(
        body,
        mesh=fine,
        in_specs=(rows, rows, rows, rows, vector, rows, rows, rows, rows, vector)
        + (rows, rows, rows, rows)
        + banks,
        out_specs=(rows, rows, vector, rows, rows, rows, rows, vector)
        + (rows, rows, rows, rows)
        + banks,
        check_vma=False,
    )
```

profile of v0, /device:TPU:0, one launch (start us, length us, event | category | flops | bytes accessed | tf_op | source)
XLA Modules:
  0.0 740.9 jit_solution(8970232964773563377)
XLA Ops:
  10.5 15.4 %all-gather.1 = bf16[4,12,7296]{2,1,0:T(8,128)(2,1)S(1)} all-gather(bf16[1,12,7296]{2,1,0:T(8,128)(2,1)S(1)} %bitcast.55), channel_id=2, replica_groups=mesh['zh'=2,'x'=4,'y'=4,'c'=2,'zl'=2] {'zh','zl'}, dimensions={0}, use_global_device_ids=true | all-gather | bytes 875520 | tf_op jit(solution)/shard_map/all_gather | solution.py:641
  34.3 14.5 %collective-permute-done.refs_1_.gate_other_ref = bf16[1536,256]{1,0:T(8,128)(2,1)} collective-permute-done((bf16[1536,256]{1,0:T(8,128)(2,1)}, bf16[1536,256]{1,0:T(8,128)(2,1)}, u32[]{:S(2)}, u32[]{:S(2)}) %collective-permute-start) | collective-permute-done | bytes 786464 | tf_op jit(solution)/shard_map/ppermute | solution.py:47
  48.8 16.9 %collective-permute-done.1.refs_2_.up_other_ref = bf16[1536,256]{1,0:T(8,128)(2,1)} collective-permute-done((bf16[1536,256]{1,0:T(8,128)(2,1)}, bf16[1536,256]{1,0:T(8,128)(2,1)}, u32[]{:S(2)}, u32[]{:S(2)}) %collective-permute-start.1) | collective-permute-done | bytes 786464 | tf_op jit(solution)/shard_map/ppermute | solution.py:47
  65.7 13.7 %collective-permute-done.2.refs_3_.other_ref = bf16[256,1536]{1,0:T(8,128)(2,1)S(1)} collective-permute-done((bf16[256,1536]{1,0:T(8,128)(2,1)S(1)}, bf16[256,1536]{1,0:T(8,128)(2,1)S(1)}, u32[]{:S(2)}, u32[]{:S(2)}) %collective-permute-start.2) | collective-permute-done | bytes 786464 | tf_op jit(solution)/shard_map/ppermute | solution.py:47
  79.3 13.0 %all-gather.6.cloned.1.call-done = bf16[2,768,4224]{2,1,0:T(8,128)(2,1)} async-done(((bf16[2,24,4224]{2,1,0:T(8,128)(2,1)}), bf16[2,768,4224]{2,1,0:T(8,128)(2,1)}) %all-gather.6.cloned.1.call-update) | async-done | bytes 12976144 | tf_op jit(solution)/shard_map/all_gather | solution.py:73
  92.4 7.3 shard_map.282
  99.7 8.9 %all-to-all-start.1 = ((bf16[64,32,1664]{2,1,0:T(8,128)(2,1)}), bf16[64,32,1664]{2,1,0:T(8,128)(2,1)}, u32[]{:S(2)}, u32[]{:S(2)}) async-start(bf16[64,32,1664]{2,1,0:T(8,128)(2,1)} %bitcast.46), calls=%async_computation.1 | async-start | bytes 13631488 | tf_op jit(solution)/shard_map/all_to_all | solution.py:118
  109.4 12.1 %shard_map.280 = (bf16[256,1536]{1,0:T(8,128)(2,1)}, bf16[256,1536]{1,0:T(8,128)(2,1)}, bf16[256,1024]{1,0:T(8,128)(2,1)}, f32[12,256,256]{2,1,0:T(8,128)}, bf16...) custom-call(bf16[256,1536]{1,0:T(8,128)(2,1)} %hidden_ref.3, ...), custom_call_target="tpu_custom_call" | custom-call | tf_op jit(solution)/shard_map/pallas_call | solution.py:243
  121.4 7.0 shard_map.281
  128.4 76.9 %all-to-all-done.1 = bf16[64,32,1664]{2,1,0:T(8,128)(2,1)} async-done(((bf16[64,32,1664]{2,1,0:T(8,128)(2,1)}), bf16[64,32,1664]{2,1,0:T(8,128)(2,1)}, u32[]{:S(2)}, u32[]{:S(2)}) %all-to-all-start.1) | async-done | bytes 6815776 | tf_op jit(solution)/shard_map/all_to_all | solution.py:118
  205.3 16.2 %all-to-all-start = ((bf16[64,32,1536]{2,1,0:T(8,128)(2,1)}), bf16[64,32,1536]{2,1,0:T(8,128)(2,1)}, u32[]{:S(2)}, u32[]{:S(2)}) async-start(bf16[64,32,1536]{2,1,0:T(8,128)(2,1)} %bitcast.47), calls=%async_computation | async-start | bytes 12582912 | tf_op jit(solution)/shard_map/all_to_all | solution.py:118
  222.3 5.9 fusion.8
  228.2 73.7 %all-gather.8.cloned.1.call-done = bf16[2,512,1536]{2,1,0:T(8,128)(2,1)} async-done(((bf16[2,16,1536]{2,1,0:T(8,128)(2,1)}), bf16[2,512,1536]{2,1,0:T(8,128)(2,1)}) %all-gather.8.cloned.1.call-update) | async-done | bytes 3145744 | tf_op jit(solution)/shard_map/all_gather | solution.py:73
  302.0 4.7 multiply_convert_fusion.2
  310.7 9.6 %shard_map.283.act_cot_ref = f32[2048,512]{1,0:T(8,128)} custom-call(bf16[2048,1664]{1,0:T(8,128)(2,1)} %bitcast.11.cot_ref.marks_ref, bf16[256,1536]{1,0:T(8,128)(2,1)} %bitcast.50, bf16[256,1536]{1,0:T(8,128)(2,1)} %copy-done), custom_call_target="tpu_custom_call" | custom-call | tf_op jit(solution)/shard_map/pallas_call | solution.py:258
  320.3 21.2 %shard_map.284 = (bf16[2048,1664]{1,0:T(8,128)(2,1)}, bf16[2048,512]{1,0:T(8,128)(2,1)}, bf16[2048,512]{1,0:T(8,128)(2,1)}, bf16[2048,512]{1,0:T(8,128)(2,1)}) custom-call(bf16[2048,1536]{1,0:T(8,128)(2,1)} %bitcast.6.rows_ref, bf16[2048,1664]{1,0:T(8,128)(2,1)} %bitcast.11.cot_ref.marks_ref, f32[2048,512]{1,0:T(8,128)} %shard_map.283.act_cot_ref, ...), custom_call_target="tpu_custom_call" | custom-call | tf_op jit(solution)/shard_map/pallas_call | solution.py:322
  341.5 6.4 shard_map.290
  348.5 98.6 %all_to_all.20 = bf16[64,32,1664]{2,1,0:T(8,128)(2,1)} all-to-all(bf16[64,32,1664]{2,1,0:T(8,128)(2,1)} %bitcast.49), channel_id=1, replica_groups=mesh['zh'=2,'x'=4,'y'=4,'c'=2,'zl'=2] {'zh','x','y','c'}, dimensions={0} | all-to-all | bytes 13631488 | tf_op jit(solution)/shard_map/all_to_all | solution.py:118
  447.1 14.6 %shard_map.287 = (f32[256,1536]{1,0:T(8,128)}, bf16[256,1536]{1,0:T(8,128)(2,1)}, bf16[256,1536]{1,0:T(8,128)(2,1)}, bf16[256,128]{1,0:T(8,128)(2,1)}, bf16[256,1536]{1,0:T(8,128)(2,1)}) custom-call(f32[64,256]{1,0:T(8,128)} %slice_select_fusion.rank_ref, bf16[2048,1664]{1,0:T(8,128)(2,1)} %bitcast.44, f32[256,1536]{1,0:T(8,128)} %fusion.4._after_ref.shared_cot_ref, ...), custom_call_target="tpu_custom_call" | custom-call | tf_op jit(solution)/shard_map/pallas_call | solution.py:470
  461.7 14.7 %shard_map.288 = (bf16[256,1536]{1,0:T(8,128)(2,1)}, bf16[256,512]{1,0:T(8,128)(2,1)}, bf16[256,512]{1,0:T(8,128)(2,1)}, f32[256,1536]{1,0:T(8,128)}, bf16[256,1536]{1,0:T(8,128)(2,1)}) custom-call(bf16[256,1536]{1,0:T(8,128)(2,1)} %get-tuple-element.50.q_ref, bf16[256,1024]{1,0:T(8,128)(2,1)} %get-tuple-element.51.k_ref.v_ref, ...), custom_call_target="tpu_custom_call" | custom-call | tf_op jit(solution)/shard_map/pallas_call | solution.py:551
  476.4 9.7 %shard_map.289._after_ref = bf16[768,8448]{1,0:T(8,128)(2,1)} custom-call(bf16[256,1536]{1,0:T(8,128)(2,1)} %get-tuple-element.59.attn_in_ref, bf16[256,1536]{1,0:T(8,128)(2,1)} %get-tuple-element.60.attended_ref, bf16[256,1536]{1,0:T(8,128)(2,1)} %get-tuple-element.46.rows_ref.ffn_in_ref, bf16[256,1536]{1,0:T(8,128)(2,1)} %get-tuple-element.61.gain_one_ref, ...), custom_call_target="tpu_custom_call" | custom-call | tf_op jit(solution)/shard_map/pallas_call | solution.py:611
  486.1 9.2 %shard_map.285 = bf16[2048,1536]{1,0:T(8,128)(2,1)} custom-call(bf16[2048,512]{1,0:T(8,128)(2,1)} %get-tuple-element.47.act_ref._after_ref, bf16[256,1536]{1,0:T(8,128)(2,1)} %bitcast.51, bf16[256,1536]{1,0:T(8,128)(2,1)} %copy-done, bf16[2048,512]{1,0:T(8,128)(2,1)} %get-tuple-element.48._after_ref.gate_cot_ref), custom_call_target="tpu_custom_call" | custom-call | tf_op jit(solution)/shard_map/pallas_call | solution.py:339
  495.3 6.3 all-to-all-start.2
  505.5 20.4 %collective-permute-done.7 = bf16[16,1536]{1,0:T(8,128)(2,1)S(1)} collective-permute-done((bf16[16,1536]{1,0:T(8,128)(2,1)S(1)}, bf16[16,1536]{1,0:T(8,128)(2,1)S(1)}, u32[]{:S(2)}, u32[]{:S(2)}) %collective-permute-start.7) | collective-permute-done | bytes 49184 | tf_op jit(solution)/shard_map/ppermute | solution.py:47
  526.9 12.6 %shard_map.292 = (bf16[1536,256]{1,0:T(8,128)(2,1)}, bf16[1536,256]{1,0:T(8,128)(2,1)}, bf16[256,1536]{1,0:T(8,128)(2,1)}) custom-call(bf16[2048,1536]{1,0:T(8,128)(2,1)} %bitcast.6.rows_ref, bf16[2048,1664]{1,0:T(8,128)(2,1)} %bitcast.11.cot_ref.marks_ref, bf16[2048,512]{1,0:T(8,128)(2,1)} %get-tuple-element.47.act_ref._after_ref, ...), custom_call_target="tpu_custom_call" | custom-call | tf_op jit(solution)/shard_map/pallas_call | solution.py:378
  544.3 43.4 %all-to-all-done.2 = bf16[64,32,1536]{2,1,0:T(8,128)(2,1)} async-done(((bf16[64,32,1536]{2,1,0:T(8,128)(2,1)}), bf16[64,32,1536]{2,1,0:T(8,128)(2,1)}, u32[]{:S(2)}, u32[]{:S(2)}) %all-to-all-start.2) | async-done | bytes 6291488 | tf_op jit(solution)/shard_map/all_to_all | solution.py:118
  587.7 8.4 %shard_map.286 = bf16[256,1536]{1,0:T(8,128)(2,1)} custom-call(f32[64,256]{1,0:T(8,128)} %slice_select_fusion.rank_ref, bf16[2048,1536]{1,0:T(8,128)(2,1)} %bitcast.16.rows_ref, f32[256,1536]{1,0:T(8,128)} %convolution_add_fusion.base_ref), custom_call_target="tpu_custom_call" | custom-call | tf_op jit(solution)/shard_map/pallas_call | solution.py:138
  596.1 13.3 %shard_map.291 = (f32[1536,256]{1,0:T(8,128)}, f32[1536,256]{1,0:T(8,128)}, f32[256,1536]{1,0:T(8,128)}) custom-call(bf16[2048,1536]{1,0:T(8,128)(2,1)} %bitcast.6.rows_ref, bf16[2048,1664]{1,0:T(8,128)(2,1)} %bitcast.11.cot_ref.marks_ref, bf16[2048,512]{1,0:T(8,128)(2,1)} %get-tuple-element.47.act_ref._after_ref, ...), custom_call_target="tpu_custom_call" | custom-call | tf_op jit(solution)/shard_map/pallas_call | solution.py:378
  615.4 3.8 collective-permute-start.5
  619.2 10.5 %collective-permute-done.11 = bf16[256,1536]{1,0:T(8,128)(2,1)S(1)} collective-permute-done((bf16[256,1536]{1,0:T(8,128)(2,1)}, bf16[256,1536]{1,0:T(8,128)(2,1)S(1)}, u32[]{:S(2)}, u32[]{:S(2)}) %collective-permute-start.11) | collective-permute-done | bytes 786464 | tf_op jit(solution)/shard_map/ppermute | solution.py:47
  634.8 81.8 %reduce-scatter.4.cloned.1.call-done = bf16[24,8448]{1,0:T(8,128)(2,1)} async-done(((bf16[768,8448]{1,0:T(8,128)(2,1)}), bf16[24,8448]{1,0:T(8,128)(2,1)}) %reduce-scatter.4.cloned.1.call-update) | async-done | bytes 405520 | tf_op jit(solution)/shard_map/reduce_scatter | solution.py:78
  721.0 4.1 collective-permute-done.3
  (103 shorter events, 51.8 us)
Async XLA Ops:
  7.2 85.2 %all-gather.6.cloned.1.call-start = ((), (), s32[]{:S(2)}) async-start(), calls=%async_computation.7 | async-start | bytes 13381632 | tf_op jit(solution)/shard_map/all_gather | solution.py:73
  25.9 6.2 copy-start.11
  25.9 7.5 %copy-start.2 = (bf16[256,1536]{1,0:T(8,128)(2,1)S(1)}, bf16[256,1536]{1,0:T(8,128)(2,1)}, u32[]{:S(2)}) copy-start(bf16[256,1536]{1,0:T(8,128)(2,1)} %cot_ref.1) | copy-start | bytes 2359300
  26.8 195.5 %all-gather.10.cloned.1.call-start = ((), (), s32[]{:S(2)}) async-start(), calls=%async_computation.9 | async-start | bytes 6488064 | tf_op jit(solution)/shard_map/all_gather | solution.py:73
  27.6 21.2 %collective-permute-start = (bf16[1536,256]{1,0:T(8,128)(2,1)}, bf16[1536,256]{1,0:T(8,128)(2,1)}, u32[]{:S(2)}, u32[]{:S(2)}) collective-permute-start(bf16[1536,256]{1,0:T(8,128)(2,1)} %bitcast.56), channel_id=1, source_target_pairs={{0,1},{1,0},{2,3},{3,2},{4,5},{5,4},{6,7},{7,6},{8,9},{9,8},{10,11... | collective-permute-start | bytes 2359304 | tf_op jit(solution)/shard_map/ppermute | solution.py:47
  30.0 35.6 %collective-permute-start.1 = (bf16[1536,256]{1,0:T(8,128)(2,1)}, bf16[1536,256]{1,0:T(8,128)(2,1)}, u32[]{:S(2)}, u32[]{:S(2)}) collective-permute-start(bf16[1536,256]{1,0:T(8,128)(2,1)} %bitcast.58), channel_id=1, source_target_pairs={{0,1},{1,0},{2,3},{3,2},{4,5},{5,4},{6,7},{7,6},{8,9},{9,8},{10,11... | collective-permute-start | bytes 2359304 | tf_op jit(solution)/shard_map/ppermute | solution.py:47
  30.1 49.2 %collective-permute-start.2 = (bf16[256,1536]{1,0:T(8,128)(2,1)S(1)}, bf16[256,1536]{1,0:T(8,128)(2,1)S(1)}, u32[]{:S(2)}, u32[]{:S(2)}) collective-permute-start(bf16[256,1536]{1,0:T(8,128)(2,1)S(1)} %bitcast.52), channel_id=1, source_target_pairs={{0,1},{1,0},{2,3},{3,2},{4,5},{5,4},{6,7},{7,6},{8,9},{9,8},{10,11... | collective-permute-start | bytes 2359304 | tf_op jit(solution)/shard_map/ppermute | solution.py:47
  32.5 67.2 %copy-start.10 = (bf16[256,128]{1,0:T(8,128)(2,1)}, bf16[256,128]{1,0:T(8,128)(2,1)S(1)}, u32[]{:S(2)}) copy-start(bf16[256,128]{1,0:T(8,128)(2,1)S(1)} %convert.hits_ref) | copy-start | bytes 196612
  79.3 13.0 %copy-start = (bf16[256,1536]{1,0:T(8,128)(2,1)}, bf16[256,1536]{1,0:T(8,128)(2,1)S(1)}, u32[]{:S(2)}) copy-start(bf16[256,1536]{1,0:T(8,128)(2,1)S(1)} %collective-permute-done.2.refs_3_.other_ref) | copy-start | bytes 2359300
  99.7 105.6 %all-to-all-start.1 = ((bf16[64,32,1664]{2,1,0:T(8,128)(2,1)}), bf16[64,32,1664]{2,1,0:T(8,128)(2,1)}, u32[]{:S(2)}, u32[]{:S(2)}) async-start(bf16[64,32,1664]{2,1,0:T(8,128)(2,1)} %bitcast.46), calls=%async_computation.1 | async-start | bytes 13631488 | tf_op jit(solution)/shard_map/all_to_all | solution.py:118
  108.6 193.4 %all-gather.8.cloned.1.call-start = ((), (), s32[]{:S(2)}) async-start(), calls=%async_computation.8 | async-start | bytes 3244032 | tf_op jit(solution)/shard_map/all_gather | solution.py:73
  205.3 17.0 %copy-start.1 = (bf16[256,1536]{1,0:T(8,128)(2,1)S(1)}, bf16[256,1536]{1,0:T(8,128)(2,1)}, u32[]{:S(2)}) copy-start(bf16[256,1536]{1,0:T(8,128)(2,1)} %get-tuple-element.46.rows_ref.ffn_in_ref) | copy-start | bytes 2359300
  205.3 114.9 %all-to-all-start = ((bf16[64,32,1536]{2,1,0:T(8,128)(2,1)}), bf16[64,32,1536]{2,1,0:T(8,128)(2,1)}, u32[]{:S(2)}, u32[]{:S(2)}) async-start(bf16[64,32,1536]{2,1,0:T(8,128)(2,1)} %bitcast.47), calls=%async_computation | async-start | bytes 12582912 | tf_op jit(solution)/shard_map/all_to_all | solution.py:118
  221.6 280.0 %reduce-scatter.8.cloned.1.call-start = ((), (), s32[]{:S(2)}) async-start(), calls=%async_computation.12 | async-start | bytes 3244032 | tf_op jit(solution)/shard_map/reduce_scatter | solution.py:78
  302.0 5.7 slice-start.1
  347.9 266.5 %reduce-scatter.6.cloned.1.call-start = ((), (), s32[]{:S(2)}) async-start(), calls=%async_computation.11 | async-start | bytes 6488064 | tf_op jit(solution)/shard_map/reduce_scatter | solution.py:78
  348.5 368.1 %reduce-scatter.4.cloned.1.call-start = ((), (), s32[]{:S(2)}) async-start(), calls=%async_computation.10 | async-start | bytes 13381632 | tf_op jit(solution)/shard_map/reduce_scatter | solution.py:78
  495.3 92.4 %all-to-all-start.2 = ((bf16[64,32,1536]{2,1,0:T(8,128)(2,1)}), bf16[64,32,1536]{2,1,0:T(8,128)(2,1)}, u32[]{:S(2)}, u32[]{:S(2)}) async-start(bf16[64,32,1536]{2,1,0:T(8,128)(2,1)} %bitcast.48), calls=%async_computation.2 | async-start | bytes 12582912 | tf_op jit(solution)/shard_map/all_to_all | solution.py:118
  502.5 23.4 %collective-permute-start.7 = (bf16[16,1536]{1,0:T(8,128)(2,1)S(1)}, bf16[16,1536]{1,0:T(8,128)(2,1)S(1)}, u32[]{:S(2)}, u32[]{:S(2)}) collective-permute-start(bf16[16,1536]{1,0:T(8,128)(2,1)S(1)} %broadcast_select_fusion.2), channel_id=1, source_target_pairs={{0,64},{64,0},{1,65},{65,1},{2,66},{66,2},{3,67},{67,3},{4,68},{68... | collective-permute-start | bytes 147464 | tf_op jit(solution)/shard_map/ppermute | solution.py:47
  526.8 16.9 %collective-permute-start.8 = (bf16[8,1536]{1,0:T(8,128)(2,1)S(1)}, bf16[8,1536]{1,0:T(8,128)(2,1)S(1)}, u32[]{:S(2)}, u32[]{:S(2)}) collective-permute-start(bf16[8,1536]{1,0:T(8,128)(2,1)S(1)} %select_convert_fusion.2), channel_id=1, source_target_pairs={{0,1},{1,0},{2,3},{3,2},{4,5},{5,4},{6,7},{7,6},{8,9},{9,8},{10,11... | collective-permute-start | bytes 73736 | tf_op jit(solution)/shard_map/ppermute | solution.py:47
  526.9 14.7 %copy-start.3 = (f32[256,1536]{1,0:T(8,128)S(1)}, f32[256,1536]{1,0:T(8,128)}, u32[]{:S(2)}) copy-start(f32[256,1536]{1,0:T(8,128)} %get-tuple-element.49.middle_ref) | copy-start | bytes 4718596
  526.9 14.6 %copy-start.5 = (bf16[2,512,1536]{2,1,0:T(8,128)(2,1)S(1)}, bf16[2,512,1536]{2,1,0:T(8,128)(2,1)}, u32[]{:S(2)}) copy-start(bf16[2,512,1536]{2,1,0:T(8,128)(2,1)} %all-gather.8.cloned.1.call-done) | copy-start | bytes 9437188
  526.9 14.6 %copy-start.6 = (bf16[256,1024]{1,0:T(8,128)(2,1)S(1)}, bf16[256,1024]{1,0:T(8,128)(2,1)}, u32[]{:S(2)}) copy-start(bf16[256,1024]{1,0:T(8,128)(2,1)} %get-tuple-element.81.act_ref) | copy-start | bytes 1572868
  539.5 70.8 %collective-permute-start.9 = (bf16[1536,256]{1,0:T(8,128)(2,1)}, bf16[1536,256]{1,0:T(8,128)(2,1)S(1)}, u32[]{:S(2)}, u32[]{:S(2)}) collective-permute-start(bf16[1536,256]{1,0:T(8,128)(2,1)} %get-tuple-element.72), channel_id=1, source_target_pairs={{0,1},{1,0},{2,3},{3,2},{4,5},{5,4},{6,7},{7,6},{8,9},{9,8},{10,11... | collective-permute-start | bytes 2359304 | tf_op jit(solution)/shard_map/ppermute | solution.py:47
  543.6 69.4 %collective-permute-start.10 = (bf16[1536,256]{1,0:T(8,128)(2,1)}, bf16[1536,256]{1,0:T(8,128)(2,1)S(1)}, u32[]{:S(2)}, u32[]{:S(2)}) collective-permute-start(bf16[1536,256]{1,0:T(8,128)(2,1)} %get-tuple-element.74), channel_id=1, source_target_pairs={{0,1},{1,0},{2,3},{3,2},{4,5},{5,4},{6,7},{7,6},{8,9},{9,8},{10,11... | collective-permute-start | bytes 2359304 | tf_op jit(solution)/shard_map/ppermute | solution.py:47
  609.4 20.2 %collective-permute-start.11 = (bf16[256,1536]{1,0:T(8,128)(2,1)}, bf16[256,1536]{1,0:T(8,128)(2,1)S(1)}, u32[]{:S(2)}, u32[]{:S(2)}) collective-permute-start(bf16[256,1536]{1,0:T(8,128)(2,1)} %get-tuple-element.76), channel_id=1, source_target_pairs={{0,1},{1,0},{2,3},{3,2},{4,5},{5,4},{6,7},{7,6},{8,9},{9,8},{10,11... | collective-permute-start | bytes 2359304 | tf_op jit(solution)/shard_map/ppermute | solution.py:47
  613.0 16.6 %copy-start.7 = (f32[256,1536]{1,0:T(8,128)S(1)}, f32[256,1536]{1,0:T(8,128)}, u32[]{:S(2)}) copy-start(f32[256,1536]{1,0:T(8,128)} %get-tuple-element.75) | copy-start | bytes 4718596
  614.4 20.3 %copy-start.9 = (bf16[24,4096]{1,0:T(8,128)(2,1)S(1)}, bf16[24,4096]{1,0:T(8,128)(2,1)}, u32[]{:S(2)}) copy-start(bf16[24,4096]{1,0:T(8,128)(2,1)} %reduce-scatter.6.cloned.1.call-done) | copy-start | bytes 589828
  615.4 19.3 %collective-permute-start.5 = (bf16[24,2048]{1,0:T(8,128)(2,1)S(1)}, bf16[24,2048]{1,0:T(8,128)(2,1)S(1)}, u32[]{:S(2)}, u32[]{:S(2)}) collective-permute-start(bf16[24,2048]{1,0:T(8,128)(2,1)S(1)} %broadcast_select_fusion.1), channel_id=1, source_target_pairs={{0,64},{64,0},{1,65},{65,1},{2,66},{66,2},{3,67},{67,3},{4,68},{68... | collective-permute-start | bytes 294920 | tf_op jit(solution)/shard_map/ppermute | solution.py:47
  634.7 86.2 %collective-permute-start.6 = (bf16[12,2048]{1,0:T(8,128)(2,1)S(1)}, bf16[12,2048]{1,0:T(8,128)(2,1)S(1)}, u32[]{:S(2)}, u32[]{:S(2)}) collective-permute-start(bf16[12,2048]{1,0:T(8,128)(2,1)S(1)} %select_convert_fusion.1), channel_id=1, source_target_pairs={{0,1},{1,0},{2,3},{3,2},{4,5},{5,4},{6,7},{7,6},{8,9},{9,8},{10,11... | collective-permute-start | bytes 147464 | tf_op jit(solution)/shard_map/ppermute | solution.py:47
  717.7 7.4 collective-permute-start.3
  726.3 5.1 collective-permute-start.4
  (3 other events, 13.5 us)
Sparse Core Ops, SparseCore 0:
  26.9 65.3 all-gather.5
  95.2 107.5 all-gather.9
  205.7 96.1 all-gather.7
  348.0 116.5 reduce-scatter.7
  468.6 140.0 reduce-scatter.5
  612.5 104.1 reduce-scatter.3
where the time goes:
time: 743 us; the launch traced here: 741 us
  waiting for transfers between devices  376 us (51%)
  Pallas kernels  146 us (20%)
  blocking collectives  114 us (15%)
  starting transfers between devices  51 us (7%)
  matrix products  15.9 us (2%)
  other arithmetic  14.5 us (2%)
  between operations  14.4 us (2%)
  local copies, waits for them, and re-layouts  9.04 us (1%)
    all_to_all x3, waiting for transfers between devices, to_experts(): lax.all_to_all(rows.reshape(EXPERTS, SLOTS, -1), DP, split_axis=0, concat...  120 us
    all_to_all x1, blocking collectives, to_experts(): lax.all_to_all(rows.reshape(EXPERTS, SLOTS, -1), DP, split_axis=0, concat...  98.6 us
    all_gather x3, waiting for transfers between devices, gather_plane(): lax.all_gather(four.reshape(2, 2 * rows, width), PLANE, axis=1, tiled=True)  86.8 us
    ppermute x12, waiting for transfers between devices, swap(): return lax.ppermute(x, axis, [(0, 1), (1, 0)])  86.5 us
    reduce_scatter x3, waiting for transfers between devices, scatter_plane(): return lax.psum_scatter(grads, PLANE, scatter_dimension=0, tiled=True)  81.9 us
    all_to_all x3, starting transfers between devices, to_experts(): lax.all_to_all(rows.reshape(EXPERTS, SLOTS, -1), DP, split_axis=0, concat...  31.4 us
    pallas_call x2, Pallas kernels, expert_grads(): call(expert_grad_kernel, (8,), [tile(WIDTH), tile(WIDTH), tile(HALF, half...  25.9 us
    pallas_call x1, Pallas kernels, expert_phase(): call(expert_kernel, (8,), [tile(WIDTH), tile(128, 12), tile(512), full((1...  21.2 us
  transfers between devices with their start and end apart: 21, of which 13 were waited for; matrix products, arithmetic and copies ran while one was open for 4% of the time, Pallas kernels for 16%

commit v1 on v0

--- a/solution.py
+++ b/solution.py
@@ -1,5 +1,3 @@
-import functools
-
 import jax
 import jax.numpy as jnp
 from jax import lax
@@ -68,27 +66,53 @@
     )
 
 
-def gather_plane(four):
-    _, rows, width = four.shape
-    whole = lax.all_gather(four.reshape(2, 2 * rows, width), PLANE, axis=1, tiled=True)
-    return whole.reshape(128 * rows, width)
+def tie_kernel(*refs):
+    pass
+
+
+def tie(x, *after):
+    return pl.pallas_call(
+        tie_kernel,
+        in_specs=[ANY] * (1 + len(after)),
+        out_specs=ANY,
+        out_shape=out(x.shape, x.dtype),
+        input_output_aliases={0: 0},
+    )(x, *after)
+
+
+def gather_plane(pairs):
+    _, rows, width = pairs.shape
+    return lax.all_gather(pairs, PLANE, axis=1, tiled=True).reshape(64 * rows, width)
 
 
 def scatter_plane(grads):
     return lax.psum_scatter(grads, PLANE, scatter_dimension=0, tiled=True)
 
 
-def scatter_line(plane):
-    r, width = plane.shape[0] // 2, plane.shape[1] // 2
+def sum_zh(plane):
+    width = plane.shape[1] // 2
     zh = lax.axis_index("zh")
-    zl = lax.axis_index("zl")
     low, high = plane[:, :width], plane[:, width:]
     keep = jnp.where(zh == 0, low, high)
     give = jnp.where(zh == 0, high, low)
-    pair = keep.astype(F32) + swap(give, "zh").astype(F32)
-    keep = jnp.where(zl == 0, pair[:r], pair[r:])
-    give = jnp.where(zl == 0, pair[r:], pair[:r]).astype(BF)
+    return keep.astype(F32) + swap(give, "zh").astype(F32)
+
+
+def sum_zl(mine, other):
+    zl = lax.axis_index("zl")
+    keep = jnp.where(zl == 0, mine, other)
+    give = jnp.where(zl == 0, other, mine).astype(BF)
     return keep + swap(give, "zl").astype(F32)
+
+
+def fold_down(rows):
+    tail = [rows[:, :8, 1024:], rows[:, 8:, 1024:]]
+    return jnp.concatenate([rows[:, :, :1024], jnp.concatenate(tail, axis=2)], axis=1)
+
+
+def unfold_down(rows):
+    tail = jnp.concatenate([rows[:, 16:, :512], rows[:, 16:, 512:]], axis=1)
+    return jnp.concatenate([rows[:, :16], tail], axis=2)
 
 
 def one_hot(rank_ref):
@@ -98,20 +122,19 @@
     return hit.reshape(8 * SLOTS, TOKENS).astype(BF)
 
 
-def dispatch_kernel(n, rank_ref, rows_ref, *refs):
-    refs[n][...] = mm(one_hot(rank_ref), rows_ref[...]).astype(BF)
-
-
-def dispatch(rank, rows, *after):
+def dispatch_kernel(rank_ref, rows_ref, out_ref):
+    out_ref[...] = mm(one_hot(rank_ref), rows_ref[...]).astype(BF)
+
+
+def dispatch(rank, rows):
     width = rows.shape[1]
     return call(
-        functools.partial(dispatch_kernel, len(after)),
+        dispatch_kernel,
         (8,),
-        [pl.BlockSpec((8, TOKENS), lambda i: (i, 0)), full((TOKENS, width))]
-        + [ANY] * len(after),
+        [pl.BlockSpec((8, TOKENS), lambda i: (i, 0)), full((TOKENS, width))],
         pl.BlockSpec((8 * SLOTS, width), lambda i: (i, 0)),
         out((ROWS, width), BF),
-    )(rank, rows, *after)
+    )(rank, rows)
 
 
 def to_experts(rows):
@@ -146,6 +169,7 @@
         full((TOKENS, WIDTH)),
         out((TOKENS, WIDTH), BF),
         [pltpu.VMEM((TOKENS, WIDTH), F32)],
+        flops=10**12,
     )(rank, rows, base)
 
 
@@ -347,6 +371,7 @@
         ],
         pl.BlockSpec((256, WIDTH), lambda i: (i, 0)),
         out((ROWS, WIDTH), BF),
+        flops=10**11,
     )(act, down, other, after)
 
 
@@ -382,16 +407,20 @@
         [full(s) for s in shapes],
         [out(s, dtype) for s in shapes],
         [pltpu.VMEM(s, F32) for s in shapes],
+        flops=10**11,
     )(rows, cot_rows, act, gate_cot, up_cot, after)
 
 
-def shared_grad_kernel(ffn_in_ref, pair_ref, act_ref, cot_ref, _after_ref, pair_out_ref, down_out_ref):
+def shared_grad_kernel(ffn_in_ref, pair_ref, act_ref, cot_ref, _after_ref, out_ref):
     for j in range(0, 2 * SHARED, 512):
         at = slice(j, j + 512)
-        pair_out_ref[:, at] = mm_l(ffn_in_ref[...], pair_ref[:, at]).astype(BF)
-    for j in range(0, WIDTH, 512):
-        at = slice(j, j + 512)
-        down_out_ref[:, at] = mm_l(act_ref[...], cot_ref[:, at]).astype(BF)
+        out_ref[:, at] = mm_l(ffn_in_ref[...], pair_ref[:, at]).astype(BF)
+    for j in range(0, 1024, 512):
+        body = mm_l(act_ref[...], cot_ref[:, j : j + 512]).reshape(32, 16, 512)
+        tail = mm_l(act_ref[...], cot_ref[:, 1024:]).reshape(32, 16, 512)
+        tail = tail[:, :8] if j == 0 else tail[:, 8:]
+        both = jnp.concatenate([body, tail], axis=1).reshape(768, 512)
+        out_ref[:, 2 * SHARED + j : 2 * SHARED + j + 512] = both.astype(BF)
 
 
 def shared_grads(ffn_in, pair_low, shared_low, out_grad, after):
@@ -405,11 +434,9 @@
             full((TOKENS, WIDTH)),
             ANY,
         ],
-        [
-            pl.BlockSpec((768, 2 * SHARED), lambda h: (0, h)),
-            pl.BlockSpec((512, WIDTH), lambda h: (0, h)),
-        ],
-        [out((768, 4 * SHARED), BF), out((512, 2 * WIDTH), BF)],
+        pl.BlockSpec((768, 2 * SHARED + 1024), lambda h: (0, h)),
+        out((768, 4 * SHARED + 2048), BF),
+        flops=10**11,
     )(ffn_in, pair_low, shared_low, out_grad, after)
 
 
@@ -429,6 +456,7 @@
     out_grad_ref,
     small_ref,
     wo_ref,
+    _after_ref,
     middle_cot_ref,
     middle_low_ref,
     attended_cot_ref,
@@ -463,7 +491,7 @@
             attended_cot_ref[:, at] = mm_r(middle_low_ref[...], wo_ref[at, :]).astype(BF)
 
 
-def middle_back(rank, back, shared_cot, gates, middle, gains, out_grad, pack):
+def middle_back(rank, back, shared_cot, gates, middle, gains, out_grad, pack, after):
     wide = (TOKENS, WIDTH)
     shapes = [(wide, F32), (wide, BF), (wide, BF), ((TOKENS, 128), BF), (wide, BF)]
     specs = pack_specs()
@@ -480,11 +508,12 @@
             full(wide),
             specs[3],
             specs[1],
+            ANY,
         ],
         [full(s) for s, _ in shapes],
         [out(s, d) for s, d in shapes],
         [pltpu.VMEM((TOKENS, WIDE), F32)],
-    )(rank, back, shared_cot, gates, middle, gains, out_grad, pack, pack)
+    )(rank, back, shared_cot, gates, middle, gains, out_grad, pack, pack, after)
 
 
 def attention_back_kernel(
@@ -639,9 +668,9 @@
     parts = [w_query, w_out, w_key, w_value, w_router, gain_attn[:, None], gain_ffn[:, None]]
     parts += [jnp.zeros((12, 62), BF), w_shared_gate, w_shared_up, w_shared_down.reshape(12, 1024)]
     line = lax.all_gather(jnp.concatenate(parts, axis=1), ("zh", "zl"), axis=0, tiled=False)
-    pack = gather_plane(line[:, :, :PACK])
-    pair_w = gather_plane(line[:, :, PACK : PACK + 2 * SHARED])
-    down_w = gather_plane(line[:, :, PACK + 2 * SHARED :].reshape(4, 8, WIDTH))
+    dense_w = line[:, :, : PACK + 2 * SHARED].reshape(2, 24, PACK + 2 * SHARED)
+    down_w = fold_down(line[:, :, PACK + 2 * SHARED :].reshape(2, 16, WIDTH))
+    pack = gather_plane(jnp.concatenate([dense_w, down_w], axis=2))
     gate, up, down = expert_gate[0], expert_up[0], expert_down[0]
     gate_other, up_other, down_other = swap(gate, "zl"), swap(up, "zl"), swap(down, "zl")
 
@@ -654,12 +683,17 @@
     own = (lanes == lax.axis_index(DP)).astype(F32)[None]
 
     marked = jnp.concatenate([out_grad, hits_low], axis=1)
-    cot_rows = to_experts(dispatch(rank, marked, pack, gate_other, up_other, down_other))
+    cot_rows = to_experts(
+        tie(dispatch(rank, marked), pack, gate_other, up_other, down_other)
+    )
 
     attn_in, q, kv, probs, attended, middle, ffn_in, gates, gains = forward(
         hidden_in, doc_lengths, hits_low, pack
     )
-    rows = to_experts(dispatch(rank, ffn_in))
+    send_rows = dispatch(rank, ffn_in)
+    rows = to_experts(send_rows)
+    pair_w = pack[:, PACK : PACK + 2 * SHARED]
+    down_w = unfold_down(pack[:, PACK + 2 * SHARED :].reshape(64, 24, 1024)).reshape(SHARED, WIDTH)
 
     pair = mm(ffn_in, pair_w)
     shared_gate, shared_upper = pair[:, :SHARED], pair[:, SHARED:]
@@ -678,13 +712,15 @@
     back, act, gate_cot, up_cot = expert_phase(
         rows, cot_rows, act_cot, own, pack, gate, gate_other, up, up_other, shared_cot
     )
-    pair_grad, down_grad = shared_grads(ffn_in, pair_low, shared_low, out_grad, act)
-    pair_grad, down_grad = scatter_plane(pair_grad), scatter_plane(down_grad)
+    shared_grad = shared_grads(ffn_in, pair_low, shared_low, out_grad, act)
+    kept = expert_grads(0, F32, rows, cot_rows, act, gate_cot, up_cot, shared_grad)
+    shared_grad = scatter_plane(shared_grad)
+    result_rows = expert_outs(act, down, down_other, kept[0])
     back = to_experts(back)
-    result = to_experts(expert_outs(act, down, down_other, gate_cot))
+    result = to_experts(result_rows)
 
     middle_cot, middle_low, attended_cot, logit, gain_two_rows = middle_back(
-        rank, back, shared_cot, gates, middle, gains, out_grad, pack
+        rank, back, shared_cot, gates, middle, gains, out_grad, pack, result_rows
     )
     dq, dk, dv, grad_in, gain_one_rows = attention_back(
         q, kv, probs, attended_cot, pack, hidden_in, gains, middle_cot
@@ -692,12 +728,15 @@
     dense_grad = dense_grads(
         attn_in, attended, ffn_in, gain_one_rows, gain_two_rows, dq, middle_low, dk, dv, logit
     )
-    dense = scatter_line(scatter_plane(dense_grad))
-    pair_grad = scatter_line(pair_grad)
-    down_grad = scatter_line(down_grad)
+    dense = sum_zh(scatter_plane(dense_grad))
+    dense = sum_zl(dense[:12], dense[12:])
+    shared_grad = sum_zh(shared_grad)
+    pair_grad = shared_grad[:, : 2 * SHARED]
+    down_grad = unfold_down(shared_grad[None, :, 2 * SHARED :])[0]
+    pair_grad = sum_zl(pair_grad[:12], pair_grad[12:])
+    down_grad = sum_zl(down_grad[:8], down_grad[8:])
     block_out = add_results(rank, result, shared_sum)
     sent = expert_grads(1, BF, rows, cot_rows, act, gate_cot, up_cot, dense_grad)
-    kept = expert_grads(0, F32, rows, cot_rows, act, gate_cot, up_cot, back)
     expert = [(k + swap(s, "zl").astype(F32))[None] for k, s in zip(kept, sent)]
     at = 2 * WIDTH
     return (

time: 743 us -> 643 us (0.87)
  blocking collectives: 114 us -> 15.4 us
  waiting for transfers between devices: 376 us -> 346 us
  starting transfers between devices: 51 us -> 78.5 us
    all_to_all x3 -> x4, waiting for transfers between devices: 120 us -> 222 us  [to_experts(): lax.all_to_all(rows.reshape(EXPERTS, SLOTS, -1), DP, split_axis=0, concat...]
    all_to_all x1 -> x0, blocking collectives: 98.6 us -> none  [to_experts(): lax.all_to_all(rows.reshape(EXPERTS, SLOTS, -1), DP, split_axis=0, concat...]
    reduce_scatter x3 -> x2, waiting for transfers between devices: 81.9 us -> 9.05 us  [scatter_plane(): return lax.psum_scatter(grads, PLANE, scatter_dimension=0, tiled=True)]
    all_gather x3 -> x1, waiting for transfers between devices: 86.8 us -> 35.9 us  [gather_plane(): lax.all_gather(pairs, PLANE, axis=1, tiled=True).reshape(64 * rows, width)]
    all_to_all x3 -> x4, starting transfers between devices: 31.4 us -> 61 us  [to_experts(): lax.all_to_all(rows.reshape(EXPERTS, SLOTS, -1), DP, split_axis=0, concat...]
    ppermute x12 -> x11, waiting for transfers between devices: 86.5 us -> 78.6 us  [swap(): return lax.ppermute(x, axis, [(0, 1), (1, 0)])]
    ppermute x12 -> x11, starting transfers between devices: 19.2 us -> 17.1 us  [swap(): return lax.ppermute(x, axis, [(0, 1), (1, 0)])]
  transfers between devices with their start and end apart: 21 -> 18, of which waited for: 13 -> 16; matrix products, arithmetic and copies ran while one was open for 4% -> 5% of each run, Pallas kernels for 16% -> 20%
where the time goes in v1:
time: 643 us; the launch traced here: 641 us
  waiting for transfers between devices  346 us (54%)
  Pallas kernels  147 us (23%)
  starting transfers between devices  78.5 us (12%)
  blocking collectives  15.4 us (2%)
  other arithmetic  15.1 us (2%)
  between operations  14.1 us (2%)
  matrix products  14 us (2%)
  local copies, waits for them, and re-layouts  11.1 us (2%)
    all_to_all x4, waiting for transfers between devices, to_experts(): lax.all_to_all(rows.reshape(EXPERTS, SLOTS, -1), DP, split_axis=0, concat...  222 us
    ppermute x11, waiting for transfers between devices, swap(): return lax.ppermute(x, axis, [(0, 1), (1, 0)])  78.6 us
    all_to_all x4, starting transfers between devices, to_experts(): lax.all_to_all(rows.reshape(EXPERTS, SLOTS, -1), DP, split_axis=0, concat...  61 us
    all_gather x1, waiting for transfers between devices, gather_plane(): lax.all_gather(pairs, PLANE, axis=1, tiled=True).reshape(64 * rows, width)  35.9 us
    pallas_call x2, Pallas kernels, expert_grads(): call(expert_grad_kernel, (8,), [tile(WIDTH), tile(WIDTH), tile(HALF, half...  26.1 us
    pallas_call x1, Pallas kernels, expert_phase(): call(expert_kernel, (8,), [tile(WIDTH), tile(128, 12), tile(512), full((1...  21.2 us
    ppermute x11, starting transfers between devices, swap(): return lax.ppermute(x, axis, [(0, 1), (1, 0)])  17.1 us
    all_gather x1, blocking collectives, body(): lax.all_gather(jnp.concatenate(parts, axis=1), ('zh', 'zl'), axis=0, tile...  15.4 us
  transfers between devices with their start and end apart: 18, of which 16 were waited for; matrix products, arithmetic and copies ran while one was open for 5% of the time, Pallas kernels for 20%

profile of v1, /device:TPU:0, one launch (start us, length us, event | category | flops | bytes accessed | tf_op | source)
XLA Modules:
  0.0 640.9 jit_solution(7947293137931114727)
XLA Ops:
  10.5 15.4 %all-gather.1 = bf16[4,12,7296]{2,1,0:T(8,128)(2,1)S(1)} all-gather(bf16[1,12,7296]{2,1,0:T(8,128)(2,1)S(1)} %bitcast.59), channel_id=2, replica_groups=mesh['zh'=2,'x'=4,'y'=4,'c'=2,'zl'=2] {'zh','zl'}, dimensions={0}, use_global_device_ids=true | all-gather | bytes 875520 | tf_op jit(solution)/shard_map/all_gather | solution.py:670
  33.9 7.3 %shard_map.282.refs_0_ = bf16[2048,1664]{1,0:T(8,128)(2,1)} custom-call(f32[64,256]{1,0:T(8,128)} %slice_select_fusion.rank_ref, bf16[256,1664]{1,0:T(8,128)(2,1)} %pad_maximum_fusion.1.rows_ref), custom_call_target="tpu_custom_call" | custom-call | tf_op jit(solution)/shard_map/pallas_call | solution.py:131
  41.2 7.1 %collective-permute-done.refs_2_.gate_other_ref = bf16[1536,256]{1,0:T(8,128)(2,1)S(1)} collective-permute-done((bf16[1536,256]{1,0:T(8,128)(2,1)}, bf16[1536,256]{1,0:T(8,128)(2,1)S(1)}, u32[]{:S(2)}, u32[]{:S(2)}) %collective-permute-start) | collective-permute-done | bytes 786464 | tf_op jit(solution)/shard_map/ppermute | solution.py:45
  48.3 16.9 %collective-permute-done.1.refs_3_.up_other_ref = bf16[1536,256]{1,0:T(8,128)(2,1)S(1)} collective-permute-done((bf16[1536,256]{1,0:T(8,128)(2,1)}, bf16[1536,256]{1,0:T(8,128)(2,1)S(1)}, u32[]{:S(2)}, u32[]{:S(2)}) %collective-permute-start.1) | collective-permute-done | bytes 786464 | tf_op jit(solution)/shard_map/ppermute | solution.py:45
  65.1 13.8 %collective-permute-done.2.refs_4_.other_ref = bf16[256,1536]{1,0:T(8,128)(2,1)S(1)} collective-permute-done((bf16[256,1536]{1,0:T(8,128)(2,1)}, bf16[256,1536]{1,0:T(8,128)(2,1)S(1)}, u32[]{:S(2)}, u32[]{:S(2)}) %collective-permute-start.2) | collective-permute-done | bytes 786464 | tf_op jit(solution)/shard_map/ppermute | solution.py:45
  78.9 35.9 %all-gather.4.cloned.1.call-done = bf16[2,768,7296]{2,1,0:T(8,128)(2,1)} async-done(((bf16[2,24,7296]{2,1,0:T(8,128)(2,1)}), bf16[2,768,7296]{2,1,0:T(8,128)(2,1)}) %all-gather.4.cloned.1.call-update) | async-done | bytes 22413328 | tf_op jit(solution)/shard_map/all_gather | solution.py:85
  114.8 8.8 %all-to-all-start.1 = ((bf16[64,32,1664]{2,1,0:T(8,128)(2,1)}), bf16[64,32,1664]{2,1,0:T(8,128)(2,1)}, u32[]{:S(2)}, u32[]{:S(2)}) async-start(bf16[64,32,1664]{2,1,0:T(8,128)(2,1)} %bitcast.51), calls=%async_computation.1 | async-start | bytes 13631488 | tf_op jit(solution)/shard_map/all_to_all | solution.py:141
  123.6 12.0 %shard_map.280 = (bf16[256,1536]{1,0:T(8,128)(2,1)}, bf16[256,1536]{1,0:T(8,128)(2,1)}, bf16[256,1024]{1,0:T(8,128)(2,1)}, f32[12,256,256]{2,1,0:T(8,128)}, bf16...) custom-call(bf16[256,1536]{1,0:T(8,128)(2,1)} %hidden_ref.3, ...), custom_call_target="tpu_custom_call" | custom-call | tf_op jit(solution)/shard_map/pallas_call | solution.py:267
  135.6 6.9 %shard_map.281 = bf16[2048,1536]{1,0:T(8,128)(2,1)} custom-call(f32[64,256]{1,0:T(8,128)} %slice_select_fusion.rank_ref, bf16[256,1536]{1,0:T(8,128)(2,1)} %get-tuple-element.44.rows_ref.ffn_in_ref), custom_call_target="tpu_custom_call" | custom-call | tf_op jit(solution)/shard_map/pallas_call | solution.py:131
  142.5 68.7 %all-to-all-done.1 = bf16[64,32,1664]{2,1,0:T(8,128)(2,1)} async-done(((bf16[64,32,1664]{2,1,0:T(8,128)(2,1)}), bf16[64,32,1664]{2,1,0:T(8,128)(2,1)}, u32[]{:S(2)}, u32[]{:S(2)}) %all-to-all-start.1) | async-done | bytes 6815776 | tf_op jit(solution)/shard_map/all_to_all | solution.py:141
  211.2 19.4 %all-to-all-start = ((bf16[64,32,1536]{2,1,0:T(8,128)(2,1)}), bf16[64,32,1536]{2,1,0:T(8,128)(2,1)}, u32[]{:S(2)}, u32[]{:S(2)}) async-start(bf16[64,32,1536]{2,1,0:T(8,128)(2,1)} %bitcast.52), calls=%async_computation | async-start | bytes 12582912 | tf_op jit(solution)/shard_map/all_to_all | solution.py:141
  234.8 4.6 fusion.2
  244.9 5.8 fusion._after_ref.shared_cot_ref
  250.6 9.6 %shard_map.284.act_cot_ref = f32[2048,512]{1,0:T(8,128)} custom-call(bf16[2048,1664]{1,0:T(8,128)(2,1)} %bitcast.11.cot_ref.marks_ref, bf16[256,1536]{1,0:T(8,128)(2,1)} %bitcast.61, bf16[256,1536]{1,0:T(8,128)(2,1)} %copy-done.3), custom_call_target="tpu_custom_call" | custom-call | tf_op jit(solution)/shard_map/pallas_call | solution.py:282
  260.2 52.7 %all-to-all-done = bf16[64,32,1536]{2,1,0:T(8,128)(2,1)} async-done(((bf16[64,32,1536]{2,1,0:T(8,128)(2,1)}), bf16[64,32,1536]{2,1,0:T(8,128)(2,1)}, u32[]{:S(2)}, u32[]{:S(2)}) %all-to-all-start) | async-done | bytes 6291488 | tf_op jit(solution)/shard_map/all_to_all | solution.py:141
  313.0 21.2 %shard_map.285 = (bf16[2048,1664]{1,0:T(8,128)(2,1)}, bf16[2048,512]{1,0:T(8,128)(2,1)}, bf16[2048,512]{1,0:T(8,128)(2,1)}, bf16[2048,512]{1,0:T(8,128)(2,1)}) custom-call(bf16[2048,1536]{1,0:T(8,128)(2,1)} %bitcast.6.rows_ref, bf16[2048,1664]{1,0:T(8,128)(2,1)} %bitcast.11.cot_ref.marks_ref, f32[2048,512]{1,0:T(8,128)} %shard_map.284.act_cot_ref, ...), custom_call_target="tpu_custom_call" | custom-call | tf_op jit(solution)/shard_map/pallas_call | solution.py:346
  334.2 15.8 %all-to-all-start.3 = ((bf16[64,32,1664]{2,1,0:T(8,128)(2,1)}), bf16[64,32,1664]{2,1,0:T(8,128)(2,1)}, u32[]{:S(2)}, u32[]{:S(2)}) async-start(bf16[64,32,1664]{2,1,0:T(8,128)(2,1)} %bitcast.58), calls=%async_computation.3 | async-start | bytes 13631488 | tf_op jit(solution)/shard_map/all_to_all | solution.py:141
  350.0 7.1 %shard_map.286._after_ref = bf16[768,6144]{1,0:T(8,128)(2,1)} custom-call(bf16[256,1536]{1,0:T(8,128)(2,1)} %get-tuple-element.44.rows_ref.ffn_in_ref, bf16[256,2048]{1,0:T(8,128)(2,1)} %pad_maximum_fusion.pair_ref, bf16[256,1024]{1,0:T(8,128)(2,1)} %copy-done.11, bf16[256,1536]{1,0:T(8,128)(2,1)} %out_grad_ref.1, ...), custom_call_target="tpu_custom_call" | custom-call | flops 99999997952 | tf_op jit(solution)/shard_map/pallas_call | solution.py:427
  357.1 13.4 %shard_map.287 = (f32[1536,256]{1,0:T(8,128)}, f32[1536,256]{1,0:T(8,128)}, f32[256,1536]{1,0:T(8,128)}) custom-call(bf16[2048,1536]{1,0:T(8,128)(2,1)} %bitcast.6.rows_ref, bf16[2048,1664]{1,0:T(8,128)(2,1)} %bitcast.11.cot_ref.marks_ref, bf16[2048,512]{1,0:T(8,128)(2,1)} %get-tuple-element.45._after_ref.act_ref, ...), custom_call_target="tpu_custom_call" | custom-call | flops 99999997952 | tf_op jit(solution)/shard_map/pallas_call | solution.py:403
  370.5 9.2 %shard_map.288._after_ref = bf16[2048,1536]{1,0:T(8,128)(2,1)} custom-call(bf16[2048,512]{1,0:T(8,128)(2,1)} %get-tuple-element.45._after_ref.act_ref, bf16[256,1536]{1,0:T(8,128)(2,1)} %bitcast.62, bf16[256,1536]{1,0:T(8,128)(2,1)} %copy-done.3, f32[1536,256]{1,0:T(8,128)} %get-tuple-element.48._after_ref), custom_call_target="tpu_custom_call" | custom-call | flops 99999997952 | tf_op jit(solution)/shard_map/pallas_call | solution.py:363
  379.7 75.0 %all-to-all-done.3 = bf16[64,32,1664]{2,1,0:T(8,128)(2,1)} async-done(((bf16[64,32,1664]{2,1,0:T(8,128)(2,1)}), bf16[64,32,1664]{2,1,0:T(8,128)(2,1)}, u32[]{:S(2)}, u32[]{:S(2)}) %all-to-all-start.3) | async-done | bytes 6815776 | tf_op jit(solution)/shard_map/all_to_all | solution.py:141
  454.7 17.1 %all-to-all-start.2 = ((bf16[64,32,1536]{2,1,0:T(8,128)(2,1)}), bf16[64,32,1536]{2,1,0:T(8,128)(2,1)}, u32[]{:S(2)}, u32[]{:S(2)}) async-start(bf16[64,32,1536]{2,1,0:T(8,128)(2,1)} %bitcast.53), calls=%async_computation.2 | async-start | bytes 12582912 | tf_op jit(solution)/shard_map/all_to_all | solution.py:141
  472.1 14.7 %shard_map.290 = (f32[256,1536]{1,0:T(8,128)}, bf16[256,1536]{1,0:T(8,128)(2,1)}, bf16[256,1536]{1,0:T(8,128)(2,1)}, bf16[256,128]{1,0:T(8,128)(2,1)}, bf16[256,1536]{1,0:T(8,128)(2,1)}) custom-call(f32[64,256]{1,0:T(8,128)} %slice_select_fusion.rank_ref, bf16[2048,1664]{1,0:T(8,128)(2,1)} %bitcast.18.back_ref, f32[256,1536]{1,0:T(8,128)} %fusion._after_ref.shared_cot_ref, ...), custom_call_target="tpu_custom_call" | custom-call | tf_op jit(solution)/shard_map/pallas_call | solution.py:498
  486.8 14.6 %shard_map.291 = (bf16[256,1536]{1,0:T(8,128)(2,1)}, bf16[256,512]{1,0:T(8,128)(2,1)}, bf16[256,512]{1,0:T(8,128)(2,1)}, f32[256,1536]{1,0:T(8,128)}, bf16[256,1536]{1,0:T(8,128)(2,1)}) custom-call(bf16[256,1536]{1,0:T(8,128)(2,1)} %get-tuple-element.50.q_ref, bf16[256,1024]{1,0:T(8,128)(2,1)} %get-tuple-element.51.k_ref.v_ref, ...), custom_call_target="tpu_custom_call" | custom-call | tf_op jit(solution)/shard_map/pallas_call | solution.py:580
  501.4 9.4 %shard_map.292._after_ref = bf16[768,8448]{1,0:T(8,128)(2,1)} custom-call(bf16[256,1536]{1,0:T(8,128)(2,1)} %get-tuple-element.59.attn_in_ref, bf16[256,1536]{1,0:T(8,128)(2,1)} %get-tuple-element.60.attended_ref, bf16[256,1536]{1,0:T(8,128)(2,1)} %get-tuple-element.44.rows_ref.ffn_in_ref, bf16[256,1536]{1,0:T(8,128)(2,1)} %get-tuple-element.61.gain_one_ref, ...), custom_call_target="tpu_custom_call" | custom-call | tf_op jit(solution)/shard_map/pallas_call | solution.py:640
  510.9 12.7 %shard_map.293 = (bf16[1536,256]{1,0:T(8,128)(2,1)}, bf16[1536,256]{1,0:T(8,128)(2,1)}, bf16[256,1536]{1,0:T(8,128)(2,1)}) custom-call(bf16[2048,1536]{1,0:T(8,128)(2,1)} %bitcast.6.rows_ref, bf16[2048,1664]{1,0:T(8,128)(2,1)} %bitcast.11.cot_ref.marks_ref, bf16[2048,512]{1,0:T(8,128)(2,1)} %get-tuple-element.45._after_ref.act_ref, ...), custom_call_target="tpu_custom_call" | custom-call | flops 99999997952 | tf_op jit(solution)/shard_map/pallas_call | solution.py:403
  525.6 25.7 %all-to-all-done.2 = bf16[64,32,1536]{2,1,0:T(8,128)(2,1)} async-done(((bf16[64,32,1536]{2,1,0:T(8,128)(2,1)}), bf16[64,32,1536]{2,1,0:T(8,128)(2,1)}, u32[]{:S(2)}, u32[]{:S(2)}) %all-to-all-start.2) | async-done | bytes 6291488 | tf_op jit(solution)/shard_map/all_to_all | solution.py:141
  551.3 8.6 %shard_map.289 = bf16[256,1536]{1,0:T(8,128)(2,1)} custom-call(f32[64,256]{1,0:T(8,128)} %slice_select_fusion.rank_ref, bf16[2048,1536]{1,0:T(8,128)(2,1)} %bitcast.16.rows_ref, f32[256,1536]{1,0:T(8,128)} %convolution_add_fusion.base_ref), custom_call_target="tpu_custom_call" | custom-call | flops 999999995904 | tf_op jit(solution)/shard_map/pallas_call | solution.py:161
  559.9 4.3 collective-permute-done.8
  566.7 14.4 %collective-permute-done.9 = bf16[1536,256]{1,0:T(8,128)(2,1)} collective-permute-done((bf16[1536,256]{1,0:T(8,128)(2,1)}, bf16[1536,256]{1,0:T(8,128)(2,1)}, u32[]{:S(2)}, u32[]{:S(2)}) %collective-permute-start.9) | collective-permute-done | bytes 786464 | tf_op jit(solution)/shard_map/ppermute | solution.py:45
  588.3 9.5 %collective-permute-done.10 = bf16[256,1536]{1,0:T(8,128)(2,1)S(1)} collective-permute-done((bf16[256,1536]{1,0:T(8,128)(2,1)S(1)}, bf16[256,1536]{1,0:T(8,128)(2,1)S(1)}, u32[]{:S(2)}, u32[]{:S(2)}) %collective-permute-start.10) | collective-permute-done | bytes 786464 | tf_op jit(solution)/shard_map/ppermute | solution.py:45
  608.0 9.0 %reduce-scatter.3.cloned.1.call-done = bf16[24,8448]{1,0:T(8,128)(2,1)} async-done(((bf16[768,8448]{1,0:T(8,128)(2,1)}), bf16[24,8448]{1,0:T(8,128)(2,1)}) %reduce-scatter.3.cloned.1.call-update) | async-done | bytes 405520 | tf_op jit(solution)/shard_map/reduce_scatter | solution.py:89
  (100 shorter events, 60.3 us)
Async XLA Ops:
  7.2 107.6 %all-gather.4.cloned.1.call-start = ((), (), s32[]{:S(2)}) async-start(), calls=%async_computation.6 | async-start | bytes 23113728 | tf_op jit(solution)/shard_map/all_gather | solution.py:85
  26.0 5.6 copy-start.12
  26.1 6.8 %copy-start.1 = (bf16[256,1536]{1,0:T(8,128)(2,1)S(1)}, bf16[256,1536]{1,0:T(8,128)(2,1)}, u32[]{:S(2)}) copy-start(bf16[256,1536]{1,0:T(8,128)(2,1)} %out_grad_ref.1) | copy-start | bytes 2359300
  27.2 21.1 %collective-permute-start = (bf16[1536,256]{1,0:T(8,128)(2,1)}, bf16[1536,256]{1,0:T(8,128)(2,1)S(1)}, u32[]{:S(2)}, u32[]{:S(2)}) collective-permute-start(bf16[1536,256]{1,0:T(8,128)(2,1)} %bitcast.63), channel_id=1, source_target_pairs={{0,1},{1,0},{2,3},{3,2},{4,5},{5,4},{6,7},{7,6},{8,9},{9,8},{10,11... | collective-permute-start | bytes 2359304 | tf_op jit(solution)/shard_map/ppermute | solution.py:45
  29.6 35.5 %collective-permute-start.1 = (bf16[1536,256]{1,0:T(8,128)(2,1)}, bf16[1536,256]{1,0:T(8,128)(2,1)S(1)}, u32[]{:S(2)}, u32[]{:S(2)}) collective-permute-start(bf16[1536,256]{1,0:T(8,128)(2,1)} %bitcast.65), channel_id=1, source_target_pairs={{0,1},{1,0},{2,3},{3,2},{4,5},{5,4},{6,7},{7,6},{8,9},{9,8},{10,11... | collective-permute-start | bytes 2359304 | tf_op jit(solution)/shard_map/ppermute | solution.py:45
  29.7 49.2 %collective-permute-start.2 = (bf16[256,1536]{1,0:T(8,128)(2,1)}, bf16[256,1536]{1,0:T(8,128)(2,1)S(1)}, u32[]{:S(2)}, u32[]{:S(2)}) collective-permute-start(bf16[256,1536]{1,0:T(8,128)(2,1)} %bitcast.60), channel_id=1, source_target_pairs={{0,1},{1,0},{2,3},{3,2},{4,5},{5,4},{6,7},{7,6},{8,9},{9,8},{10,11... | collective-permute-start | bytes 2359304 | tf_op jit(solution)/shard_map/ppermute | solution.py:45
  32.0 9.2 %copy-start.10 = (bf16[256,128]{1,0:T(8,128)(2,1)}, bf16[256,128]{1,0:T(8,128)(2,1)S(1)}, u32[]{:S(2)}) copy-start(bf16[256,128]{1,0:T(8,128)(2,1)S(1)} %convert.hits_ref) | copy-start | bytes 196612
  48.3 66.5 %copy-start.4 = (bf16[1536,256]{1,0:T(8,128)(2,1)}, bf16[1536,256]{1,0:T(8,128)(2,1)S(1)}, u32[]{:S(2)}) copy-start(bf16[1536,256]{1,0:T(8,128)(2,1)S(1)} %collective-permute-done.refs_2_.gate_other_ref) | copy-start | bytes 2359300
  65.1 49.7 %copy-start.5 = (bf16[1536,256]{1,0:T(8,128)(2,1)}, bf16[1536,256]{1,0:T(8,128)(2,1)S(1)}, u32[]{:S(2)}) copy-start(bf16[1536,256]{1,0:T(8,128)(2,1)S(1)} %collective-permute-done.1.refs_3_.up_other_ref) | copy-start | bytes 2359300
  78.9 35.9 %copy-start.3 = (bf16[256,1536]{1,0:T(8,128)(2,1)}, bf16[256,1536]{1,0:T(8,128)(2,1)S(1)}, u32[]{:S(2)}) copy-start(bf16[256,1536]{1,0:T(8,128)(2,1)S(1)} %collective-permute-done.2.refs_4_.other_ref) | copy-start | bytes 2359300
  114.8 96.4 %all-to-all-start.1 = ((bf16[64,32,1664]{2,1,0:T(8,128)(2,1)}), bf16[64,32,1664]{2,1,0:T(8,128)(2,1)}, u32[]{:S(2)}, u32[]{:S(2)}) async-start(bf16[64,32,1664]{2,1,0:T(8,128)(2,1)} %bitcast.51), calls=%async_computation.1 | async-start | bytes 13631488 | tf_op jit(solution)/shard_map/all_to_all | solution.py:141
  211.2 101.7 %all-to-all-start = ((bf16[64,32,1536]{2,1,0:T(8,128)(2,1)}), bf16[64,32,1536]{2,1,0:T(8,128)(2,1)}, u32[]{:S(2)}, u32[]{:S(2)}) async-start(bf16[64,32,1536]{2,1,0:T(8,128)(2,1)} %bitcast.52), calls=%async_computation | async-start | bytes 12582912 | tf_op jit(solution)/shard_map/all_to_all | solution.py:141
  233.7 1.1 copy-start.2
  240.7 4.2 copy-start.11
  240.7 2.0 copy-start
  334.2 120.6 %all-to-all-start.3 = ((bf16[64,32,1664]{2,1,0:T(8,128)(2,1)}), bf16[64,32,1664]{2,1,0:T(8,128)(2,1)}, u32[]{:S(2)}, u32[]{:S(2)}) async-start(bf16[64,32,1664]{2,1,0:T(8,128)(2,1)} %bitcast.58), calls=%async_computation.3 | async-start | bytes 13631488 | tf_op jit(solution)/shard_map/all_to_all | solution.py:141
  349.9 233.7 %reduce-scatter.5.cloned.1.call-start = ((), (), s32[]{:S(2)}) async-start(), calls=%async_computation.8 | async-start | bytes 9732096 | tf_op jit(solution)/shard_map/reduce_scatter | solution.py:89
  454.7 96.6 %all-to-all-start.2 = ((bf16[64,32,1536]{2,1,0:T(8,128)(2,1)}), bf16[64,32,1536]{2,1,0:T(8,128)(2,1)}, u32[]{:S(2)}, u32[]{:S(2)}) async-start(bf16[64,32,1536]{2,1,0:T(8,128)(2,1)} %bitcast.53), calls=%async_computation.2 | async-start | bytes 12582912 | tf_op jit(solution)/shard_map/all_to_all | solution.py:141
  471.8 145.2 %reduce-scatter.3.cloned.1.call-start = ((), (), s32[]{:S(2)}) async-start(), calls=%async_computation.7 | async-start | bytes 13381632 | tf_op jit(solution)/shard_map/reduce_scatter | solution.py:89
  523.5 40.6 %collective-permute-start.8 = (bf16[1536,256]{1,0:T(8,128)(2,1)}, bf16[1536,256]{1,0:T(8,128)(2,1)}, u32[]{:S(2)}, u32[]{:S(2)}) collective-permute-start(bf16[1536,256]{1,0:T(8,128)(2,1)} %get-tuple-element.68), channel_id=1, source_target_pairs={{0,1},{1,0},{2,3},{3,2},{4,5},{5,4},{6,7},{7,6},{8,9},{9,8},{10,11... | collective-permute-start | bytes 2359304 | tf_op jit(solution)/shard_map/ppermute | solution.py:45
  524.0 57.1 %collective-permute-start.9 = (bf16[1536,256]{1,0:T(8,128)(2,1)}, bf16[1536,256]{1,0:T(8,128)(2,1)}, u32[]{:S(2)}, u32[]{:S(2)}) collective-permute-start(bf16[1536,256]{1,0:T(8,128)(2,1)} %get-tuple-element.70), channel_id=1, source_target_pairs={{0,1},{1,0},{2,3},{3,2},{4,5},{5,4},{6,7},{7,6},{8,9},{9,8},{10,11... | collective-permute-start | bytes 2359304 | tf_op jit(solution)/shard_map/ppermute | solution.py:45
  551.3 8.6 %copy-start.13 = (bf16[256,1536]{1,0:T(8,128)(2,1)S(1)}, bf16[256,1536]{1,0:T(8,128)(2,1)}, u32[]{:S(2)}) copy-start(bf16[256,1536]{1,0:T(8,128)(2,1)} %get-tuple-element.72) | copy-start | bytes 2359300
  551.3 12.9 %copy-start.8 = (f32[1536,256]{1,0:T(8,128)S(1)}, f32[1536,256]{1,0:T(8,128)}, u32[]{:S(2)}) copy-start(f32[1536,256]{1,0:T(8,128)} %get-tuple-element.48._after_ref) | copy-start | bytes 4718596
  559.9 21.1 %copy-start.7 = (f32[1536,256]{1,0:T(8,128)S(1)}, f32[1536,256]{1,0:T(8,128)}, u32[]{:S(2)}) copy-start(f32[1536,256]{1,0:T(8,128)} %get-tuple-element.69) | copy-start | bytes 4718596
  559.9 37.9 %collective-permute-start.10 = (bf16[256,1536]{1,0:T(8,128)(2,1)S(1)}, bf16[256,1536]{1,0:T(8,128)(2,1)S(1)}, u32[]{:S(2)}, u32[]{:S(2)}) collective-permute-start(bf16[256,1536]{1,0:T(8,128)(2,1)S(1)} %copy-done.13), channel_id=1, source_target_pairs={{0,1},{1,0},{2,3},{3,2},{4,5},{5,4},{6,7},{7,6},{8,9},{9,8},{10,11... | collective-permute-start | bytes 2359304 | tf_op jit(solution)/shard_map/ppermute | solution.py:45
  581.0 16.7 %copy-start.6 = (f32[256,1536]{1,0:T(8,128)S(1)}, f32[256,1536]{1,0:T(8,128)}, u32[]{:S(2)}) copy-start(f32[256,1536]{1,0:T(8,128)} %get-tuple-element.71) | copy-start | bytes 4718596
  583.6 19.5 %copy-start.9 = (bf16[24,6144]{1,0:T(8,128)(2,1)S(1)}, bf16[24,6144]{1,0:T(8,128)(2,1)}, u32[]{:S(2)}) copy-start(bf16[24,6144]{1,0:T(8,128)(2,1)} %reduce-scatter.5.cloned.1.call-done) | copy-start | bytes 884740
  584.7 18.4 %collective-permute-start.5 = (bf16[24,3072]{1,0:T(8,128)(2,1)S(1)}, bf16[24,3072]{1,0:T(8,128)(2,1)S(1)}, u32[]{:S(2)}, u32[]{:S(2)}) collective-permute-start(bf16[24,3072]{1,0:T(8,128)(2,1)S(1)} %broadcast_select_fusion.1), channel_id=1, source_target_pairs={{0,64},{64,0},{1,65},{65,1},{2,66},{66,2},{3,67},{67,3},{4,68},{68... | collective-permute-start | bytes 442376 | tf_op jit(solution)/shard_map/ppermute | solution.py:45
  603.2 4.1 collective-permute-start.7
  604.0 17.3 %collective-permute-start.6 = (bf16[12,2048]{1,0:T(8,128)(2,1)S(1)}, bf16[12,2048]{1,0:T(8,128)(2,1)S(1)}, u32[]{:S(2)}, u32[]{:S(2)}) collective-permute-start(bf16[12,2048]{1,0:T(8,128)(2,1)S(1)} %select_convert_fusion.1), channel_id=1, source_target_pairs={{0,1},{1,0},{2,3},{3,2},{4,5},{5,4},{6,7},{7,6},{8,9},{9,8},{10,11... | collective-permute-start | bytes 147464 | tf_op jit(solution)/shard_map/ppermute | solution.py:45
  618.1 7.4 %collective-permute-start.3 = (bf16[24,4224]{1,0:T(8,128)(2,1)S(1)}, bf16[24,4224]{1,0:T(8,128)(2,1)S(1)}, u32[]{:S(2)}, u32[]{:S(2)}) collective-permute-start(bf16[24,4224]{1,0:T(8,128)(2,1)S(1)} %broadcast_select_fusion), channel_id=1, source_target_pairs={{0,64},{64,0},{1,65},{65,1},{2,66},{66,2},{3,67},{67,3},{4,68},{68... | collective-permute-start | bytes 608264 | tf_op jit(solution)/shard_map/ppermute | solution.py:45
  626.6 5.1 collective-permute-start.4
Sparse Core Ops, SparseCore 0:
  27.3 87.4 all-gather.3
  357.2 116.5 reduce-scatter.4
  511.0 105.9 reduce-scatter.2

commit v2 on v1

v2 whole, which is shorter than its diff:
```python
import jax
import jax.numpy as jnp
from jax import lax
from jax.experimental import pallas as pl
from jax.experimental.pallas import tpu as pltpu
from jax.sharding import Mesh, PartitionSpec as P

GROUP = 3
HEAD = 128
EXPERTS = 64
SLOTS = 32
TOKENS = 256
WIDTH = 1536
SHARED = 1024
HALF = 256
ROWS = EXPERTS * SLOTS
WIDE = WIDTH + 128
PACK = 2 * WIDTH + 1024 + 128

EPSILON = 1e-06
NEGATIVE = -1e30
SCALING = HEAD ** (-0.5)
BF = jnp.bfloat16
F32 = jnp.float32

AXES = ("zh", "x", "y", "c", "zl")
DP = ("zh", "x", "y", "c")
PLANE = ("x", "y", "c")
ANY = pl.BlockSpec(memory_space=pl.ANY)


def mm(a, b):
    return jnp.dot(a, b, preferred_element_type=F32)


def mm_l(a, b):
    return lax.dot_general(a, b, (((0,), (0,)), ((), ())), preferred_element_type=F32)


def mm_r(a, b):
    return lax.dot_general(a, b, (((1,), (1,)), ((), ())), preferred_element_type=F32)


def swap(x, axis):
    return lax.ppermute(x, axis, [(0, 1), (1, 0)])


def out(shape, dtype):
    return jax.ShapeDtypeStruct(shape, dtype)


def full(shape):
    return pl.BlockSpec(shape, lambda *i: (0,) * len(shape))


def call(kernel, grid, in_specs, out_specs, out_shape, scratch=(), flops=0, aliases=None):
    return pl.pallas_call(
        kernel,
        grid=grid,
        in_specs=in_specs,
        out_specs=out_specs,
        out_shape=out_shape,
        scratch_shapes=list(scratch),
        input_output_aliases=aliases or {},
        compiler_params=pltpu.CompilerParams(vmem_limit_bytes=56 * 1024 * 1024),
        cost_estimate=pl.CostEstimate(flops=flops, bytes_accessed=0, transcendentals=0),
    )


def fetch(source, target, sem):
    copy = pltpu.make_async_copy(source, target, sem)
    copy.start()
    return copy


def tie_kernel(*refs):
    pass


def tie(x, *after):
    return pl.pallas_call(
        tie_kernel,
        in_specs=[ANY] * (1 + len(after)),
        out_specs=ANY,
        out_shape=out(x.shape, x.dtype),
        input_output_aliases={0: 0},
    )(x, *after)


def gather_plane(pairs):
    _, rows, width = pairs.shape
    return lax.all_gather(pairs, PLANE, axis=1, tiled=True).reshape(64 * rows, width)


def scatter_plane(grads):
    return lax.psum_scatter(grads, PLANE, scatter_dimension=0, tiled=True)


def sum_zh(plane):
    width = plane.shape[1] // 2
    zh = lax.axis_index("zh")
    low, high = plane[:, :width], plane[:, width:]
    keep = jnp.where(zh == 0, low, high)
    give = jnp.where(zh == 0, high, low)
    return keep.astype(F32) + swap(give, "zh").astype(F32)


def sum_zl(mine, other):
    zl = lax.axis_index("zl")
    keep = jnp.where(zl == 0, mine, other)
    give = jnp.where(zl == 0, other, mine).astype(BF)
    return keep + swap(give, "zl").astype(F32)


def fold_down(rows):
    tail = [rows[:, :8, 1024:], rows[:, 8:, 1024:]]
    return jnp.concatenate([rows[:, :, :1024], jnp.concatenate(tail, axis=2)], axis=1)


def unfold_down(rows):
    tail = jnp.concatenate([rows[:, 16:, :512], rows[:, 16:, 512:]], axis=1)
    return jnp.concatenate([rows[:, :16], tail], axis=2)


def deal_kernel(rank_ref, cot_ref, hits_ref, deal_ref, turned_ref, out_ref):
    rank = rank_ref[...]
    slot = lax.broadcasted_iota(jnp.int32, (8, SLOTS, TOKENS), 1).astype(F32)
    hit = jnp.where(rank[:, None, :] == slot, 1.0, 0.0).reshape(8 * SLOTS, TOKENS)
    deal = hit.astype(BF)
    deal_ref[...] = deal
    turned_ref[...] = jnp.transpose(hit).astype(BF)
    out_ref[:, :WIDTH] = mm(deal, cot_ref[...]).astype(BF)
    out_ref[:, WIDTH:] = mm(deal, hits_ref[...]).astype(BF)


def deal_out(rank, out_grad, hits):
    return call(
        deal_kernel,
        (8,),
        [
            pl.BlockSpec((8, TOKENS), lambda i: (i, 0)),
            full((TOKENS, WIDTH)),
            full((TOKENS, 128)),
        ],
        [
            pl.BlockSpec((256, TOKENS), lambda i: (i, 0)),
            pl.BlockSpec((TOKENS, 256), lambda i: (0, i)),
            pl.BlockSpec((256, WIDE), lambda i: (i, 0)),
        ],
        [out((ROWS, TOKENS), BF), out((TOKENS, ROWS), BF), out((ROWS, WIDE), BF)],
    )(rank, out_grad, hits)


def dispatch_kernel(deal_ref, rows_ref, out_ref):
    out_ref[...] = mm(deal_ref[...], rows_ref[...]).astype(BF)


def dispatch(deal, rows):
    return call(
        dispatch_kernel,
        (6,),
        [full((ROWS, TOKENS)), pl.BlockSpec((TOKENS, 256), lambda j: (0, j))],
        pl.BlockSpec((ROWS, 256), lambda j: (0, j)),
        out((ROWS, WIDTH), BF),
    )(deal, rows)


def to_experts(rows):
    return lax.all_to_all(
        rows.reshape(EXPERTS, SLOTS, -1), DP, split_axis=0, concat_axis=0, tiled=True
    ).reshape(ROWS, -1)


def result_kernel(turned_ref, rows_ref, base_ref, out_ref, acc):
    step = pl.program_id(0)

    @pl.when(step == 0)
    def _():
        acc[...] = base_ref[...]

    acc[...] += mm(turned_ref[...], rows_ref[...])

    @pl.when(step == 3)
    def _():
        out_ref[...] = acc[...].astype(BF)


def add_results(turned, rows, base):
    return call(
        result_kernel,
        (4,),
        [
            pl.BlockSpec((TOKENS, 512), lambda i: (0, i)),
            pl.BlockSpec((512, WIDTH), lambda i: (i, 0)),
            full((TOKENS, WIDTH)),
        ],
        full((TOKENS, WIDTH)),
        out((TOKENS, WIDTH), BF),
        [pltpu.VMEM((TOKENS, WIDTH), F32)],
        flops=10**13,
    )(turned, rows, base)


def root_scale(values):
    return lax.rsqrt(jnp.mean(values * values, axis=-1, keepdims=True) + EPSILON)


def forward_kernel(
    hidden_ref,
    docs_ref,
    hits_ref,
    pack_ref,
    attn_in_ref,
    q_ref,
    kv_ref,
    probs_ref,
    attended_ref,
    middle_ref,
    ffn_in_ref,
    gates_ref,
    gains_ref,
    small_ref,
    wq_ref,
    wkv_ref,
    wo_ref,
    sems,
):
    copies = [
        fetch(pack_ref.at[:, at : at + ref.shape[1]], ref, sems.at[i])
        for i, (at, ref) in enumerate(
            [(2 * WIDTH + 1024, small_ref), (0, wq_ref), (2 * WIDTH, wkv_ref), (WIDTH, wo_ref)]
        )
    ]
    copies[0].wait()
    gains = jnp.transpose(small_ref[...].astype(F32))
    gains_ref[...] = gains[64:72]
    gain_one, gain_two = gains[64:65], gains[65:66]
    tokens = hidden_ref[...].astype(F32)
    attn_in_ref[...] = (tokens * root_scale(tokens) * gain_one).astype(BF)
    copies[1].wait()
    for j in range(0, WIDTH, 512):
        q_ref[:, j : j + 512] = mm(attn_in_ref[...], wq_ref[:, j : j + 512]).astype(BF)
    copies[2].wait()
    for j in range(0, 1024, 512):
        kv_ref[:, j : j + 512] = mm(attn_in_ref[...], wkv_ref[:, j : j + 512]).astype(BF)
    first = docs_ref[0, 0]
    second = first + docs_ref[0, 1]
    third = second + docs_ref[0, 2]
    row = lax.broadcasted_iota(jnp.int32, (TOKENS, TOKENS), 0)
    col = lax.broadcasted_iota(jnp.int32, (TOKENS, TOKENS), 1)

    def segment(place):
        return (
            (place >= first).astype(jnp.int32)
            + (place >= second).astype(jnp.int32)
            + (place >= third).astype(jnp.int32)
        )

    visible = (segment(row) == segment(col)) & (row >= col)
    for kv_head in range(4):
        key = kv_ref[:, kv_head * HEAD : (kv_head + 1) * HEAD]
        value = kv_ref[:, 512 + kv_head * HEAD : 512 + (kv_head + 1) * HEAD]
        for head in range(kv_head * GROUP, (kv_head + 1) * GROUP):
            at = slice(head * HEAD, (head + 1) * HEAD)
            scores = jnp.where(visible, mm_r(q_ref[:, at], key) * SCALING, NEGATIVE)
            exponent = jnp.exp(scores - jnp.max(scores, axis=-1, keepdims=True))
            probs = exponent / jnp.sum(exponent, axis=-1, keepdims=True)
            probs_ref[head] = probs
            attended_ref[:, at] = mm(probs.astype(BF), value).astype(BF)
    copies[3].wait()
    for j in range(0, WIDTH, 512):
        at = slice(j, j + 512)
        middle_ref[:, at] = hidden_ref[:, at].astype(F32) + mm(
            attended_ref[...], wo_ref[:, at]
        )
    middle = middle_ref[...]
    ffn_in_ref[...] = (middle * root_scale(middle) * gain_two).astype(BF)
    logits = mm(ffn_in_ref[...], small_ref[...])
    hits = hits_ref[...] > 0
    top = jnp.max(jnp.where(hits, logits, NEGATIVE), axis=-1, keepdims=True)
    weight = jnp.where(hits, jnp.exp(jnp.where(hits, logits - top, 0.0)), 0.0)
    gates_ref[...] = weight / jnp.sum(weight, axis=-1, keepdims=True)


def forward(hidden, docs, hits, pack):
    wide = (TOKENS, WIDTH)
    shapes = [
        (wide, BF),
        (wide, BF),
        ((TOKENS, 1024), BF),
        ((12, TOKENS, TOKENS), F32),
        (wide, BF),
        (wide, F32),
        (wide, BF),
        ((TOKENS, 128), F32),
        ((8, WIDTH), F32),
    ]
    return call(
        forward_kernel,
        (1,),
        [full(wide), pl.BlockSpec(memory_space=pltpu.SMEM), full((TOKENS, 128)), ANY],
        [full(s) for s, _ in shapes],
        [out(s, d) for s, d in shapes],
        [pltpu.VMEM((WIDTH, w), BF) for w in (128, WIDTH, 1024, WIDTH)]
        + [pltpu.SemaphoreType.DMA((4,))],
    )(hidden, docs, hits, pack)


def act_cot_kernel(cot_ref, down_ref, other_ref, _after_ref, out_ref):
    out_ref[:, :HALF] = mm_r(cot_ref[...], down_ref[...])
    out_ref[:, HALF:] = mm_r(cot_ref[...], other_ref[...])


def act_cots(cot_rows, down, other, after):
    return call(
        act_cot_kernel,
        (8,),
        [
            pl.BlockSpec((256, WIDTH), lambda i: (i, 0)),
            full((HALF, WIDTH)),
            full((HALF, WIDTH)),
            ANY,
        ],
        pl.BlockSpec((256, 2 * HALF), lambda i: (i, 0)),
        out((ROWS, 2 * HALF), F32),
    )(cot_rows, down, other, after)


def expert_kernel(
    rows_ref,
    marks_ref,
    act_cot_ref,
    own_ref,
    small_ref,
    gate_ref,
    gate_other_ref,
    up_ref,
    up_other_ref,
    _after_ref,
    back_ref,
    act_ref,
    gate_cot_ref,
    up_cot_ref,
):
    rows = rows_ref[...]
    marks = marks_ref[...] > 0
    logits = mm(rows, small_ref[...])
    top = jnp.max(jnp.where(marks, logits, NEGATIVE), axis=-1, keepdims=True)
    weight = jnp.where(marks, jnp.exp(jnp.where(marks, logits - top, 0.0)), 0.0)
    own = own_ref[...]
    total = jnp.sum(weight, axis=-1, keepdims=True)
    mine = jnp.sum(weight * own, axis=-1, keepdims=True)
    route_gate = mine / jnp.where(total > 0, total, 1.0)
    share = jnp.zeros((256, 1), F32)
    for half, gate_w, up_w in ((0, gate_ref, up_ref), (1, gate_other_ref, up_other_ref)):
        at = slice(half * HALF, (half + 1) * HALF)
        gate = mm(rows, gate_w[...])
        upper = mm(rows, up_w[...])
        sig = 1.0 / (1.0 + jnp.exp(-gate))
        silu = gate * sig
        act_cot = act_cot_ref[:, at]
        act = route_gate * silu * upper
        act_ref[:, at] = act.astype(BF)
        share += jnp.sum(act_cot * act, axis=-1, keepdims=True)
        scaled = route_gate * act_cot
        gate_cot_ref[:, at] = (scaled * upper * (sig * (1.0 + gate * (1.0 - sig)))).astype(BF)
        up_cot_ref[:, at] = (scaled * silu).astype(BF)
    for j in range(0, WIDTH, 512):
        at = slice(j, j + 512)
        total = mm_r(gate_cot_ref[:, :HALF], gate_ref[at, :])
        total += mm_r(gate_cot_ref[:, HALF:], gate_other_ref[at, :])
        total += mm_r(up_cot_ref[:, :HALF], up_ref[at, :])
        total += mm_r(up_cot_ref[:, HALF:], up_other_ref[at, :])
        back_ref[:, at] = total.astype(BF)
    high = share.astype(BF).astype(F32)
    lane = lax.broadcasted_iota(jnp.int32, (1, 128), 1)
    placed = jnp.where(lane < 64, high, share - high) * (own + pltpu.roll(own, 64, 1))
    back_ref[:, WIDTH:] = placed.astype(BF)


def expert_phase(rows, cot_rows, act_cot, own, pack, weights, after):
    tile = lambda w, j=0: pl.BlockSpec((256, w), lambda i: (i, j))
    small = pl.BlockSpec((WIDTH, 128), lambda i: (0, 32))
    return call(
        expert_kernel,
        (8,),
        [tile(WIDTH), tile(128, 12), tile(512), full((1, 128)), small]
        + [full(w.shape) for w in weights]
        + [ANY],
        [tile(WIDE), tile(512), tile(512), tile(512)],
        [out((ROWS, WIDE), BF)] + [out((ROWS, 512), BF)] * 3,
    )(rows, cot_rows, act_cot, own, pack, *weights, after)


def expert_out_kernel(act_ref, down_ref, other_ref, _after_ref, out_ref):
    total = mm(act_ref[:, :HALF], down_ref[...]) + mm(act_ref[:, HALF:], other_ref[...])
    out_ref[...] = total.astype(BF)


def expert_outs(act, down, other, after):
    return call(
        expert_out_kernel,
        (8,),
        [
            pl.BlockSpec((256, 512), lambda i: (i, 0)),
            full((HALF, WIDTH)),
            full((HALF, WIDTH)),
            ANY,
        ],
        pl.BlockSpec((256, WIDTH), lambda i: (i, 0)),
        out((ROWS, WIDTH), BF),
    )(act, down, other, after)


def expert_grad_kernel(
    rows_ref, cot_ref, act_ref, gate_cot_ref, up_cot_ref, _after_ref, gate_ref, up_ref, down_ref, gate, up, down
):
    step = pl.program_id(0)

    @pl.when(step == 0)
    def _():
        gate[...] = jnp.zeros_like(gate)
        up[...] = jnp.zeros_like(up)
        down[...] = jnp.zeros_like(down)

    gate[...] += mm_l(rows_ref[...], gate_cot_ref[...])
    up[...] += mm_l(rows_ref[...], up_cot_ref[...])
    down[...] += mm_l(act_ref[...], cot_ref[...])

    @pl.when(step == 7)
    def _():
        gate_ref[...] = gate[...].astype(gate_ref.dtype)
        up_ref[...] = up[...].astype(up_ref.dtype)
        down_ref[...] = down[...].astype(down_ref.dtype)


def expert_grads(half, dtype, rows, cot_rows, act, gate_cot, up_cot, after):
    tile = lambda w, j=0: pl.BlockSpec((256, w), lambda i: (i, j))
    shapes = [(WIDTH, HALF), (WIDTH, HALF), (HALF, WIDTH)]
    return call(
        expert_grad_kernel,
        (8,),
        [tile(WIDTH), tile(WIDTH), tile(HALF, half), tile(HALF, half), tile(HALF, half), ANY],
        [full(s) for s in shapes],
        [out(s, dtype) for s in shapes],
        [pltpu.VMEM(s, F32) for s in shapes],
    )(rows, cot_rows, act, gate_cot, up_cot, after)


def shared_kernel(
    ffn_in_ref,
    out_grad_ref,
    middle_ref,
    second_ref,
    _after_ref,
    act_ref,
    pair_cot_ref,
    sum_ref,
    cot_ref,
    pair_w_ref,
    fold_ref,
    down_ref,
    tail_ref,
    sems,
):
    pair_copy = fetch(second_ref.at[:, : 2 * SHARED], pair_w_ref, sems.at[0])
    fold_copy = fetch(second_ref.at[:, 2 * SHARED :], fold_ref, sems.at[1])
    fold_copy.wait()
    for j in range(2):
        at = slice(j * 512, (j + 1) * 512)
        rows = fold_ref[:, at].astype(F32).reshape(64, 24, 512)
        down_ref[:, at] = rows[:, :16].reshape(SHARED, 512).astype(BF)
        tail_ref[:, j * 8 : (j + 1) * 8] = rows[:, 16:]
    down_ref[:, 1024:] = tail_ref[...].reshape(SHARED, 512).astype(BF)
    pair_copy.wait()
    for j in range(0, SHARED, 256):
        at = slice(j, j + 256)
        up_at = slice(SHARED + j, SHARED + j + 256)
        gate = mm(ffn_in_ref[...], pair_w_ref[:, at])
        upper = mm(ffn_in_ref[...], pair_w_ref[:, up_at])
        sig = 1.0 / (1.0 + jnp.exp(-gate))
        silu = gate * sig
        act_ref[:, at] = (silu * upper).astype(BF)
        cot = mm_r(out_grad_ref[...], down_ref[at, :])
        pair_cot_ref[:, at] = (cot * upper * (sig * (1.0 + gate * (1.0 - sig)))).astype(BF)
        pair_cot_ref[:, up_at] = (cot * silu).astype(BF)
    for j in range(0, WIDTH, 512):
        at = slice(j, j + 512)
        sum_ref[:, at] = middle_ref[:, at] + mm(act_ref[...], down_ref[:, at])
        cot_ref[:, at] = mm_r(pair_cot_ref[...], pair_w_ref[at, :])


def shared_phase(ffn_in, out_grad, middle, second, after):
    wide = (TOKENS, WIDTH)
    shapes = [((TOKENS, SHARED), BF), ((TOKENS, 2 * SHARED), BF), (wide, F32), (wide, F32)]
    return call(
        shared_kernel,
        (1,),
        [full(wide), full(wide), full(wide), ANY, ANY],
        [full(s) for s, _ in shapes],
        [out(s, d) for s, d in shapes],
        [
            pltpu.VMEM((WIDTH, 2 * SHARED), BF),
            pltpu.VMEM((WIDTH, 1024), BF),
            pltpu.VMEM((SHARED, WIDTH), BF),
            pltpu.VMEM((64, 16, 512), F32),
            pltpu.SemaphoreType.DMA((2,)),
        ],
    )(ffn_in, out_grad, middle, second, after)


def shared_grad_kernel(ffn_in_ref, pair_ref, act_ref, cot_ref, _after_ref, out_ref):
    for j in range(0, 2 * SHARED, 512):
        at = slice(j, j + 512)
        out_ref[:, at] = mm_l(ffn_in_ref[...], pair_ref[:, at]).astype(BF)
    for j in range(0, 1024, 512):
        body = mm_l(act_ref[...], cot_ref[:, j : j + 512]).reshape(32, 16, 512)
        tail = mm_l(act_ref[...], cot_ref[:, 1024:]).reshape(32, 16, 512)
        tail = tail[:, :8] if j == 0 else tail[:, 8:]
        both = jnp.concatenate([body, tail], axis=1).reshape(768, 512)
        out_ref[:, 2 * SHARED + j : 2 * SHARED + j + 512] = both.astype(BF)


def shared_grads(ffn_in, pair_low, shared_low, out_grad, after):
    return call(
        shared_grad_kernel,
        (2,),
        [
            pl.BlockSpec((TOKENS, 768), lambda h: (0, h)),
            full((TOKENS, 2 * SHARED)),
            pl.BlockSpec((TOKENS, 512), lambda h: (0, h)),
            full((TOKENS, WIDTH)),
            ANY,
        ],
        pl.BlockSpec((768, 2 * SHARED + 1024), lambda h: (0, h)),
        out((768, 4 * SHARED + 2048), BF),
    )(ffn_in, pair_low, shared_low, out_grad, after)


def norm_back(values, scale, gain, cot):
    weighted = cot * gain
    centre = jnp.mean(weighted * values, axis=-1, keepdims=True)
    return scale * weighted - values * (scale * scale * scale * centre)


def backward_kernel(*refs):
    n_in, n_out = 13, 8
    sources, outs, scratch = refs[:n_in], refs[n_in : n_in + n_out], refs[n_in + n_out :]
    back_hbm, pack_hbm = sources[:2]
    middle_low_ref, dq_ref, dkv_ref, grad_in_ref, logit_ref, one_ref, two_ref, cot_ref = outs
    back_ref, wo_ref, wq_ref, wkv_ref, small_ref, acc, sems = scratch[:7]
    held = scratch[7:]
    loads = [(back_hbm.at[:1024], back_ref.at[:1024]), (back_hbm.at[1024:], back_ref.at[1024:])]
    loads += [(a, b) for a, b in zip(sources[2:7], held[:5])]
    loads += [
        (pack_hbm.at[:, 2 * WIDTH + 1024 : PACK], small_ref),
        (pack_hbm.at[:, WIDTH : 2 * WIDTH], wo_ref),
    ]
    loads += [(a, b) for a, b in zip(sources[7:12], held[5:])]
    loads += [
        (pack_hbm.at[:, :WIDTH], wq_ref),
        (pack_hbm.at[:, 2 * WIDTH : 2 * WIDTH + 1024], wkv_ref),
    ]
    turned_ref, shared_ref, gates_ref, middle_ref, gains_ref = held[:5]
    out_grad_ref, q_ref, kv_ref, probs_ref, hidden_ref = held[5:]
    loads = [loads[2], loads[0], loads[1]] + loads[3:]
    copies = [fetch(a, b, sems.at[i]) for i, (a, b) in enumerate(loads)]
    for i in (0, 1):
        copies[i].wait()
    acc[...] = mm(turned_ref[:, :1024], back_ref[:1024])
    copies[2].wait()
    acc[...] += mm(turned_ref[:, 1024:], back_ref[1024:])
    for i in range(3, 10):
        copies[i].wait()
    extra = acc[:, WIDTH:]
    lane = lax.broadcasted_iota(jnp.int32, (1, 128), 1)
    shares = jnp.where(lane < 64, extra + pltpu.roll(extra, 64, 1), 0.0)
    logit = shares - gates_ref[...] * jnp.sum(shares, axis=-1, keepdims=True)
    logit_ref[...] = logit.astype(BF)
    cot = acc[:, :WIDTH] + shared_ref[...] + mm_r(logit_ref[...], small_ref[...])
    middle = middle_ref[...]
    scale = root_scale(middle)
    two_ref[...] = (cot * middle * scale).astype(BF)
    total = out_grad_ref[...].astype(F32) + norm_back(middle, scale, gains_ref[1:2], cot)
    grad_in_ref[...] = total
    middle_low_ref[...] = total.astype(BF)
    for j in range(0, WIDTH, 512):
        at = slice(j, j + 512)
        cot_ref[:, at] = mm_r(middle_low_ref[...], wo_ref[at, :]).astype(BF)
    for i in range(10, 14):
        copies[i].wait()
    for kv_head in range(4):
        key_at = slice(kv_head * HEAD, (kv_head + 1) * HEAD)
        value_at = slice(512 + kv_head * HEAD, 512 + (kv_head + 1) * HEAD)
        key, value = kv_ref[:, key_at], kv_ref[:, value_at]
        dk = jnp.zeros((TOKENS, HEAD), F32)
        dv = jnp.zeros((TOKENS, HEAD), F32)
        for head in range(kv_head * GROUP, (kv_head + 1) * GROUP):
            at = slice(head * HEAD, (head + 1) * HEAD)
            probs = probs_ref[head]
            head_cot = cot_ref[:, at]
            dprobs = mm_r(head_cot, value)
            dv += mm_l(probs.astype(BF), head_cot)
            centre = jnp.sum(probs * dprobs, axis=-1, keepdims=True)
            dscores = (probs * (dprobs - centre)).astype(BF)
            dq_ref[:, at] = (mm(dscores, key) * SCALING).astype(BF)
            dk += mm_l(dscores, q_ref[:, at])
        dkv_ref[:, key_at] = (dk * SCALING).astype(BF)
        dkv_ref[:, value_at] = dv.astype(BF)
    for i in range(14, 16):
        copies[i].wait()
    for j in range(0, WIDTH, 512):
        at = slice(j, j + 512)
        acc[:, at] = mm_r(dq_ref[...], wq_ref[at, :]) + mm_r(dkv_ref[...], wkv_ref[at, :])
    tokens = hidden_ref[...].astype(F32)
    scale = root_scale(tokens)
    cot = acc[:, :WIDTH]
    one_ref[...] = (cot * tokens * scale).astype(BF)
    grad_in_ref[...] += norm_back(tokens, scale, gains_ref[0:1], cot)


def backward(back, pack, turned, shared_cot, gates, middle, gains, out_grad, q, kv, probs, hidden, after):
    wide = (TOKENS, WIDTH)
    shapes = [
        (wide, BF),
        (wide, BF),
        ((TOKENS, 1024), BF),
        (wide, F32),
        ((TOKENS, 128), BF),
        (wide, BF),
        (wide, BF),
        (wide, BF),
    ]
    held = [turned, shared_cot, gates, middle, gains, out_grad, q, kv, probs, hidden]
    scratch = [
        pltpu.VMEM((ROWS, WIDE), BF),
        pltpu.VMEM((WIDTH, WIDTH), BF),
        pltpu.VMEM((WIDTH, WIDTH), BF),
        pltpu.VMEM((WIDTH, 1024), BF),
        pltpu.VMEM((WIDTH, 128), BF),
        pltpu.VMEM((TOKENS, WIDE), F32),
        pltpu.SemaphoreType.DMA((16,)),
    ] + [pltpu.VMEM(a.shape, a.dtype) for a in held]
    return call(
        backward_kernel,
        (1,),
        [ANY] * 13,
        [full(s) for s, _ in shapes],
        [out(s, d) for s, d in shapes],
        scratch,
    )(back, pack, *held, after)


def dense_grad_kernel(
    attn_in_ref,
    attended_ref,
    ffn_in_ref,
    gain_one_ref,
    gain_two_ref,
    dq_ref,
    middle_ref,
    dkv_ref,
    logit_ref,
    out_ref,
    held,
    sems,
):
    copies = []

    def send(at, width):
        where = slice(at, at + width)
        copies.append(fetch(held.at[:, where], out_ref.at[:, where], sems.at[len(copies)]))

    for half in range(2):
        rows = slice(half * 768, (half + 1) * 768)
        base = half * PACK
        attended = attended_ref[:, rows]
        for j in range(0, WIDTH, 512):
            at = base + WIDTH + j
            held[:, at : at + 512] = mm_l(attended, middle_ref[:, j : j + 512]).astype(BF)
        send(base + WIDTH, WIDTH)
        attn_in = attn_in_ref[:, rows]
        for j in range(0, WIDTH, 512):
            at = base + j
            held[:, at : at + 512] = mm_l(attn_in, dq_ref[:, j : j + 512]).astype(BF)
        send(base, WIDTH)
        for j in range(0, 1024, 512):
            at = base + 2 * WIDTH + j
            held[:, at : at + 512] = mm_l(attn_in, dkv_ref[:, j : j + 512]).astype(BF)
        lane = lax.broadcasted_iota(jnp.int32, (TOKENS, 128), 1)
        small = mm_l(ffn_in_ref[:, rows], logit_ref[...])
        small += mm_l(gain_one_ref[:, rows], jnp.where(lane == 64, 1.0, 0.0).astype(BF))
        small += mm_l(gain_two_ref[:, rows], jnp.where(lane == 65, 1.0, 0.0).astype(BF))
        held[:, base + 2 * WIDTH + 1024 : base + PACK] = small.astype(BF)
        send(base + 2 * WIDTH, 1024 + 128)
    for copy in copies:
        copy.wait()


def dense_grads(attn_in, attended, ffn_in, gain_one, gain_two, dq, middle_low, dkv, logit):
    ins = [attn_in, attended, ffn_in, gain_one, gain_two, dq, middle_low, dkv, logit]
    return call(
        dense_grad_kernel,
        (1,),
        [full(a.shape) for a in ins],
        ANY,
        out((768, 2 * PACK), BF),
        [pltpu.VMEM((768, 2 * PACK), BF), pltpu.SemaphoreType.DMA((6,))],
        flops=10**13,
    )(*ins)


def body(
    hidden_in,
    out_grad,
    doc_lengths,
    expert_ids,
    gain_attn,
    w_query,
    w_key,
    w_value,
    w_out,
    gain_ffn,
    w_router,
    w_shared_gate,
    w_shared_up,
    w_shared_down,
    expert_gate,
    expert_up,
    expert_down,
):
    parts = [w_query, w_out, w_key, w_value, w_router, gain_attn[:, None], gain_ffn[:, None]]
    parts += [jnp.zeros((12, 62), BF), w_shared_gate, w_shared_up, w_shared_down.reshape(12, 1024)]
    line = lax.all_gather(jnp.concatenate(parts, axis=1), ("zh", "zl"), axis=0, tiled=False)
    pack = gather_plane(line[:, :, :PACK].reshape(2, 24, PACK))
    pair_w = line[:, :, PACK : PACK + 2 * SHARED].reshape(2, 24, 2 * SHARED)
    down_w = fold_down(line[:, :, PACK + 2 * SHARED :].reshape(2, 16, WIDTH))
    second = gather_plane(jnp.concatenate([pair_w, down_w], axis=2))
    gate, up, down = expert_gate[0], expert_up[0], expert_down[0]
    gate_other, up_other, down_other = swap(gate, "zl"), swap(up, "zl"), swap(down, "zl")

    lanes = jnp.arange(128, dtype=jnp.int32)
    hits = jnp.any(expert_ids[:, :, None] == lanes, axis=1)
    hits_low = hits.astype(BF)
    place = jnp.arange(TOKENS, dtype=jnp.int32)
    earlier = (place[:, None] > place[None, :]).astype(BF)
    rank = jnp.where(hits, mm(earlier, hits_low), -1.0).T[:EXPERTS]
    own = (lanes == lax.axis_index(DP)).astype(F32)[None]

    deal, turned, send_cot = deal_out(rank, out_grad, hits_low)
    cot_rows = to_experts(tie(send_cot, line, gate_other, up_other))

    attn_in, q, kv, probs, attended, middle, ffn_in, gates, gains = forward(
        hidden_in, doc_lengths, hits_low, pack
    )
    send_rows = tie(dispatch(deal, ffn_in), down_other)
    rows = to_experts(send_rows)

    act_cot = act_cots(cot_rows, down, down_other, send_rows)
    weights = (gate, gate_other, up, up_other)
    back, act, gate_cot, up_cot = expert_phase(
        rows, cot_rows, act_cot, own, pack, weights, send_rows
    )
    shared_low, pair_low, shared_sum, shared_cot = shared_phase(
        ffn_in, out_grad, middle, second, act
    )
    shared_grad = shared_grads(ffn_in, pair_low, shared_low, out_grad, shared_cot)

    kept = expert_grads(0, F32, rows, cot_rows, act, gate_cot, up_cot, shared_grad)
    shared_grad = scatter_plane(shared_grad)
    sent = expert_grads(1, BF, rows, cot_rows, act, gate_cot, up_cot, kept[0])
    result = expert_outs(act, down, down_other, sent[0])
    back = to_experts(back)

    middle_low, dq, dkv, grad_in, logit, one_rows, two_rows, _ = backward(
        back, pack, turned, shared_cot, gates, middle, gains, out_grad, q, kv, probs, hidden_in, result
    )
    result = to_experts(result)
    dense_grad = dense_grads(
        attn_in, attended, ffn_in, one_rows, two_rows, dq, middle_low, dkv, logit
    )
    dense = sum_zh(scatter_plane(dense_grad))
    dense = sum_zl(dense[:12], dense[12:])
    shared_grad = sum_zh(shared_grad)
    pair_grad = shared_grad[:, : 2 * SHARED]
    down_grad = unfold_down(shared_grad[None, :, 2 * SHARED :])[0]
    pair_grad = sum_zl(pair_grad[:12], pair_grad[12:])
    down_grad = sum_zl(down_grad[:8], down_grad[8:])
    block_out = add_results(turned, result, shared_sum)
    sent = [tie(x, dense_grad) for x in sent]
    expert = [(k + swap(s, "zl").astype(F32))[None] for k, s in zip(kept, sent)]
    at = 2 * WIDTH
    return (
        block_out,
        grad_in,
        dense[:, at + 1088],
        dense[:, :WIDTH],
        dense[:, at : at + 512],
        dense[:, at + 512 : at + 1024],
        dense[:, WIDTH:at],
        dense[:, at + 1089],
        dense[:, at + 1024 : at + 1088],
        pair_grad[:, :SHARED],
        pair_grad[:, SHARED:],
        down_grad,
        expert[0],
        expert[1],
        expert[2],
    )


def solution(mesh):
    fine = Mesh(mesh.devices.reshape(2, 4, 4, 2, 2), AXES)
    rows, vector = P(AXES, None), P(AXES)
    banks = (P(DP, None, "zl"), P(DP, None, "zl"), P(DP, "zl", None))
    return jax.shard_map(
        body,
        mesh=fine,
        in_specs=(rows, rows, rows, rows, vector, rows, rows, rows, rows, vector)
        + (rows, rows, rows, rows)
        + banks,
        out_specs=(rows, rows, vector, rows, rows, rows, rows, vector)
        + (rows, rows, rows, rows)
        + banks,
        check_vma=False,
    )
```

time: 643 us -> 627 us (0.975); the launches traced: 641 us -> 616 us
  matrix products: 14 us -> 0.2 us
    all_gather x1 -> x2, waiting for transfers between devices: 35.9 us -> 78.1 us  [gather_plane(): lax.all_gather(pairs, PLANE, axis=1, tiled=True).reshape(64 * rows, width)]
    all_to_all x4, waiting for transfers between devices: 222 us -> 185 us  [to_experts(): lax.all_to_all(rows.reshape(EXPERTS, SLOTS, -1), DP, split_axis=0, concat...]
    ppermute x11, waiting for transfers between devices: 78.6 us -> 62.1 us  [swap(): return lax.ppermute(x, axis, [(0, 1), (1, 0)])]
    reduce_scatter x2, waiting for transfers between devices: 9.05 us -> 17.5 us  [scatter_plane(): return lax.psum_scatter(grads, PLANE, scatter_dimension=0, tiled=True)]
    dot_general x2 -> x0, matrix products: 7.06 us -> none  [mm_r(): lax.dot_general(a, b, (((1,), (1,)), ((), ())), preferred_element_type=F32)]
    dot_general x3 -> x1, matrix products: 6.98 us -> 0.2 us  [mm(): return jnp.dot(a, b, preferred_element_type=F32)]
  transfers between devices with their start and end apart: 18 -> 19, of which waited for: 16 -> 14; matrix products, arithmetic and copies ran while one was open for 5% -> 2% of each run, Pallas kernels for 20% -> 23%
where the time goes in v2:
time: 627 us; the launch traced here: 616 us
  waiting for transfers between devices  342 us (55%)
  Pallas kernels  143 us (23%)
  starting transfers between devices  77.8 us (12%)
  blocking collectives  15.4 us (2%)
  between operations  14.5 us (2%)
  other arithmetic  13.1 us (2%)
  local copies, waits for them, and re-layouts  9.81 us (2%)
    all_to_all x4, waiting for transfers between devices, to_experts(): lax.all_to_all(rows.reshape(EXPERTS, SLOTS, -1), DP, split_axis=0, concat...  185 us
    all_gather x2, waiting for transfers between devices, gather_plane(): lax.all_gather(pairs, PLANE, axis=1, tiled=True).reshape(64 * rows, width)  78.1 us
    ppermute x11, waiting for transfers between devices, swap(): return lax.ppermute(x, axis, [(0, 1), (1, 0)])  62.1 us
    all_to_all x4, starting transfers between devices, to_experts(): lax.all_to_all(rows.reshape(EXPERTS, SLOTS, -1), DP, split_axis=0, concat...  61.6 us
    pallas_call x2, Pallas kernels, expert_grads(): call(expert_grad_kernel, (8,), [tile(WIDTH), tile(WIDTH), tile(HALF, half...  26.4 us
    pallas_call x1, Pallas kernels, expert_phase(): call(expert_kernel, (8,), [tile(WIDTH), tile(128, 12), tile(512), full((1...  21.2 us
    reduce_scatter x2, waiting for transfers between devices, scatter_plane(): return lax.psum_scatter(grads, PLANE, scatter_dimension=0, tiled=True)  17.5 us
    pallas_call x1, Pallas kernels, backward(): call(backward_kernel, (1,), [ANY] * 13, [full(s) for s, _ in shapes], [ou...  16.2 us
  transfers between devices with their start and end apart: 19, of which 14 were waited for; matrix products, arithmetic and copies ran while one was open for 2% of the time, Pallas kernels for 23%

profile of v2, /device:TPU:0, one launch (start us, length us, event | category | flops | bytes accessed | tf_op | source)
XLA Modules:
  0.0 616.2 jit_solution(440196282952086101)
XLA Ops:
  10.5 15.4 %all-gather.1.refs_1_ = bf16[4,12,7296]{2,1,0:T(8,128)(2,1)S(1)} all-gather(bf16[1,12,7296]{2,1,0:T(8,128)(2,1)S(1)} %bitcast.40), channel_id=2, replica_groups=mesh['zh'=2,'x'=4,'y'=4,'c'=2,'zl'=2] {'zh','zl'}, dimensions={0}, use_global_device_ids=true | all-gather | bytes 875520 | tf_op jit(solution)/shard_map/all_gather | solution.py:734
  31.4 7.3 %shard_map.280 = (bf16[2048,256]{1,0:T(8,128)(2,1)}, bf16[256,2048]{1,0:T(8,128)(2,1)}, bf16[2048,1664]{1,0:T(8,128)(2,1)}) custom-call(f32[64,256]{1,0:T(8,128)} %slice_select_fusion.rank_ref, bf16[256,1536]{1,0:T(8,128)(2,1)} %refs_7_.1, bf16[256,128]{1,0:T(8,128)(2,1)} %convert.hits_ref), custom_call_target="tpu_custom_call" | custom-call | tf_op jit(solution)/shard_map/pallas_call | solution.py:137
  38.7 9.4 %collective-permute-done.1.refs_2_.gate_other_ref = bf16[1536,256]{1,0:T(8,128)(2,1)S(1)} collective-permute-done((bf16[1536,256]{1,0:T(8,128)(2,1)}, bf16[1536,256]{1,0:T(8,128)(2,1)S(1)}, u32[]{:S(2)}, u32[]{:S(2)}) %collective-permute-start.1) | collective-permute-done | bytes 786464 | tf_op jit(solution)/shard_map/ppermute | solution.py:45
  48.1 13.8 %collective-permute-done.2.refs_3_.up_other_ref = bf16[1536,256]{1,0:T(8,128)(2,1)S(1)} collective-permute-done((bf16[1536,256]{1,0:T(8,128)(2,1)}, bf16[1536,256]{1,0:T(8,128)(2,1)S(1)}, u32[]{:S(2)}, u32[]{:S(2)}) %collective-permute-start.2) | collective-permute-done | bytes 786464 | tf_op jit(solution)/shard_map/ppermute | solution.py:45
  62.7 9.2 %all-to-all-start.1 = ((bf16[64,32,1664]{2,1,0:T(8,128)(2,1)}), bf16[64,32,1664]{2,1,0:T(8,128)(2,1)}, u32[]{:S(2)}, u32[]{:S(2)}) async-start(bf16[64,32,1664]{2,1,0:T(8,128)(2,1)} %bitcast.34), calls=%async_computation.1 | async-start | bytes 13631488 | tf_op jit(solution)/shard_map/all_to_all | solution.py:169
  73.9 78.0 %all-gather.5.cloned.1.call-done = bf16[2,768,4224]{2,1,0:T(8,128)(2,1)} async-done(((bf16[2,24,4224]{2,1,0:T(8,128)(2,1)}), bf16[2,768,4224]{2,1,0:T(8,128)(2,1)}) %all-gather.5.cloned.1.call-update) | async-done | bytes 12976144 | tf_op jit(solution)/shard_map/all_gather | solution.py:92
  151.9 11.1 %shard_map.281 = (bf16[256,1536]{1,0:T(8,128)(2,1)}, bf16[256,1536]{1,0:T(8,128)(2,1)}, bf16[256,1024]{1,0:T(8,128)(2,1)}, f32[12,256,256]{2,1,0:T(8,128)}, bf16...) custom-call(bf16[256,1536]{1,0:T(8,128)(2,1)} %refs_11_.1, ...), custom_call_target="tpu_custom_call" | custom-call | tf_op jit(solution)/shard_map/pallas_call | solution.py:298
  163.0 6.8 %shard_map.282.refs_0_ = bf16[2048,1536]{1,0:T(8,128)(2,1)} custom-call(bf16[2048,256]{1,0:T(8,128)(2,1)} %get-tuple-element.49.deal_ref, bf16[256,1536]{1,0:T(8,128)(2,1)} %get-tuple-element.50.rows_ref.ffn_in_ref), custom_call_target="tpu_custom_call" | custom-call | tf_op jit(solution)/shard_map/pallas_call | solution.py:159
  170.7 20.1 %all-to-all-start = ((bf16[64,32,1536]{2,1,0:T(8,128)(2,1)}), bf16[64,32,1536]{2,1,0:T(8,128)(2,1)}, u32[]{:S(2)}, u32[]{:S(2)}) async-start(bf16[64,32,1536]{2,1,0:T(8,128)(2,1)} %bitcast.29), calls=%async_computation | async-start | bytes 12582912 | tf_op jit(solution)/shard_map/all_to_all | solution.py:169
  191.3 9.8 %shard_map.285.act_cot_ref = f32[2048,512]{1,0:T(8,128)} custom-call(bf16[2048,1664]{1,0:T(8,128)(2,1)} %bitcast.11.cot_ref.marks_ref, bf16[256,1536]{1,0:T(8,128)(2,1)} %bitcast.37, bf16[256,1536]{1,0:T(8,128)(2,1)} %copy-done.1, bf16[2048,1536]{1,0:T(8,128)(2,1)} %shard_map.283._after_ref), custom_call_target="tpu_custom_call" | custom-call | tf_op jit(solution)/shard_map/pallas_call | solution.py:315
  201.2 82.0 %all-to-all-done = bf16[64,32,1536]{2,1,0:T(8,128)(2,1)} async-done(((bf16[64,32,1536]{2,1,0:T(8,128)(2,1)}), bf16[64,32,1536]{2,1,0:T(8,128)(2,1)}, u32[]{:S(2)}, u32[]{:S(2)}) %all-to-all-start) | async-done | bytes 6291488 | tf_op jit(solution)/shard_map/all_to_all | solution.py:169
  283.2 21.2 %shard_map.286 = (bf16[2048,1664]{1,0:T(8,128)(2,1)}, bf16[2048,512]{1,0:T(8,128)(2,1)}, bf16[2048,512]{1,0:T(8,128)(2,1)}, bf16[2048,512]{1,0:T(8,128)(2,1)}) custom-call(bf16[2048,1536]{1,0:T(8,128)(2,1)} %bitcast.7.rows_ref, bf16[2048,1664]{1,0:T(8,128)(2,1)} %bitcast.11.cot_ref.marks_ref, f32[2048,512]{1,0:T(8,128)} %shard_map.285.act_cot_ref, ...), custom_call_target="tpu_custom_call" | custom-call | tf_op jit(solution)/shard_map/pallas_call | solution.py:384
  304.4 12.9 %all-to-all-start.3 = ((bf16[64,32,1664]{2,1,0:T(8,128)(2,1)}), bf16[64,32,1664]{2,1,0:T(8,128)(2,1)}, u32[]{:S(2)}, u32[]{:S(2)}) async-start(bf16[64,32,1664]{2,1,0:T(8,128)(2,1)} %bitcast.36), calls=%async_computation.3 | async-start | bytes 13631488 | tf_op jit(solution)/shard_map/all_to_all | solution.py:169
  317.3 12.1 %shard_map.287 = (bf16[256,1024]{1,0:T(8,128)(2,1)}, bf16[256,2048]{1,0:T(8,128)(2,1)}, f32[256,1536]{1,0:T(8,128)}, f32[256,1536]{1,0:T(8,128)}) custom-call(bf16[256,1536]{1,0:T(8,128)(2,1)} %get-tuple-element.50.rows_ref.ffn_in_ref, bf16[256,1536]{1,0:T(8,128)(2,1)} %refs_7_.1, f32[256,1536]{1,0:T(8,128)} %get-tuple-element.55.middle_ref.refs_5_, ...), custom_call_target="tpu_custom_call" | custom-call | tf_op jit(solution)/shard_map/pallas_call | solution.py:496
  329.5 7.1 %shard_map.288._after_ref = bf16[768,6144]{1,0:T(8,128)(2,1)} custom-call(bf16[256,1536]{1,0:T(8,128)(2,1)} %get-tuple-element.50.rows_ref.ffn_in_ref, bf16[256,2048]{1,0:T(8,128)(2,1)} %get-tuple-element.56.pair_ref, bf16[256,1024]{1,0:T(8,128)(2,1)} %get-tuple-element.57.act_ref, bf16[256,1536]{1,0:T(8,128)(2,1)} %refs_7_.1, ...), custom_call_target="tpu_custom_call" | custom-call | tf_op jit(solution)/shard_map/pallas_call | solution.py:525
  336.6 13.4 %shard_map.289 = (f32[1536,256]{1,0:T(8,128)}, f32[1536,256]{1,0:T(8,128)}, f32[256,1536]{1,0:T(8,128)}) custom-call(bf16[2048,1536]{1,0:T(8,128)(2,1)} %bitcast.7.rows_ref, bf16[2048,1664]{1,0:T(8,128)(2,1)} %bitcast.11.cot_ref.marks_ref, bf16[2048,512]{1,0:T(8,128)(2,1)} %get-tuple-element.52._after_ref.act_ref, ...), custom_call_target="tpu_custom_call" | custom-call | tf_op jit(solution)/shard_map/pallas_call | solution.py:440
  350.0 12.9 %shard_map.290 = (bf16[1536,256]{1,0:T(8,128)(2,1)}, bf16[1536,256]{1,0:T(8,128)(2,1)}, bf16[256,1536]{1,0:T(8,128)(2,1)}) custom-call(bf16[2048,1536]{1,0:T(8,128)(2,1)} %bitcast.7.rows_ref, bf16[2048,1664]{1,0:T(8,128)(2,1)} %bitcast.11.cot_ref.marks_ref, bf16[2048,512]{1,0:T(8,128)(2,1)} %get-tuple-element.52._after_ref.act_ref, ...), custom_call_target="tpu_custom_call" | custom-call | tf_op jit(solution)/shard_map/pallas_call | solution.py:440
  362.9 9.2 %shard_map.291.refs_12_ = bf16[2048,1536]{1,0:T(8,128)(2,1)} custom-call(bf16[2048,512]{1,0:T(8,128)(2,1)} %get-tuple-element.52._after_ref.act_ref, bf16[256,1536]{1,0:T(8,128)(2,1)} %bitcast.38, bf16[256,1536]{1,0:T(8,128)(2,1)} %copy-done.1, bf16[1536,256]{1,0:T(8,128)(2,1)} %get-tuple-element.60._after_ref.refs_0_), custom_call_target="tpu_custom_call" | custom-call | tf_op jit(solution)/shard_map/pallas_call | solution.py:401
  372.2 49.8 %all-to-all-done.3 = bf16[64,32,1664]{2,1,0:T(8,128)(2,1)} async-done(((bf16[64,32,1664]{2,1,0:T(8,128)(2,1)}), bf16[64,32,1664]{2,1,0:T(8,128)(2,1)}, u32[]{:S(2)}, u32[]{:S(2)}) %all-to-all-start.3) | async-done | bytes 6815776 | tf_op jit(solution)/shard_map/all_to_all | solution.py:169
  422.0 19.4 %all-to-all-start.2 = ((bf16[64,32,1536]{2,1,0:T(8,128)(2,1)}), bf16[64,32,1536]{2,1,0:T(8,128)(2,1)}, u32[]{:S(2)}, u32[]{:S(2)}) async-start(bf16[64,32,1536]{2,1,0:T(8,128)(2,1)} %bitcast.33), calls=%async_computation.2 | async-start | bytes 12582912 | tf_op jit(solution)/shard_map/all_to_all | solution.py:169
  441.6 16.2 %shard_map.293 = (bf16[256,1536]{1,0:T(8,128)(2,1)}, bf16[256,1536]{1,0:T(8,128)(2,1)}, bf16[256,1024]{1,0:T(8,128)(2,1)}, f32[256,1536]{1,0:T(8,128)}, bf16[256...) custom-call(bf16[2048,1664]{1,0:T(8,128)(2,1)} %bitcast.16.refs_0_, ...), custom_call_target="tpu_custom_call" | custom-call | tf_op jit(solution)/shard_map/pallas_call | solution.py:644
  457.9 9.0 %shard_map.294.refs_1_ = bf16[768,8448]{1,0:T(8,128)(2,1)} custom-call(bf16[256,1536]{1,0:T(8,128)(2,1)} %get-tuple-element.69.attn_in_ref, bf16[256,1536]{1,0:T(8,128)(2,1)} %get-tuple-element.70.attended_ref, bf16[256,1536]{1,0:T(8,128)(2,1)} %get-tuple-element.50.rows_ref.ffn_in_ref, bf16[256,1536]{1,0:T(8,128)(2,1)} %get-tuple-element.71.gain_one_ref, ...), custom_call_target="tpu_custom_call" | custom-call | flops 9999999827968 | tf_op jit(solution)/shard_map/pallas_call | solution.py:702
  469.0 52.7 %all-to-all-done.2 = bf16[64,32,1536]{2,1,0:T(8,128)(2,1)} async-done(((bf16[64,32,1536]{2,1,0:T(8,128)(2,1)}), bf16[64,32,1536]{2,1,0:T(8,128)(2,1)}, u32[]{:S(2)}, u32[]{:S(2)}) %all-to-all-start.2) | async-done | bytes 6291488 | tf_op jit(solution)/shard_map/all_to_all | solution.py:169
  521.7 6.8 %shard_map.292 = bf16[256,1536]{1,0:T(8,128)(2,1)} custom-call(bf16[256,2048]{1,0:T(8,128)(2,1)} %get-tuple-element.48.turned_ref.refs_2_, bf16[2048,1536]{1,0:T(8,128)(2,1)} %bitcast.14.rows_ref, f32[256,1536]{1,0:T(8,128)} %get-tuple-element.61.base_ref), custom_call_target="tpu_custom_call" | custom-call | flops 9999999827968 | tf_op jit(solution)/shard_map/pallas_call | solution.py:189
  533.3 14.4 %collective-permute-done.9 = bf16[1536,256]{1,0:T(8,128)(2,1)} collective-permute-done((bf16[1536,256]{1,0:T(8,128)(2,1)}, bf16[1536,256]{1,0:T(8,128)(2,1)}, u32[]{:S(2)}, u32[]{:S(2)}) %collective-permute-start.9) | collective-permute-done | bytes 786464 | tf_op jit(solution)/shard_map/ppermute | solution.py:45
  551.2 3.2 collective-permute-start.5
  554.4 10.0 %collective-permute-done.10 = bf16[256,1536]{1,0:T(8,128)(2,1)S(1)} collective-permute-done((bf16[256,1536]{1,0:T(8,128)(2,1)}, bf16[256,1536]{1,0:T(8,128)(2,1)S(1)}, u32[]{:S(2)}, u32[]{:S(2)}) %collective-permute-start.10) | collective-permute-done | bytes 786464 | tf_op jit(solution)/shard_map/ppermute | solution.py:45
  565.8 3.7 collective-permute-done.5
  574.3 17.5 %reduce-scatter.3.cloned.1.call-done = bf16[24,8448]{1,0:T(8,128)(2,1)} async-done(((bf16[768,8448]{1,0:T(8,128)(2,1)}), bf16[24,8448]{1,0:T(8,128)(2,1)}) %reduce-scatter.3.cloned.1.call-update) | async-done | bytes 405520 | tf_op jit(solution)/shard_map/reduce_scatter | solution.py:96
  592.9 3.2 collective-permute-start.3
  596.2 4.1 collective-permute-done.3
  603.7 2.8 collective-permute-done.4
  (93 shorter events, 36.9 us)
Async XLA Ops:
  7.2 22.3 %copy-start.9 = (s32[256,6]{0,1:T(8,128)S(1)}, s32[256,6]{0,1:T(8,128)}, u32[]{:S(2)}) copy-start(s32[256,6]{0,1:T(8,128)} %param.20) | copy-start | bytes 18436
  7.2 144.7 %all-gather.5.cloned.1.call-start = ((), (), s32[]{:S(2)}) async-start(), calls=%async_computation.6 | async-start | bytes 13381632 | tf_op jit(solution)/shard_map/all_gather | solution.py:92
  25.9 35.9 %copy-start = (bf16[4,12,7296]{2,1,0:T(8,128)(2,1)}, bf16[4,12,7296]{2,1,0:T(8,128)(2,1)S(1)}, u32[]{:S(2)}) copy-start(bf16[4,12,7296]{2,1,0:T(8,128)(2,1)S(1)} %all-gather.1.refs_1_) | copy-start | bytes 2101252
  27.0 21.1 %collective-permute-start.1 = (bf16[1536,256]{1,0:T(8,128)(2,1)}, bf16[1536,256]{1,0:T(8,128)(2,1)S(1)}, u32[]{:S(2)}, u32[]{:S(2)}) collective-permute-start(bf16[1536,256]{1,0:T(8,128)(2,1)} %bitcast.8.gate_ref), channel_id=1, source_target_pairs={{0,1},{1,0},{2,3},{3,2},{4,5},{5,4},{6,7},{7,6},{8,9},{9,8},{10,11... | collective-permute-start | bytes 2359304 | tf_op jit(solution)/shard_map/ppermute | solution.py:45
  29.4 32.4 %collective-permute-start.2 = (bf16[1536,256]{1,0:T(8,128)(2,1)}, bf16[1536,256]{1,0:T(8,128)(2,1)S(1)}, u32[]{:S(2)}, u32[]{:S(2)}) collective-permute-start(bf16[1536,256]{1,0:T(8,128)(2,1)} %bitcast.41), channel_id=1, source_target_pairs={{0,1},{1,0},{2,3},{3,2},{4,5},{5,4},{6,7},{7,6},{8,9},{9,8},{10,11... | collective-permute-start | bytes 2359304 | tf_op jit(solution)/shard_map/ppermute | solution.py:45
  48.1 13.8 %copy-start.4 = (bf16[1536,256]{1,0:T(8,128)(2,1)}, bf16[1536,256]{1,0:T(8,128)(2,1)S(1)}, u32[]{:S(2)}) copy-start(bf16[1536,256]{1,0:T(8,128)(2,1)S(1)} %collective-permute-done.1.refs_2_.gate_other_ref) | copy-start | bytes 2359300
  61.8 0.9 copy-start.5
  62.7 9.3 %slice-start = ((bf16[4,12,7296]{2,1,0:T(8,128)(2,1)}), bf16[4,12,1024]{2,1,0:T(8,128)(2,1)S(1)}, s32[]{:S(2)}) async-start(bf16[4,12,7296]{2,1,0:T(8,128)(2,1)} %copy-done), calls=%async_computation.10 | async-start | bytes 262144 | tf_op jit(solution)/shard_map/slice | solution.py:737
  62.7 9.4 %slice-start.1 = ((bf16[4,12,7296]{2,1,0:T(8,128)(2,1)}), bf16[4,12,2048]{2,1,0:T(8,128)(2,1)S(1)}, s32[]{:S(2)}) async-start(bf16[4,12,7296]{2,1,0:T(8,128)(2,1)} %copy-done), calls=%async_computation.11 | async-start | bytes 524288 | tf_op jit(solution)/shard_map/slice | solution.py:736
  62.7 107.9 %all-to-all-start.1 = ((bf16[64,32,1664]{2,1,0:T(8,128)(2,1)}), bf16[64,32,1664]{2,1,0:T(8,128)(2,1)}, u32[]{:S(2)}, u32[]{:S(2)}) async-start(bf16[64,32,1664]{2,1,0:T(8,128)(2,1)} %bitcast.34), calls=%async_computation.1 | async-start | bytes 13631488 | tf_op jit(solution)/shard_map/all_to_all | solution.py:169
  71.9 1.2 copy-start.3
  72.0 245.4 %all-gather.7.cloned.1.call-start = ((), (), s32[]{:S(2)}) async-start(), calls=%async_computation.7 | async-start | bytes 9732096 | tf_op jit(solution)/shard_map/all_gather | solution.py:92
  73.1 96.7 %collective-permute-start = (bf16[256,1536]{1,0:T(8,128)(2,1)S(1)}, bf16[256,1536]{1,0:T(8,128)(2,1)S(1)}, u32[]{:S(2)}, u32[]{:S(2)}) collective-permute-start(bf16[256,1536]{1,0:T(8,128)(2,1)S(1)} %bitcast.39), channel_id=1, source_target_pairs={{0,1},{1,0},{2,3},{3,2},{4,5},{5,4},{6,7},{7,6},{8,9},{9,8},{10,11... | collective-permute-start | bytes 2359304 | tf_op jit(solution)/shard_map/ppermute | solution.py:45
  169.8 0.9 copy-start.1
  170.7 112.5 %all-to-all-start = ((bf16[64,32,1536]{2,1,0:T(8,128)(2,1)}), bf16[64,32,1536]{2,1,0:T(8,128)(2,1)}, u32[]{:S(2)}, u32[]{:S(2)}) async-start(bf16[64,32,1536]{2,1,0:T(8,128)(2,1)} %bitcast.29), calls=%async_computation | async-start | bytes 12582912 | tf_op jit(solution)/shard_map/all_to_all | solution.py:169
  304.4 117.6 %all-to-all-start.3 = ((bf16[64,32,1664]{2,1,0:T(8,128)(2,1)}), bf16[64,32,1664]{2,1,0:T(8,128)(2,1)}, u32[]{:S(2)}, u32[]{:S(2)}) async-start(bf16[64,32,1664]{2,1,0:T(8,128)(2,1)} %bitcast.36), calls=%async_computation.3 | async-start | bytes 13631488 | tf_op jit(solution)/shard_map/all_to_all | solution.py:169
  317.3 232.9 %reduce-scatter.5.cloned.1.call-start = ((), (), s32[]{:S(2)}) async-start(), calls=%async_computation.9 | async-start | bytes 9732096 | tf_op jit(solution)/shard_map/reduce_scatter | solution.py:96
  422.0 99.7 %all-to-all-start.2 = ((bf16[64,32,1536]{2,1,0:T(8,128)(2,1)}), bf16[64,32,1536]{2,1,0:T(8,128)(2,1)}, u32[]{:S(2)}, u32[]{:S(2)}) async-start(bf16[64,32,1536]{2,1,0:T(8,128)(2,1)} %bitcast.33), calls=%async_computation.2 | async-start | bytes 12582912 | tf_op jit(solution)/shard_map/all_to_all | solution.py:169
  441.4 150.5 %reduce-scatter.3.cloned.1.call-start = ((), (), s32[]{:S(2)}) async-start(), calls=%async_computation.8 | async-start | bytes 13381632 | tf_op jit(solution)/shard_map/reduce_scatter | solution.py:96
  466.8 64.0 %collective-permute-start.8 = (bf16[1536,256]{1,0:T(8,128)(2,1)}, bf16[1536,256]{1,0:T(8,128)(2,1)}, u32[]{:S(2)}, u32[]{:S(2)}) collective-permute-start(bf16[1536,256]{1,0:T(8,128)(2,1)} %shard_map.295), channel_id=1, source_target_pairs={{0,1},{1,0},{2,3},{3,2},{4,5},{5,4},{6,7},{7,6},{8,9},{9,8},{10,11... | collective-permute-start | bytes 2359304 | tf_op jit(solution)/shard_map/ppermute | solution.py:45
  467.5 80.2 %collective-permute-start.9 = (bf16[1536,256]{1,0:T(8,128)(2,1)}, bf16[1536,256]{1,0:T(8,128)(2,1)}, u32[]{:S(2)}, u32[]{:S(2)}) collective-permute-start(bf16[1536,256]{1,0:T(8,128)(2,1)} %shard_map.296), channel_id=1, source_target_pairs={{0,1},{1,0},{2,3},{3,2},{4,5},{5,4},{6,7},{7,6},{8,9},{9,8},{10,11... | collective-permute-start | bytes 2359304 | tf_op jit(solution)/shard_map/ppermute | solution.py:45
  528.5 2.3 copy-start.2
  528.5 19.2 %copy-start.7 = (f32[1536,256]{1,0:T(8,128)S(1)}, f32[1536,256]{1,0:T(8,128)}, u32[]{:S(2)}) copy-start(f32[1536,256]{1,0:T(8,128)} %get-tuple-element.77) | copy-start | bytes 4718596
  528.5 35.9 %collective-permute-start.10 = (bf16[256,1536]{1,0:T(8,128)(2,1)}, bf16[256,1536]{1,0:T(8,128)(2,1)S(1)}, u32[]{:S(2)}, u32[]{:S(2)}) collective-permute-start(bf16[256,1536]{1,0:T(8,128)(2,1)} %shard_map.297), channel_id=1, source_target_pairs={{0,1},{1,0},{2,3},{3,2},{4,5},{5,4},{6,7},{7,6},{8,9},{9,8},{10,11... | collective-permute-start | bytes 2359304 | tf_op jit(solution)/shard_map/ppermute | solution.py:45
  533.3 31.2 %copy-start.6 = (f32[256,1536]{1,0:T(8,128)S(1)}, f32[256,1536]{1,0:T(8,128)}, u32[]{:S(2)}) copy-start(f32[256,1536]{1,0:T(8,128)} %get-tuple-element.79) | copy-start | bytes 4718596
  550.2 19.3 %copy-start.8 = (bf16[24,6144]{1,0:T(8,128)(2,1)S(1)}, bf16[24,6144]{1,0:T(8,128)(2,1)}, u32[]{:S(2)}) copy-start(bf16[24,6144]{1,0:T(8,128)(2,1)} %reduce-scatter.5.cloned.1.call-done) | copy-start | bytes 884740
  551.2 18.2 %collective-permute-start.5 = (bf16[24,3072]{1,0:T(8,128)(2,1)S(1)}, bf16[24,3072]{1,0:T(8,128)(2,1)S(1)}, u32[]{:S(2)}, u32[]{:S(2)}) collective-permute-start(bf16[24,3072]{1,0:T(8,128)(2,1)S(1)} %broadcast_select_fusion.1), channel_id=1, source_target_pairs={{0,64},{64,0},{1,65},{65,1},{2,66},{66,2},{3,67},{67,3},{4,68},{68... | collective-permute-start | bytes 442376 | tf_op jit(solution)/shard_map/ppermute | solution.py:45
  569.6 4.1 collective-permute-start.7
  570.3 25.8 %collective-permute-start.6 = (bf16[12,2048]{1,0:T(8,128)(2,1)S(1)}, bf16[12,2048]{1,0:T(8,128)(2,1)S(1)}, u32[]{:S(2)}, u32[]{:S(2)}) collective-permute-start(bf16[12,2048]{1,0:T(8,128)(2,1)S(1)} %select_convert_fusion.1), channel_id=1, source_target_pairs={{0,1},{1,0},{2,3},{3,2},{4,5},{5,4},{6,7},{7,6},{8,9},{9,8},{10,11... | collective-permute-start | bytes 147464 | tf_op jit(solution)/shard_map/ppermute | solution.py:45
  592.9 7.4 %collective-permute-start.3 = (bf16[24,4224]{1,0:T(8,128)(2,1)S(1)}, bf16[24,4224]{1,0:T(8,128)(2,1)S(1)}, u32[]{:S(2)}, u32[]{:S(2)}) collective-permute-start(bf16[24,4224]{1,0:T(8,128)(2,1)S(1)} %broadcast_select_fusion), channel_id=1, source_target_pairs={{0,64},{64,0},{1,65},{65,1},{2,66},{66,2},{3,67},{67,3},{4,68},{68... | collective-permute-start | bytes 608264 | tf_op jit(solution)/shard_map/ppermute | solution.py:45
  601.4 5.1 collective-permute-start.4
Sparse Core Ops, SparseCore 0:
  27.1 124.7 all-gather.4
  154.2 127.3 all-gather.6
  336.7 135.7 reduce-scatter.4
  476.7 115.0 reduce-scatter.2

commit v3 on v2

--- a/solution.py
+++ b/solution.py
@@ -14,7 +14,8 @@
 SHARED = 1024
 HALF = 256
 ROWS = EXPERTS * SLOTS
-WIDE = WIDTH + 128
+PAIRS = ROWS // 2
+WIDE = 2 * WIDTH + 128
 PACK = 2 * WIDTH + 1024 + 128
 
 EPSILON = 1e-06
@@ -96,20 +97,20 @@
     return lax.psum_scatter(grads, PLANE, scatter_dimension=0, tiled=True)
 
 
-def sum_zh(plane):
+def sum_line(plane, cut):
     width = plane.shape[1] // 2
     zh = lax.axis_index("zh")
+    zl = lax.axis_index("zl")
     low, high = plane[:, :width], plane[:, width:]
-    keep = jnp.where(zh == 0, low, high)
-    give = jnp.where(zh == 0, high, low)
-    return keep.astype(F32) + swap(give, "zh").astype(F32)
-
-
-def sum_zl(mine, other):
-    zl = lax.axis_index("zl")
-    keep = jnp.where(zl == 0, mine, other)
-    give = jnp.where(zl == 0, other, mine).astype(BF)
-    return keep + swap(give, "zl").astype(F32)
+    near, far = jnp.where(zh == 0, low, high), jnp.where(zh == 0, high, low)
+    ours, theirs = cut(near)
+    total = jnp.where(zl == 0, ours, theirs).astype(F32)
+    total += swap(jnp.where(zl == 0, theirs, ours), "zl").astype(F32)
+    ours, theirs = cut(far)
+    total += swap(jnp.where(zl == 0, ours, theirs), "zh").astype(F32)
+    across = [(i, 3 - i) for i in range(4)]
+    give = jnp.where(zl == 0, theirs, ours)
+    return total + lax.ppermute(give, ("zh", "zl"), across).astype(F32)
 
 
 def fold_down(rows):
@@ -125,12 +126,18 @@
 def deal_kernel(rank_ref, cot_ref, hits_ref, deal_ref, turned_ref, out_ref):
     rank = rank_ref[...]
     slot = lax.broadcasted_iota(jnp.int32, (8, SLOTS, TOKENS), 1).astype(F32)
-    hit = jnp.where(rank[:, None, :] == slot, 1.0, 0.0).reshape(8 * SLOTS, TOKENS)
-    deal = hit.astype(BF)
-    deal_ref[...] = deal
-    turned_ref[...] = jnp.transpose(hit).astype(BF)
-    out_ref[:, :WIDTH] = mm(deal, cot_ref[...]).astype(BF)
-    out_ref[:, WIDTH:] = mm(deal, hits_ref[...]).astype(BF)
+    hit = jnp.where(rank[:, None, :] == slot, 1.0, 0.0)
+    lane = lax.broadcasted_iota(jnp.int32, (128, 128), 1)
+    marks = jnp.zeros((128, 128), F32)
+    for j in range(2):
+        side = hit[:, j * 16 : (j + 1) * 16].reshape(128, TOKENS)
+        deal = side.astype(BF)
+        deal_ref[j] = deal
+        turned_ref[j] = jnp.transpose(side).astype(BF)
+        out_ref[:, j * WIDTH : (j + 1) * WIDTH] = mm(deal, cot_ref[...]).astype(BF)
+        mark = mm(deal, hits_ref[...])
+        marks += mark if j == 0 else pltpu.roll(mark, 64, 1)
+    out_ref[:, 2 * WIDTH :] = marks.astype(BF)
 
 
 def deal_out(rank, out_grad, hits):
@@ -143,32 +150,35 @@
             full((TOKENS, 128)),
         ],
         [
-            pl.BlockSpec((256, TOKENS), lambda i: (i, 0)),
-            pl.BlockSpec((TOKENS, 256), lambda i: (0, i)),
-            pl.BlockSpec((256, WIDE), lambda i: (i, 0)),
+            pl.BlockSpec((2, 128, TOKENS), lambda i: (0, i, 0)),
+            pl.BlockSpec((2, TOKENS, 128), lambda i: (0, 0, i)),
+            pl.BlockSpec((128, WIDE), lambda i: (i, 0)),
         ],
-        [out((ROWS, TOKENS), BF), out((TOKENS, ROWS), BF), out((ROWS, WIDE), BF)],
+        [out((2, PAIRS, TOKENS), BF), out((2, TOKENS, PAIRS), BF), out((PAIRS, WIDE), BF)],
     )(rank, out_grad, hits)
 
 
 def dispatch_kernel(deal_ref, rows_ref, out_ref):
-    out_ref[...] = mm(deal_ref[...], rows_ref[...]).astype(BF)
+    out_ref[...] = mm(deal_ref[0], rows_ref[...]).astype(BF)
 
 
 def dispatch(deal, rows):
     return call(
         dispatch_kernel,
-        (6,),
-        [full((ROWS, TOKENS)), pl.BlockSpec((TOKENS, 256), lambda j: (0, j))],
-        pl.BlockSpec((ROWS, 256), lambda j: (0, j)),
-        out((ROWS, WIDTH), BF),
+        (4,),
+        [
+            pl.BlockSpec((1, PAIRS, TOKENS), lambda j: (j // 2, 0, 0)),
+            pl.BlockSpec((TOKENS, 768), lambda j: (0, j % 2)),
+        ],
+        pl.BlockSpec((PAIRS, 768), lambda j: (0, j)),
+        out((PAIRS, 2 * WIDTH), BF),
     )(deal, rows)
 
 
 def to_experts(rows):
     return lax.all_to_all(
-        rows.reshape(EXPERTS, SLOTS, -1), DP, split_axis=0, concat_axis=0, tiled=True
-    ).reshape(ROWS, -1)
+        rows.reshape(EXPERTS, SLOTS // 2, -1), DP, split_axis=0, concat_axis=0, tiled=True
+    ).reshape(PAIRS, -1)
 
 
 def result_kernel(turned_ref, rows_ref, base_ref, out_ref, acc):
@@ -178,7 +188,7 @@
     def _():
         acc[...] = base_ref[...]
 
-    acc[...] += mm(turned_ref[...], rows_ref[...])
+    acc[...] += mm(turned_ref[0], rows_ref[...])
 
     @pl.when(step == 3)
     def _():
@@ -190,8 +200,8 @@
         result_kernel,
         (4,),
         [
-            pl.BlockSpec((TOKENS, 512), lambda i: (0, i)),
-            pl.BlockSpec((512, WIDTH), lambda i: (i, 0)),
+            pl.BlockSpec((1, TOKENS, 512), lambda i: (i // 2, 0, i % 2)),
+            pl.BlockSpec((512, WIDTH), lambda i: (i % 2, i // 2)),
             full((TOKENS, WIDTH)),
         ],
         full((TOKENS, WIDTH)),
@@ -306,9 +316,14 @@
     )(hidden, docs, hits, pack)
 
 
+def unpaired(ref):
+    return jnp.concatenate([ref[:, :WIDTH], ref[:, WIDTH : 2 * WIDTH]], axis=0)
+
+
 def act_cot_kernel(cot_ref, down_ref, other_ref, _after_ref, out_ref):
-    out_ref[:, :HALF] = mm_r(cot_ref[...], down_ref[...])
-    out_ref[:, HALF:] = mm_r(cot_ref[...], other_ref[...])
+    cot = unpaired(cot_ref)
+    out_ref[:, :HALF] = mm_r(cot, down_ref[...])
+    out_ref[:, HALF:] = mm_r(cot, other_ref[...])
 
 
 def act_cots(cot_rows, down, other, after):
@@ -316,7 +331,7 @@
         act_cot_kernel,
         (8,),
         [
-            pl.BlockSpec((256, WIDTH), lambda i: (i, 0)),
+            pl.BlockSpec((128, 2 * WIDTH), lambda i: (i, 0)),
             full((HALF, WIDTH)),
             full((HALF, WIDTH)),
             ANY,
@@ -342,8 +357,11 @@
     gate_cot_ref,
     up_cot_ref,
 ):
-    rows = rows_ref[...]
-    marks = marks_ref[...] > 0
+    rows = unpaired(rows_ref)
+    lane = lax.broadcasted_iota(jnp.int32, (1, 128), 1)
+    marks = marks_ref[...].astype(F32)
+    marks = jnp.concatenate([marks, pltpu.roll(marks, 64, 1)], axis=0)
+    marks = (marks > 0) & (lane < 64)
     logits = mm(rows, small_ref[...])
     top = jnp.max(jnp.where(marks, logits, NEGATIVE), axis=-1, keepdims=True)
     weight = jnp.where(marks, jnp.exp(jnp.where(marks, logits - top, 0.0)), 0.0)
@@ -371,30 +389,34 @@
         total += mm_r(gate_cot_ref[:, HALF:], gate_other_ref[at, :])
         total += mm_r(up_cot_ref[:, :HALF], up_ref[at, :])
         total += mm_r(up_cot_ref[:, HALF:], up_other_ref[at, :])
-        back_ref[:, at] = total.astype(BF)
+        back_ref[:, at] = total[:128].astype(BF)
+        back_ref[:, WIDTH + j : WIDTH + j + 512] = total[128:].astype(BF)
     high = share.astype(BF).astype(F32)
-    lane = lax.broadcasted_iota(jnp.int32, (1, 128), 1)
-    placed = jnp.where(lane < 64, high, share - high) * (own + pltpu.roll(own, 64, 1))
-    back_ref[:, WIDTH:] = placed.astype(BF)
+    extra = jnp.zeros((128, 128), F32)
+    for j, value in enumerate((high[:128], high[128:], (share - high)[:128], (share - high)[128:])):
+        extra += jnp.where(lane == j, value, 0.0)
+    back_ref[:, 2 * WIDTH :] = extra.astype(BF)
 
 
 def expert_phase(rows, cot_rows, act_cot, own, pack, weights, after):
-    tile = lambda w, j=0: pl.BlockSpec((256, w), lambda i: (i, j))
+    tile = lambda w: pl.BlockSpec((256, w), lambda i: (i, 0))
+    pair = lambda w, j=0: pl.BlockSpec((128, w), lambda i: (i, j))
     small = pl.BlockSpec((WIDTH, 128), lambda i: (0, 32))
     return call(
         expert_kernel,
         (8,),
-        [tile(WIDTH), tile(128, 12), tile(512), full((1, 128)), small]
+        [pair(2 * WIDTH), pair(128, 24), tile(512), full((1, 128)), small]
         + [full(w.shape) for w in weights]
         + [ANY],
-        [tile(WIDE), tile(512), tile(512), tile(512)],
-        [out((ROWS, WIDE), BF)] + [out((ROWS, 512), BF)] * 3,
+        [pair(WIDE), tile(512), tile(512), tile(512)],
+        [out((PAIRS, WIDE), BF)] + [out((ROWS, 512), BF)] * 3,
     )(rows, cot_rows, act_cot, own, pack, *weights, after)
 
 
 def expert_out_kernel(act_ref, down_ref, other_ref, _after_ref, out_ref):
     total = mm(act_ref[:, :HALF], down_ref[...]) + mm(act_ref[:, HALF:], other_ref[...])
-    out_ref[...] = total.astype(BF)
+    out_ref[:, :WIDTH] = total[:128].astype(BF)
+    out_ref[:, WIDTH:] = total[128:].astype(BF)
 
 
 def expert_outs(act, down, other, after):
@@ -407,8 +429,8 @@
             full((HALF, WIDTH)),
             ANY,
         ],
-        pl.BlockSpec((256, WIDTH), lambda i: (i, 0)),
-        out((ROWS, WIDTH), BF),
+        pl.BlockSpec((128, 2 * WIDTH), lambda i: (i, 0)),
+        out((PAIRS, 2 * WIDTH), BF),
     )(act, down, other, after)
 
 
@@ -423,9 +445,10 @@
         up[...] = jnp.zeros_like(up)
         down[...] = jnp.zeros_like(down)
 
-    gate[...] += mm_l(rows_ref[...], gate_cot_ref[...])
-    up[...] += mm_l(rows_ref[...], up_cot_ref[...])
-    down[...] += mm_l(act_ref[...], cot_ref[...])
+    rows = unpaired(rows_ref)
+    gate[...] += mm_l(rows, gate_cot_ref[...])
+    up[...] += mm_l(rows, up_cot_ref[...])
+    down[...] += mm_l(act_ref[...], unpaired(cot_ref))
 
     @pl.when(step == 7)
     def _():
@@ -436,11 +459,12 @@
 
 def expert_grads(half, dtype, rows, cot_rows, act, gate_cot, up_cot, after):
     tile = lambda w, j=0: pl.BlockSpec((256, w), lambda i: (i, j))
+    pair = pl.BlockSpec((128, 2 * WIDTH), lambda i: (i, 0))
     shapes = [(WIDTH, HALF), (WIDTH, HALF), (HALF, WIDTH)]
     return call(
         expert_grad_kernel,
         (8,),
-        [tile(WIDTH), tile(WIDTH), tile(HALF, half), tile(HALF, half), tile(HALF, half), ANY],
+        [pair, pair, tile(HALF, half), tile(HALF, half), tile(HALF, half), ANY],
         [full(s) for s in shapes],
         [out(s, dtype) for s in shapes],
         [pltpu.VMEM(s, F32) for s in shapes],
@@ -550,7 +574,7 @@
     middle_low_ref, dq_ref, dkv_ref, grad_in_ref, logit_ref, one_ref, two_ref, cot_ref = outs
     back_ref, wo_ref, wq_ref, wkv_ref, small_ref, acc, sems = scratch[:7]
     held = scratch[7:]
-    loads = [(back_hbm.at[:1024], back_ref.at[:1024]), (back_hbm.at[1024:], back_ref.at[1024:])]
+    loads = [(back_hbm.at[:512], back_ref.at[:512]), (back_hbm.at[512:], back_ref.at[512:])]
     loads += [(a, b) for a, b in zip(sources[2:7], held[:5])]
     loads += [
         (pack_hbm.at[:, 2 * WIDTH + 1024 : PACK], small_ref),
@@ -567,17 +591,29 @@
     copies = [fetch(a, b, sems.at[i]) for i, (a, b) in enumerate(loads)]
     for i in (0, 1):
         copies[i].wait()
-    acc[...] = mm(turned_ref[:, :1024], back_ref[:1024])
-    copies[2].wait()
-    acc[...] += mm(turned_ref[:, 1024:], back_ref[1024:])
+    lane = lax.broadcasted_iota(jnp.int32, (512, 128), 1)
+    row = lax.broadcasted_iota(jnp.int32, (512, 128), 0)
+    shares = jnp.zeros((TOKENS, 128), F32)
+    for half in range(2):
+        at = slice(half * 512, (half + 1) * 512)
+        if half:
+            copies[2].wait()
+        total = mm(turned_ref[0, :, at], back_ref[at, :WIDTH])
+        total += mm(turned_ref[1, :, at], back_ref[at, WIDTH : 2 * WIDTH])
+        if half:
+            acc[...] += total
+        else:
+            acc[...] = total
+        extra = back_ref[at, 2 * WIDTH :].astype(F32)
+        mine = lane == row // 16 + half * 32
+        for j in range(2):
+            for value in (extra[:, j : j + 1], extra[:, 2 + j : 3 + j]):
+                shares += mm(turned_ref[j, :, at], jnp.where(mine, value, 0.0).astype(BF))
     for i in range(3, 10):
         copies[i].wait()
-    extra = acc[:, WIDTH:]
-    lane = lax.broadcasted_iota(jnp.int32, (1, 128), 1)
-    shares = jnp.where(lane < 64, extra + pltpu.roll(extra, 64, 1), 0.0)
     logit = shares - gates_ref[...] * jnp.sum(shares, axis=-1, keepdims=True)
     logit_ref[...] = logit.astype(BF)
-    cot = acc[:, :WIDTH] + shared_ref[...] + mm_r(logit_ref[...], small_ref[...])
+    cot = acc[...] + shared_ref[...] + mm_r(logit_ref[...], small_ref[...])
     middle = middle_ref[...]
     scale = root_scale(middle)
     two_ref[...] = (cot * middle * scale).astype(BF)
@@ -614,7 +650,7 @@
         acc[:, at] = mm_r(dq_ref[...], wq_ref[at, :]) + mm_r(dkv_ref[...], wkv_ref[at, :])
     tokens = hidden_ref[...].astype(F32)
     scale = root_scale(tokens)
-    cot = acc[:, :WIDTH]
+    cot = acc[...]
     one_ref[...] = (cot * tokens * scale).astype(BF)
     grad_in_ref[...] += norm_back(tokens, scale, gains_ref[0:1], cot)
 
@@ -633,12 +669,12 @@
     ]
     held = [turned, shared_cot, gates, middle, gains, out_grad, q, kv, probs, hidden]
     scratch = [
-        pltpu.VMEM((ROWS, WIDE), BF),
+        pltpu.VMEM((PAIRS, WIDE), BF),
         pltpu.VMEM((WIDTH, WIDTH), BF),
         pltpu.VMEM((WIDTH, WIDTH), BF),
         pltpu.VMEM((WIDTH, 1024), BF),
         pltpu.VMEM((WIDTH, 128), BF),
-        pltpu.VMEM((TOKENS, WIDE), F32),
+        pltpu.VMEM((TOKENS, WIDTH), F32),
         pltpu.SemaphoreType.DMA((16,)),
     ] + [pltpu.VMEM(a.shape, a.dtype) for a in held]
     return call(
@@ -748,12 +784,12 @@
     own = (lanes == lax.axis_index(DP)).astype(F32)[None]
 
     deal, turned, send_cot = deal_out(rank, out_grad, hits_low)
-    cot_rows = to_experts(tie(send_cot, line, gate_other, up_other))
+    cot_rows = to_experts(tie(send_cot, line))
 
     attn_in, q, kv, probs, attended, middle, ffn_in, gates, gains = forward(
         hidden_in, doc_lengths, hits_low, pack
     )
-    send_rows = tie(dispatch(deal, ffn_in), down_other)
+    send_rows = tie(dispatch(deal, ffn_in), gate_other, up_other, down_other)
     rows = to_experts(send_rows)
 
     act_cot = act_cots(cot_rows, down, down_other, send_rows)
@@ -779,13 +815,18 @@
     dense_grad = dense_grads(
         attn_in, attended, ffn_in, one_rows, two_rows, dq, middle_low, dkv, logit
     )
-    dense = sum_zh(scatter_plane(dense_grad))
-    dense = sum_zl(dense[:12], dense[12:])
-    shared_grad = sum_zh(shared_grad)
+    dense = sum_line(scatter_plane(dense_grad), lambda x: (x[:12], x[12:]))
+
+    def cut_shared(x):
+        down = unfold_down(x[None, :, 2 * SHARED :])[0]
+        return [
+            jnp.concatenate([x[12 * i : 12 * i + 12, : 2 * SHARED], down[8 * i : 8 * i + 8].reshape(12, 1024)], axis=1)
+            for i in range(2)
+        ]
+
+    shared_grad = sum_line(shared_grad, cut_shared)
     pair_grad = shared_grad[:, : 2 * SHARED]
-    down_grad = unfold_down(shared_grad[None, :, 2 * SHARED :])[0]
-    pair_grad = sum_zl(pair_grad[:12], pair_grad[12:])
-    down_grad = sum_zl(down_grad[:8], down_grad[8:])
+    down_grad = shared_grad[:, 2 * SHARED :].reshape(8, WIDTH)
     block_out = add_results(turned, result, shared_sum)
     sent = [tie(x, dense_grad) for x in sent]
     expert = [(k + swap(s, "zl").astype(F32))[None] for k, s in zip(kept, sent)]

time: 627 us -> 621 us (level)
  starting transfers between devices: 77.8 us -> 70.3 us
    ppermute x11 -> x10, waiting for transfers between devices: 62.1 us -> 30.6 us  [swap(): return lax.ppermute(x, axis, [(0, 1), (1, 0)])]
    all_gather x2, waiting for transfers between devices: 78.1 us -> 102 us  [gather_plane(): lax.all_gather(pairs, PLANE, axis=1, tiled=True).reshape(64 * rows, width)]
    reduce_scatter x2, waiting for transfers between devices: 17.5 us -> 32.2 us  [scatter_plane(): return lax.psum_scatter(grads, PLANE, scatter_dimension=0, tiled=True)]
    all_to_all x4, starting transfers between devices: 61.6 us -> 53.4 us  [to_experts(): lax.all_to_all(rows.reshape(EXPERTS, SLOTS // 2, -1), DP, split_axis=0, c...]
    ppermute x0 -> x2, starting transfers between devices: none -> 6.28 us  [sum_line(): return total + lax.ppermute(give, ('zh', 'zl'), across).astype(F32)]
    ppermute x11 -> x10, starting transfers between devices: 15.9 us -> 10.2 us  [swap(): return lax.ppermute(x, axis, [(0, 1), (1, 0)])]
  transfers between devices with their start and end apart: 19 -> 20, of which waited for: 14 -> 11; matrix products, arithmetic and copies ran while one was open for 2% -> 2% of each run, Pallas kernels for 23% -> 23%
where the time goes in v3:
time: 621 us; the launch traced here: 612 us
  waiting for transfers between devices  346 us (56%)
  Pallas kernels  143 us (23%)
  starting transfers between devices  70.3 us (11%)
  blocking collectives  15.4 us (2%)
  between operations  14.6 us (2%)
  other arithmetic  11.9 us (2%)
  local copies, waits for them, and re-layouts  10.7 us (2%)
    all_to_all x4, waiting for transfers between devices, to_experts(): lax.all_to_all(rows.reshape(EXPERTS, SLOTS // 2, -1), DP, split_axis=0, c...  180 us
    all_gather x2, waiting for transfers between devices, gather_plane(): lax.all_gather(pairs, PLANE, axis=1, tiled=True).reshape(64 * rows, width)  102 us
    all_to_all x4, starting transfers between devices, to_experts(): lax.all_to_all(rows.reshape(EXPERTS, SLOTS // 2, -1), DP, split_axis=0, c...  53.4 us
    reduce_scatter x2, waiting for transfers between devices, scatter_plane(): return lax.psum_scatter(grads, PLANE, scatter_dimension=0, tiled=True)  32.2 us
    ppermute x10, waiting for transfers between devices, swap(): return lax.ppermute(x, axis, [(0, 1), (1, 0)])  30.6 us
    pallas_call x2, Pallas kernels, expert_grads(): call(expert_grad_kernel, (8,), [pair, pair, tile(HALF, half), tile(HALF,...  26.2 us
    pallas_call x1, Pallas kernels, expert_phase(): call(expert_kernel, (8,), [pair(2 * WIDTH), pair(128, 24), tile(512), ful...  21.2 us
    pallas_call x1, Pallas kernels, backward(): call(backward_kernel, (1,), [ANY] * 13, [full(s) for s, _ in shapes], [ou...  15.7 us
  transfers between devices with their start and end apart: 20, of which 11 were waited for; matrix products, arithmetic and copies ran while one was open for 2% of the time, Pallas kernels for 23%

profile of v3, /device:TPU:0, one launch (start us, length us, event | category | flops | bytes accessed | tf_op | source)
XLA Modules:
  0.0 611.8 jit_solution(17348703100569570628)
XLA Ops:
  10.5 15.4 %all-gather.1.refs_1_ = bf16[4,12,7296]{2,1,0:T(8,128)(2,1)S(1)} all-gather(bf16[1,12,7296]{2,1,0:T(8,128)(2,1)S(1)} %bitcast.38), channel_id=2, replica_groups=mesh['zh'=2,'x'=4,'y'=4,'c'=2,'zl'=2] {'zh','zl'}, dimensions={0}, use_global_device_ids=true | all-gather | bytes 875520 | tf_op jit(solution)/shard_map/all_gather | solution.py:770
  28.9 7.8 %shard_map.280 = (bf16[2,1024,256]{2,1,0:T(8,128)(2,1)}, bf16[2,256,1024]{2,1,0:T(8,128)(2,1)}, bf16[1024,3200]{1,0:T(8,128)(2,1)}) custom-call(f32[64,256]{1,0:T(8,128)} %slice_select_fusion.rank_ref, bf16[256,1536]{1,0:T(8,128)(2,1)} %refs_7_.1, bf16[256,128]{1,0:T(8,128)(2,1)} %convert.hits_ref), custom_call_target="tpu_custom_call" | custom-call | tf_op jit(solution)/shard_map/pallas_call | solution.py:144
  36.8 9.2 %all-to-all-start.1 = ((bf16[64,16,3200]{2,1,0:T(8,128)(2,1)}), bf16[64,16,3200]{2,1,0:T(8,128)(2,1)}, u32[]{:S(2)}, u32[]{:S(2)}) async-start(bf16[64,16,3200]{2,1,0:T(8,128)(2,1)} %bitcast.32), calls=%async_computation.1 | async-start | bytes 13107200 | tf_op jit(solution)/shard_map/all_to_all | solution.py:179
  47.0 3.0 collective-permute-start
  52.0 101.6 %all-gather.5.cloned.1.call-done = bf16[2,768,4224]{2,1,0:T(8,128)(2,1)} async-done(((bf16[2,24,4224]{2,1,0:T(8,128)(2,1)}), bf16[2,768,4224]{2,1,0:T(8,128)(2,1)}) %all-gather.5.cloned.1.call-update) | async-done | bytes 12976144 | tf_op jit(solution)/shard_map/all_gather | solution.py:93
  153.6 11.1 %shard_map.281 = (bf16[256,1536]{1,0:T(8,128)(2,1)}, bf16[256,1536]{1,0:T(8,128)(2,1)}, bf16[256,1024]{1,0:T(8,128)(2,1)}, f32[12,256,256]{2,1,0:T(8,128)}, bf16...) custom-call(bf16[256,1536]{1,0:T(8,128)(2,1)} %refs_11_.1, ...), custom_call_target="tpu_custom_call" | custom-call | tf_op jit(solution)/shard_map/pallas_call | solution.py:308
  164.7 6.3 %shard_map.282.refs_0_ = bf16[1024,3072]{1,0:T(8,128)(2,1)} custom-call(bf16[2,1024,256]{2,1,0:T(8,128)(2,1)} %get-tuple-element.49.deal_ref, bf16[256,1536]{1,0:T(8,128)(2,1)} %get-tuple-element.50.rows_ref.ffn_in_ref), custom_call_target="tpu_custom_call" | custom-call | tf_op jit(solution)/shard_map/pallas_call | solution.py:166
  173.0 10.5 %all-to-all-start = ((bf16[64,16,3072]{2,1,0:T(8,128)(2,1)}), bf16[64,16,3072]{2,1,0:T(8,128)(2,1)}, u32[]{:S(2)}, u32[]{:S(2)}) async-start(bf16[64,16,3072]{2,1,0:T(8,128)(2,1)} %bitcast.27), calls=%async_computation | async-start | bytes 12582912 | tf_op jit(solution)/shard_map/all_to_all | solution.py:179
  184.0 9.9 %shard_map.285.act_cot_ref = f32[2048,512]{1,0:T(8,128)} custom-call(bf16[1024,3200]{1,0:T(8,128)(2,1)} %bitcast.11.cot_ref.marks_ref, bf16[256,1536]{1,0:T(8,128)(2,1)} %bitcast.35, bf16[256,1536]{1,0:T(8,128)(2,1)} %copy-done.1, bf16[1024,3072]{1,0:T(8,128)(2,1)} %shard_map.283._after_ref), custom_call_target="tpu_custom_call" | custom-call | tf_op jit(solution)/shard_map/pallas_call | solution.py:330
  193.9 82.0 %all-to-all-done = bf16[64,16,3072]{2,1,0:T(8,128)(2,1)} async-done(((bf16[64,16,3072]{2,1,0:T(8,128)(2,1)}), bf16[64,16,3072]{2,1,0:T(8,128)(2,1)}, u32[]{:S(2)}, u32[]{:S(2)}) %all-to-all-start) | async-done | bytes 6291488 | tf_op jit(solution)/shard_map/all_to_all | solution.py:179
  275.9 21.2 %shard_map.286 = (bf16[1024,3200]{1,0:T(8,128)(2,1)}, bf16[2048,512]{1,0:T(8,128)(2,1)}, bf16[2048,512]{1,0:T(8,128)(2,1)}, bf16[2048,512]{1,0:T(8,128)(2,1)}) custom-call(bf16[1024,3072]{1,0:T(8,128)(2,1)} %bitcast.9.rows_ref, bf16[1024,3200]{1,0:T(8,128)(2,1)} %bitcast.11.cot_ref.marks_ref, f32[2048,512]{1,0:T(8,128)} %shard_map.285.act_cot_ref, ...), custom_call_target="tpu_custom_call" | custom-call | tf_op jit(solution)/shard_map/pallas_call | solution.py:405
  297.1 12.9 %all-to-all-start.3 = ((bf16[64,16,3200]{2,1,0:T(8,128)(2,1)}), bf16[64,16,3200]{2,1,0:T(8,128)(2,1)}, u32[]{:S(2)}, u32[]{:S(2)}) async-start(bf16[64,16,3200]{2,1,0:T(8,128)(2,1)} %bitcast.34), calls=%async_computation.3 | async-start | bytes 13107200 | tf_op jit(solution)/shard_map/all_to_all | solution.py:179
  310.0 12.1 %shard_map.287 = (bf16[256,1024]{1,0:T(8,128)(2,1)}, bf16[256,2048]{1,0:T(8,128)(2,1)}, f32[256,1536]{1,0:T(8,128)}, f32[256,1536]{1,0:T(8,128)}) custom-call(bf16[256,1536]{1,0:T(8,128)(2,1)} %get-tuple-element.50.rows_ref.ffn_in_ref, bf16[256,1536]{1,0:T(8,128)(2,1)} %refs_7_.1, f32[256,1536]{1,0:T(8,128)} %get-tuple-element.55.middle_ref.refs_5_, ...), custom_call_target="tpu_custom_call" | custom-call | tf_op jit(solution)/shard_map/pallas_call | solution.py:520
  322.1 7.0 %shard_map.288._after_ref = bf16[768,6144]{1,0:T(8,128)(2,1)} custom-call(bf16[256,1536]{1,0:T(8,128)(2,1)} %get-tuple-element.50.rows_ref.ffn_in_ref, bf16[256,2048]{1,0:T(8,128)(2,1)} %get-tuple-element.56.pair_ref, bf16[256,1024]{1,0:T(8,128)(2,1)} %get-tuple-element.57.act_ref, bf16[256,1536]{1,0:T(8,128)(2,1)} %refs_7_.1, ...), custom_call_target="tpu_custom_call" | custom-call | tf_op jit(solution)/shard_map/pallas_call | solution.py:549
  329.1 13.4 %shard_map.289 = (f32[1536,256]{1,0:T(8,128)}, f32[1536,256]{1,0:T(8,128)}, f32[256,1536]{1,0:T(8,128)}) custom-call(bf16[1024,3072]{1,0:T(8,128)(2,1)} %bitcast.9.rows_ref, bf16[1024,3200]{1,0:T(8,128)(2,1)} %bitcast.11.cot_ref.marks_ref, bf16[2048,512]{1,0:T(8,128)(2,1)} %get-tuple-element.52._after_ref.act_ref, ...), custom_call_target="tpu_custom_call" | custom-call | tf_op jit(solution)/shard_map/pallas_call | solution.py:464
  342.5 12.9 %shard_map.290 = (bf16[1536,256]{1,0:T(8,128)(2,1)}, bf16[1536,256]{1,0:T(8,128)(2,1)}, bf16[256,1536]{1,0:T(8,128)(2,1)}) custom-call(bf16[1024,3072]{1,0:T(8,128)(2,1)} %bitcast.9.rows_ref, bf16[1024,3200]{1,0:T(8,128)(2,1)} %bitcast.11.cot_ref.marks_ref, bf16[2048,512]{1,0:T(8,128)(2,1)} %get-tuple-element.52._after_ref.act_ref, ...), custom_call_target="tpu_custom_call" | custom-call | tf_op jit(solution)/shard_map/pallas_call | solution.py:464
  355.4 9.2 %shard_map.291.refs_12_ = bf16[1024,3072]{1,0:T(8,128)(2,1)} custom-call(bf16[2048,512]{1,0:T(8,128)(2,1)} %get-tuple-element.52._after_ref.act_ref, bf16[256,1536]{1,0:T(8,128)(2,1)} %bitcast.36, bf16[256,1536]{1,0:T(8,128)(2,1)} %copy-done.1, bf16[1536,256]{1,0:T(8,128)(2,1)} %get-tuple-element.60._after_ref.refs_0_), custom_call_target="tpu_custom_call" | custom-call | tf_op jit(solution)/shard_map/pallas_call | solution.py:423
  364.6 45.4 %all-to-all-done.3 = bf16[64,16,3200]{2,1,0:T(8,128)(2,1)} async-done(((bf16[64,16,3200]{2,1,0:T(8,128)(2,1)}), bf16[64,16,3200]{2,1,0:T(8,128)(2,1)}, u32[]{:S(2)}, u32[]{:S(2)}) %all-to-all-start.3) | async-done | bytes 6553632 | tf_op jit(solution)/shard_map/all_to_all | solution.py:179
  410.0 20.9 %all-to-all-start.2 = ((bf16[64,16,3072]{2,1,0:T(8,128)(2,1)}), bf16[64,16,3072]{2,1,0:T(8,128)(2,1)}, u32[]{:S(2)}, u32[]{:S(2)}) async-start(bf16[64,16,3072]{2,1,0:T(8,128)(2,1)} %bitcast.31), calls=%async_computation.2 | async-start | bytes 12582912 | tf_op jit(solution)/shard_map/all_to_all | solution.py:179
  431.1 15.7 %shard_map.293 = (bf16[256,1536]{1,0:T(8,128)(2,1)}, bf16[256,1536]{1,0:T(8,128)(2,1)}, bf16[256,1024]{1,0:T(8,128)(2,1)}, f32[256,1536]{1,0:T(8,128)}, bf16[256...) custom-call(bf16[1024,3200]{1,0:T(8,128)(2,1)} %bitcast.16.refs_0_, ...), custom_call_target="tpu_custom_call" | custom-call | tf_op jit(solution)/shard_map/pallas_call | solution.py:680
  446.8 9.1 %shard_map.294.refs_1_ = bf16[768,8448]{1,0:T(8,128)(2,1)} custom-call(bf16[256,1536]{1,0:T(8,128)(2,1)} %get-tuple-element.69.attn_in_ref, bf16[256,1536]{1,0:T(8,128)(2,1)} %get-tuple-element.70.attended_ref, bf16[256,1536]{1,0:T(8,128)(2,1)} %get-tuple-element.50.rows_ref.ffn_in_ref, bf16[256,1536]{1,0:T(8,128)(2,1)} %get-tuple-element.71.gain_one_ref, ...), custom_call_target="tpu_custom_call" | custom-call | flops 9999999827968 | tf_op jit(solution)/shard_map/pallas_call | solution.py:738
  458.1 52.1 %all-to-all-done.2 = bf16[64,16,3072]{2,1,0:T(8,128)(2,1)} async-done(((bf16[64,16,3072]{2,1,0:T(8,128)(2,1)}), bf16[64,16,3072]{2,1,0:T(8,128)(2,1)}, u32[]{:S(2)}, u32[]{:S(2)}) %all-to-all-start.2) | async-done | bytes 6291488 | tf_op jit(solution)/shard_map/all_to_all | solution.py:179
  510.2 7.0 %shard_map.292 = bf16[256,1536]{1,0:T(8,128)(2,1)} custom-call(bf16[2,256,1024]{2,1,0:T(8,128)(2,1)} %get-tuple-element.48.turned_ref.refs_2_, bf16[1024,3072]{1,0:T(8,128)(2,1)} %bitcast.14.rows_ref, f32[256,1536]{1,0:T(8,128)} %get-tuple-element.61.base_ref), custom_call_target="tpu_custom_call" | custom-call | flops 9999999827968 | tf_op jit(solution)/shard_map/pallas_call | solution.py:199
  518.1 2.3 collective-permute-done.9
  520.4 2.4 add_bitcast_fusion.2
  522.8 14.4 %collective-permute-done.10 = bf16[1536,256]{1,0:T(8,128)(2,1)} collective-permute-done((bf16[1536,256]{1,0:T(8,128)(2,1)}, bf16[1536,256]{1,0:T(8,128)(2,1)}, u32[]{:S(2)}, u32[]{:S(2)}) %collective-permute-start.10) | collective-permute-done | bytes 786464 | tf_op jit(solution)/shard_map/ppermute | solution.py:46
  537.2 2.7 add_bitcast_fusion.1
  541.3 3.3 collective-permute-start.8
  545.7 8.2 %collective-permute-done.11 = bf16[256,1536]{1,0:T(8,128)(2,1)S(1)} collective-permute-done((bf16[256,1536]{1,0:T(8,128)(2,1)}, bf16[256,1536]{1,0:T(8,128)(2,1)S(1)}, u32[]{:S(2)}, u32[]{:S(2)}) %collective-permute-start.11) | collective-permute-done | bytes 786464 | tf_op jit(solution)/shard_map/ppermute | solution.py:46
  555.3 3.4 collective-permute-done.7
  558.8 32.2 %reduce-scatter.3.cloned.1.call-done = bf16[24,8448]{1,0:T(8,128)(2,1)} async-done(((bf16[768,8448]{1,0:T(8,128)(2,1)}), bf16[24,8448]{1,0:T(8,128)(2,1)}) %reduce-scatter.3.cloned.1.call-update) | async-done | bytes 405520 | tf_op jit(solution)/shard_map/reduce_scatter | solution.py:97
  592.1 3.0 collective-permute-start.5
  (103 shorter events, 29.7 us)
Async XLA Ops:
  7.2 19.8 %copy-start.8 = (s32[256,6]{0,1:T(8,128)S(1)}, s32[256,6]{0,1:T(8,128)}, u32[]{:S(2)}) copy-start(s32[256,6]{0,1:T(8,128)} %param.20) | copy-start | bytes 18436
  7.2 146.4 %all-gather.5.cloned.1.call-start = ((), (), s32[]{:S(2)}) async-start(), calls=%async_computation.6 | async-start | bytes 13381632 | tf_op jit(solution)/shard_map/all_gather | solution.py:93
  25.9 10.8 %copy-start = (bf16[4,12,7296]{2,1,0:T(8,128)(2,1)}, bf16[4,12,7296]{2,1,0:T(8,128)(2,1)S(1)}, u32[]{:S(2)}) copy-start(bf16[4,12,7296]{2,1,0:T(8,128)(2,1)S(1)} %all-gather.1.refs_1_) | copy-start | bytes 2101252
  36.7 9.3 %slice-start = ((bf16[4,12,7296]{2,1,0:T(8,128)(2,1)}), bf16[4,12,1024]{2,1,0:T(8,128)(2,1)S(1)}, s32[]{:S(2)}) async-start(bf16[4,12,7296]{2,1,0:T(8,128)(2,1)} %copy-done), calls=%async_computation.10 | async-start | bytes 262144 | tf_op jit(solution)/shard_map/slice | solution.py:773
  36.7 9.4 %slice-start.1 = ((bf16[4,12,7296]{2,1,0:T(8,128)(2,1)}), bf16[4,12,2048]{2,1,0:T(8,128)(2,1)S(1)}, s32[]{:S(2)}) async-start(bf16[4,12,7296]{2,1,0:T(8,128)(2,1)} %copy-done), calls=%async_computation.11 | async-start | bytes 524288 | tf_op jit(solution)/shard_map/slice | solution.py:772
  36.8 136.2 %all-to-all-start.1 = ((bf16[64,16,3200]{2,1,0:T(8,128)(2,1)}), bf16[64,16,3200]{2,1,0:T(8,128)(2,1)}, u32[]{:S(2)}, u32[]{:S(2)}) async-start(bf16[64,16,3200]{2,1,0:T(8,128)(2,1)} %bitcast.32), calls=%async_computation.1 | async-start | bytes 13107200 | tf_op jit(solution)/shard_map/all_to_all | solution.py:179
  46.0 4.1 copy-start.3
  46.0 264.0 %all-gather.7.cloned.1.call-start = ((), (), s32[]{:S(2)}) async-start(), calls=%async_computation.7 | async-start | bytes 9732096 | tf_op jit(solution)/shard_map/all_gather | solution.py:93
  47.0 124.0 %collective-permute-start = (bf16[1536,256]{1,0:T(8,128)(2,1)}, bf16[1536,256]{1,0:T(8,128)(2,1)S(1)}, u32[]{:S(2)}, u32[]{:S(2)}) collective-permute-start(bf16[1536,256]{1,0:T(8,128)(2,1)} %bitcast.5.gate_ref), channel_id=1, source_target_pairs={{0,1},{1,0},{2,3},{3,2},{4,5},{5,4},{6,7},{7,6},{8,9},{9,8},{10,11... | collective-permute-start | bytes 2359304 | tf_op jit(solution)/shard_map/ppermute | solution.py:46
  50.0 121.0 %collective-permute-start.1 = (bf16[1536,256]{1,0:T(8,128)(2,1)}, bf16[1536,256]{1,0:T(8,128)(2,1)S(1)}, u32[]{:S(2)}, u32[]{:S(2)}) collective-permute-start(bf16[1536,256]{1,0:T(8,128)(2,1)} %bitcast.39), channel_id=1, source_target_pairs={{0,1},{1,0},{2,3},{3,2},{4,5},{5,4},{6,7},{7,6},{8,9},{9,8},{10,11... | collective-permute-start | bytes 2359304 | tf_op jit(solution)/shard_map/ppermute | solution.py:46
  50.1 120.9 %collective-permute-start.2 = (bf16[256,1536]{1,0:T(8,128)(2,1)S(1)}, bf16[256,1536]{1,0:T(8,128)(2,1)S(1)}, u32[]{:S(2)}, u32[]{:S(2)}) collective-permute-start(bf16[256,1536]{1,0:T(8,128)(2,1)S(1)} %bitcast.37), channel_id=1, source_target_pairs={{0,1},{1,0},{2,3},{3,2},{4,5},{5,4},{6,7},{7,6},{8,9},{9,8},{10,11... | collective-permute-start | bytes 2359304 | tf_op jit(solution)/shard_map/ppermute | solution.py:46
  170.9 0.9 copy-start.4
  171.0 1.1 copy-start.5
  172.1 0.9 copy-start.1
  173.0 102.9 %all-to-all-start = ((bf16[64,16,3072]{2,1,0:T(8,128)(2,1)}), bf16[64,16,3072]{2,1,0:T(8,128)(2,1)}, u32[]{:S(2)}, u32[]{:S(2)}) async-start(bf16[64,16,3072]{2,1,0:T(8,128)(2,1)} %bitcast.27), calls=%async_computation | async-start | bytes 12582912 | tf_op jit(solution)/shard_map/all_to_all | solution.py:179
  297.1 112.9 %all-to-all-start.3 = ((bf16[64,16,3200]{2,1,0:T(8,128)(2,1)}), bf16[64,16,3200]{2,1,0:T(8,128)(2,1)}, u32[]{:S(2)}, u32[]{:S(2)}) async-start(bf16[64,16,3200]{2,1,0:T(8,128)(2,1)} %bitcast.34), calls=%async_computation.3 | async-start | bytes 13107200 | tf_op jit(solution)/shard_map/all_to_all | solution.py:179
  309.9 230.0 %reduce-scatter.5.cloned.1.call-start = ((), (), s32[]{:S(2)}) async-start(), calls=%async_computation.9 | async-start | bytes 9732096 | tf_op jit(solution)/shard_map/reduce_scatter | solution.py:97
  410.0 100.2 %all-to-all-start.2 = ((bf16[64,16,3072]{2,1,0:T(8,128)(2,1)}), bf16[64,16,3072]{2,1,0:T(8,128)(2,1)}, u32[]{:S(2)}, u32[]{:S(2)}) async-start(bf16[64,16,3072]{2,1,0:T(8,128)(2,1)} %bitcast.31), calls=%async_computation.2 | async-start | bytes 12582912 | tf_op jit(solution)/shard_map/all_to_all | solution.py:179
  430.9 160.1 %reduce-scatter.3.cloned.1.call-start = ((), (), s32[]{:S(2)}) async-start(), calls=%async_computation.8 | async-start | bytes 13381632 | tf_op jit(solution)/shard_map/reduce_scatter | solution.py:97
  456.0 64.3 %collective-permute-start.9 = (bf16[1536,256]{1,0:T(8,128)(2,1)}, bf16[1536,256]{1,0:T(8,128)(2,1)}, u32[]{:S(2)}, u32[]{:S(2)}) collective-permute-start(bf16[1536,256]{1,0:T(8,128)(2,1)} %shard_map.295), channel_id=1, source_target_pairs={{0,1},{1,0},{2,3},{3,2},{4,5},{5,4},{6,7},{7,6},{8,9},{9,8},{10,11... | collective-permute-start | bytes 2359304 | tf_op jit(solution)/shard_map/ppermute | solution.py:46
  456.7 80.5 %collective-permute-start.10 = (bf16[1536,256]{1,0:T(8,128)(2,1)}, bf16[1536,256]{1,0:T(8,128)(2,1)}, u32[]{:S(2)}, u32[]{:S(2)}) collective-permute-start(bf16[1536,256]{1,0:T(8,128)(2,1)} %shard_map.296), channel_id=1, source_target_pairs={{0,1},{1,0},{2,3},{3,2},{4,5},{5,4},{6,7},{7,6},{8,9},{9,8},{10,11... | collective-permute-start | bytes 2359304 | tf_op jit(solution)/shard_map/ppermute | solution.py:46
  517.2 3.1 copy-start.2
  517.2 20.0 %copy-start.7 = (f32[1536,256]{1,0:T(8,128)S(1)}, f32[1536,256]{1,0:T(8,128)}, u32[]{:S(2)}) copy-start(f32[1536,256]{1,0:T(8,128)} %get-tuple-element.77) | copy-start | bytes 4718596
  517.2 36.7 %collective-permute-start.11 = (bf16[256,1536]{1,0:T(8,128)(2,1)}, bf16[256,1536]{1,0:T(8,128)(2,1)S(1)}, u32[]{:S(2)}, u32[]{:S(2)}) collective-permute-start(bf16[256,1536]{1,0:T(8,128)(2,1)} %shard_map.297), channel_id=1, source_target_pairs={{0,1},{1,0},{2,3},{3,2},{4,5},{5,4},{6,7},{7,6},{8,9},{9,8},{10,11... | collective-permute-start | bytes 2359304 | tf_op jit(solution)/shard_map/ppermute | solution.py:46
  539.9 14.0 %copy-start.6 = (f32[256,1536]{1,0:T(8,128)S(1)}, f32[256,1536]{1,0:T(8,128)}, u32[]{:S(2)}) copy-start(f32[256,1536]{1,0:T(8,128)} %get-tuple-element.79) | copy-start | bytes 4718596
  541.3 14.0 %collective-permute-start.8 = (bf16[12,3072]{1,0:T(8,128)(2,1)S(1)}, bf16[12,3072]{1,0:T(8,128)(2,1)S(1)}, u32[]{:S(2)}, u32[]{:S(2)}) collective-permute-start(bf16[12,3072]{1,0:T(8,128)(2,1)S(1)} %get-tuple-element.97), channel_id=1, source_target_pairs={{0,65},{1,64},{64,1},{65,0},{2,67},{3,66},{66,3},{67,2},{4,69},{5,... | collective-permute-start | bytes 221192 | tf_op jit(solution)/shard_map/ppermute | solution.py:113
  544.5 14.2 %collective-permute-start.7 = (bf16[12,3072]{1,0:T(8,128)(2,1)S(1)}, bf16[12,3072]{1,0:T(8,128)(2,1)S(1)}, u32[]{:S(2)}, u32[]{:S(2)}) collective-permute-start(bf16[12,3072]{1,0:T(8,128)(2,1)S(1)} %get-tuple-element.96), channel_id=1, source_target_pairs={{0,64},{64,0},{1,65},{65,1},{2,66},{66,2},{3,67},{67,3},{4,68},{68... | collective-permute-start | bytes 221192 | tf_op jit(solution)/shard_map/ppermute | solution.py:46
  545.3 13.4 %collective-permute-start.6 = (bf16[12,3072]{1,0:T(8,128)(2,1)S(1)}, bf16[12,3072]{1,0:T(8,128)(2,1)S(1)}, u32[]{:S(2)}, u32[]{:S(2)}) collective-permute-start(bf16[12,3072]{1,0:T(8,128)(2,1)S(1)} %broadcast_select_fusion.9), channel_id=1, source_target_pairs={{0,1},{1,0},{2,3},{3,2},{4,5},{5,4},{6,7},{7,6},{8,9},{9,8},{10,11... | collective-permute-start | bytes 221192 | tf_op jit(solution)/shard_map/ppermute | solution.py:46
  592.1 7.8 %collective-permute-start.5 = (bf16[12,4224]{1,0:T(8,128)(2,1)S(1)}, bf16[12,4224]{1,0:T(8,128)(2,1)S(1)}, u32[]{:S(2)}, u32[]{:S(2)}) collective-permute-start(bf16[12,4224]{1,0:T(8,128)(2,1)S(1)} %get-tuple-element.92), channel_id=1, source_target_pairs={{0,65},{1,64},{64,1},{65,0},{2,67},{3,66},{66,3},{67,2},{4,69},{5,... | collective-permute-start | bytes 304136 | tf_op jit(solution)/shard_map/ppermute | solution.py:113
  595.1 7.0 %collective-permute-start.4 = (bf16[12,4224]{1,0:T(8,128)(2,1)S(1)}, bf16[12,4224]{1,0:T(8,128)(2,1)S(1)}, u32[]{:S(2)}, u32[]{:S(2)}) collective-permute-start(bf16[12,4224]{1,0:T(8,128)(2,1)S(1)} %get-tuple-element.91), channel_id=1, source_target_pairs={{0,64},{64,0},{1,65},{65,1},{2,66},{66,2},{3,67},{67,3},{4,68},{68... | collective-permute-start | bytes 304136 | tf_op jit(solution)/shard_map/ppermute | solution.py:46
  595.8 6.3 %collective-permute-start.3 = (bf16[12,4224]{1,0:T(8,128)(2,1)S(1)}, bf16[12,4224]{1,0:T(8,128)(2,1)S(1)}, u32[]{:S(2)}, u32[]{:S(2)}) collective-permute-start(bf16[12,4224]{1,0:T(8,128)(2,1)S(1)} %broadcast_select_fusion.6), channel_id=1, source_target_pairs={{0,1},{1,0},{2,3},{3,2},{4,5},{5,4},{6,7},{7,6},{8,9},{9,8},{10,11... | collective-permute-start | bytes 304136 | tf_op jit(solution)/shard_map/ppermute | solution.py:46
Sparse Core Ops, SparseCore 0:
  27.1 126.3 all-gather.4
  156.4 117.7 all-gather.6
  329.3 138.8 reduce-scatter.4
  472.4 118.5 reduce-scatter.2

commit v4 on v3

--- a/solution.py
+++ b/solution.py
@@ -793,15 +793,15 @@
     rows = to_experts(send_rows)
 
     act_cot = act_cots(cot_rows, down, down_other, send_rows)
+    shared_low, pair_low, shared_sum, shared_cot = shared_phase(
+        ffn_in, out_grad, middle, second, act_cot
+    )
+
     weights = (gate, gate_other, up, up_other)
     back, act, gate_cot, up_cot = expert_phase(
-        rows, cot_rows, act_cot, own, pack, weights, send_rows
+        rows, cot_rows, act_cot, own, pack, weights, shared_cot
     )
-    shared_low, pair_low, shared_sum, shared_cot = shared_phase(
-        ffn_in, out_grad, middle, second, act
-    )
-    shared_grad = shared_grads(ffn_in, pair_low, shared_low, out_grad, shared_cot)
-
+    shared_grad = shared_grads(ffn_in, pair_low, shared_low, out_grad, act)
     kept = expert_grads(0, F32, rows, cot_rows, act, gate_cot, up_cot, shared_grad)
     shared_grad = scatter_plane(shared_grad)
     sent = expert_grads(1, BF, rows, cot_rows, act, gate_cot, up_cot, kept[0])

time: 621 us -> 609 us (0.981)
    all_gather x2, waiting for transfers between devices: 102 us -> 178 us  [gather_plane(): lax.all_gather(pairs, PLANE, axis=1, tiled=True).reshape(64 * rows, width)]
    all_to_all x4, waiting for transfers between devices: 180 us -> 112 us  [to_experts(): lax.all_to_all(rows.reshape(EXPERTS, SLOTS // 2, -1), DP, split_axis=0, c...]
    reduce_scatter x2, waiting for transfers between devices: 32.2 us -> 19.7 us  [scatter_plane(): return lax.psum_scatter(grads, PLANE, scatter_dimension=0, tiled=True)]
    ppermute x10, starting transfers between devices: 10.2 us -> 17.9 us  [swap(): return lax.ppermute(x, axis, [(0, 1), (1, 0)])]
  transfers between devices with their start and end apart: 20 -> 20, of which waited for: 11 -> 14; matrix products, arithmetic and copies ran while one was open for 2% -> 2% of each run, Pallas kernels for 23% -> 20%
where the time goes in v4:
time: 609 us; the launch traced here: 606 us
  waiting for transfers between devices  344 us (56%)
  Pallas kernels  142 us (23%)
  starting transfers between devices  67.8 us (11%)
  blocking collectives  15.4 us (3%)
  between operations  14.6 us (2%)
  other arithmetic  11.6 us (2%)
  local copies, waits for them, and re-layouts  9.58 us (2%)
    all_gather x2, waiting for transfers between devices, gather_plane(): lax.all_gather(pairs, PLANE, axis=1, tiled=True).reshape(64 * rows, width)  178 us
    all_to_all x4, waiting for transfers between devices, to_experts(): lax.all_to_all(rows.reshape(EXPERTS, SLOTS // 2, -1), DP, split_axis=0, c...  112 us
    all_to_all x4, starting transfers between devices, to_experts(): lax.all_to_all(rows.reshape(EXPERTS, SLOTS // 2, -1), DP, split_axis=0, c...  48 us
    ppermute x10, waiting for transfers between devices, swap(): return lax.ppermute(x, axis, [(0, 1), (1, 0)])  33.7 us
    pallas_call x2, Pallas kernels, expert_grads(): call(expert_grad_kernel, (8,), [pair, pair, tile(HALF, half), tile(HALF,...  26 us
    pallas_call x1, Pallas kernels, expert_phase(): call(expert_kernel, (8,), [pair(2 * WIDTH), pair(128, 24), tile(512), ful...  21.2 us
    reduce_scatter x2, waiting for transfers between devices, scatter_plane(): return lax.psum_scatter(grads, PLANE, scatter_dimension=0, tiled=True)  19.7 us
    ppermute x10, starting transfers between devices, swap(): return lax.ppermute(x, axis, [(0, 1), (1, 0)])  17.9 us
  transfers between devices with their start and end apart: 20, of which 14 were waited for; matrix products, arithmetic and copies ran while one was open for 2% of the time, Pallas kernels for 20%

profile of v4, /device:TPU:0, one launch (start us, length us, event | category | flops | bytes accessed | tf_op | source)
XLA Modules:
  0.0 605.6 jit_solution(2033332699343759621)
XLA Ops:
  10.5 15.4 %all-gather.1.refs_1_ = bf16[4,12,7296]{2,1,0:T(8,128)(2,1)S(1)} all-gather(bf16[1,12,7296]{2,1,0:T(8,128)(2,1)S(1)} %bitcast.38), channel_id=2, replica_groups=mesh['zh'=2,'x'=4,'y'=4,'c'=2,'zl'=2] {'zh','zl'}, dimensions={0}, use_global_device_ids=true | all-gather | bytes 875520 | tf_op jit(solution)/shard_map/all_gather | solution.py:770
  29.9 7.8 %shard_map.280 = (bf16[2,1024,256]{2,1,0:T(8,128)(2,1)}, bf16[2,256,1024]{2,1,0:T(8,128)(2,1)}, bf16[1024,3200]{1,0:T(8,128)(2,1)}) custom-call(f32[64,256]{1,0:T(8,128)} %slice_select_fusion.rank_ref, bf16[256,1536]{1,0:T(8,128)(2,1)} %refs_7_.1, bf16[256,128]{1,0:T(8,128)(2,1)} %convert.hits_ref), custom_call_target="tpu_custom_call" | custom-call | tf_op jit(solution)/shard_map/pallas_call | solution.py:144
  37.7 9.2 %all-to-all-start.1 = ((bf16[64,16,3200]{2,1,0:T(8,128)(2,1)}), bf16[64,16,3200]{2,1,0:T(8,128)(2,1)}, u32[]{:S(2)}, u32[]{:S(2)}) async-start(bf16[64,16,3200]{2,1,0:T(8,128)(2,1)} %bitcast.32), calls=%async_computation.1 | async-start | bytes 13107200 | tf_op jit(solution)/shard_map/all_to_all | solution.py:179
  46.9 3.0 collective-permute-start
  52.0 100.0 %all-gather.5.cloned.1.call-done = bf16[2,768,4224]{2,1,0:T(8,128)(2,1)} async-done(((bf16[2,24,4224]{2,1,0:T(8,128)(2,1)}), bf16[2,768,4224]{2,1,0:T(8,128)(2,1)}) %all-gather.5.cloned.1.call-update) | async-done | bytes 12976144 | tf_op jit(solution)/shard_map/all_gather | solution.py:93
  152.0 11.1 %shard_map.281 = (bf16[256,1536]{1,0:T(8,128)(2,1)}, bf16[256,1536]{1,0:T(8,128)(2,1)}, bf16[256,1024]{1,0:T(8,128)(2,1)}, f32[12,256,256]{2,1,0:T(8,128)}, bf16...) custom-call(bf16[256,1536]{1,0:T(8,128)(2,1)} %refs_11_.1, ...), custom_call_target="tpu_custom_call" | custom-call | tf_op jit(solution)/shard_map/pallas_call | solution.py:308
  163.1 6.0 shard_map.282.refs_0_
  169.1 2.5 collective-permute-done.2.refs_3_.other_ref
  172.5 11.2 %all-to-all-start = ((bf16[64,16,3072]{2,1,0:T(8,128)(2,1)}), bf16[64,16,3072]{2,1,0:T(8,128)(2,1)}, u32[]{:S(2)}, u32[]{:S(2)}) async-start(bf16[64,16,3072]{2,1,0:T(8,128)(2,1)} %bitcast.30), calls=%async_computation | async-start | bytes 12582912 | tf_op jit(solution)/shard_map/all_to_all | solution.py:179
  184.2 9.7 %shard_map.285._after_ref.act_cot_ref = f32[2048,512]{1,0:T(8,128)} custom-call(bf16[1024,3200]{1,0:T(8,128)(2,1)} %bitcast.11.cot_ref.marks_ref, bf16[256,1536]{1,0:T(8,128)(2,1)} %bitcast.35, bf16[256,1536]{1,0:T(8,128)(2,1)} %copy-done.1, bf16[1024,3072]{1,0:T(8,128)(2,1)} %shard_map.283._after_ref), custom_call_target="tpu_custom_call" | custom-call | tf_op jit(solution)/shard_map/pallas_call | solution.py:330
  193.9 77.7 %all-gather.7.cloned.1.call-done = bf16[2,768,3072]{2,1,0:T(8,128)(2,1)} async-done(((bf16[2,24,3072]{2,1,0:T(8,128)(2,1)}), bf16[2,768,3072]{2,1,0:T(8,128)(2,1)}) %all-gather.7.cloned.1.call-update) | async-done | bytes 9437200 | tf_op jit(solution)/shard_map/all_gather | solution.py:93
  271.6 12.1 %shard_map.286 = (bf16[256,1024]{1,0:T(8,128)(2,1)}, bf16[256,2048]{1,0:T(8,128)(2,1)}, f32[256,1536]{1,0:T(8,128)}, f32[256,1536]{1,0:T(8,128)}) custom-call(bf16[256,1536]{1,0:T(8,128)(2,1)} %get-tuple-element.50.rows_ref.ffn_in_ref, bf16[256,1536]{1,0:T(8,128)(2,1)} %refs_7_.1, f32[256,1536]{1,0:T(8,128)} %get-tuple-element.52.middle_ref.refs_5_, ...), custom_call_target="tpu_custom_call" | custom-call | tf_op jit(solution)/shard_map/pallas_call | solution.py:520
  283.7 21.2 %shard_map.287 = (bf16[1024,3200]{1,0:T(8,128)(2,1)}, bf16[2048,512]{1,0:T(8,128)(2,1)}, bf16[2048,512]{1,0:T(8,128)(2,1)}, bf16[2048,512]{1,0:T(8,128)(2,1)}) custom-call(bf16[1024,3072]{1,0:T(8,128)(2,1)} %bitcast.9.rows_ref, bf16[1024,3200]{1,0:T(8,128)(2,1)} %bitcast.11.cot_ref.marks_ref, f32[2048,512]{1,0:T(8,128)} %shard_map.285._after_ref.act_cot_ref, ...), custom_call_target="tpu_custom_call" | custom-call | tf_op jit(solution)/shard_map/pallas_call | solution.py:405
  304.9 12.2 %all-to-all-start.3 = ((bf16[64,16,3200]{2,1,0:T(8,128)(2,1)}), bf16[64,16,3200]{2,1,0:T(8,128)(2,1)}, u32[]{:S(2)}, u32[]{:S(2)}) async-start(bf16[64,16,3200]{2,1,0:T(8,128)(2,1)} %bitcast.34), calls=%async_computation.3 | async-start | bytes 13107200 | tf_op jit(solution)/shard_map/all_to_all | solution.py:179
  317.2 7.1 %shard_map.288._after_ref = bf16[768,6144]{1,0:T(8,128)(2,1)} custom-call(bf16[256,1536]{1,0:T(8,128)(2,1)} %get-tuple-element.50.rows_ref.ffn_in_ref, bf16[256,2048]{1,0:T(8,128)(2,1)} %get-tuple-element.57.pair_ref, bf16[256,1024]{1,0:T(8,128)(2,1)} %get-tuple-element.58.act_ref, bf16[256,1536]{1,0:T(8,128)(2,1)} %refs_7_.1, ...), custom_call_target="tpu_custom_call" | custom-call | tf_op jit(solution)/shard_map/pallas_call | solution.py:549
  324.3 13.2 %shard_map.289 = (f32[1536,256]{1,0:T(8,128)}, f32[1536,256]{1,0:T(8,128)}, f32[256,1536]{1,0:T(8,128)}) custom-call(bf16[1024,3072]{1,0:T(8,128)(2,1)} %bitcast.9.rows_ref, bf16[1024,3200]{1,0:T(8,128)(2,1)} %bitcast.11.cot_ref.marks_ref, bf16[2048,512]{1,0:T(8,128)(2,1)} %get-tuple-element.54._after_ref.act_ref, ...), custom_call_target="tpu_custom_call" | custom-call | tf_op jit(solution)/shard_map/pallas_call | solution.py:464
  337.5 12.8 %shard_map.290 = (bf16[1536,256]{1,0:T(8,128)(2,1)}, bf16[1536,256]{1,0:T(8,128)(2,1)}, bf16[256,1536]{1,0:T(8,128)(2,1)}) custom-call(bf16[1024,3072]{1,0:T(8,128)(2,1)} %bitcast.9.rows_ref, bf16[1024,3200]{1,0:T(8,128)(2,1)} %bitcast.11.cot_ref.marks_ref, bf16[2048,512]{1,0:T(8,128)(2,1)} %get-tuple-element.54._after_ref.act_ref, ...), custom_call_target="tpu_custom_call" | custom-call | tf_op jit(solution)/shard_map/pallas_call | solution.py:464
  350.4 9.2 %shard_map.291.refs_12_ = bf16[1024,3072]{1,0:T(8,128)(2,1)} custom-call(bf16[2048,512]{1,0:T(8,128)(2,1)} %get-tuple-element.54._after_ref.act_ref, bf16[256,1536]{1,0:T(8,128)(2,1)} %bitcast.36, bf16[256,1536]{1,0:T(8,128)(2,1)} %copy-done.1, bf16[1536,256]{1,0:T(8,128)(2,1)} %get-tuple-element.60._after_ref.refs_0_), custom_call_target="tpu_custom_call" | custom-call | tf_op jit(solution)/shard_map/pallas_call | solution.py:423
  359.6 60.4 %all-to-all-done.3 = bf16[64,16,3200]{2,1,0:T(8,128)(2,1)} async-done(((bf16[64,16,3200]{2,1,0:T(8,128)(2,1)}), bf16[64,16,3200]{2,1,0:T(8,128)(2,1)}, u32[]{:S(2)}, u32[]{:S(2)}) %all-to-all-start.3) | async-done | bytes 6553632 | tf_op jit(solution)/shard_map/all_to_all | solution.py:179
  420.0 15.4 %all-to-all-start.2 = ((bf16[64,16,3072]{2,1,0:T(8,128)(2,1)}), bf16[64,16,3072]{2,1,0:T(8,128)(2,1)}, u32[]{:S(2)}, u32[]{:S(2)}) async-start(bf16[64,16,3072]{2,1,0:T(8,128)(2,1)} %bitcast.31), calls=%async_computation.2 | async-start | bytes 12582912 | tf_op jit(solution)/shard_map/all_to_all | solution.py:179
  435.6 15.7 %shard_map.293 = (bf16[256,1536]{1,0:T(8,128)(2,1)}, bf16[256,1536]{1,0:T(8,128)(2,1)}, bf16[256,1024]{1,0:T(8,128)(2,1)}, f32[256,1536]{1,0:T(8,128)}, bf16[256...) custom-call(bf16[1024,3200]{1,0:T(8,128)(2,1)} %bitcast.16.refs_0_, ...), custom_call_target="tpu_custom_call" | custom-call | tf_op jit(solution)/shard_map/pallas_call | solution.py:680
  451.4 9.2 %shard_map.294.refs_1_ = bf16[768,8448]{1,0:T(8,128)(2,1)} custom-call(bf16[256,1536]{1,0:T(8,128)(2,1)} %get-tuple-element.69.attn_in_ref, bf16[256,1536]{1,0:T(8,128)(2,1)} %get-tuple-element.70.attended_ref, bf16[256,1536]{1,0:T(8,128)(2,1)} %get-tuple-element.50.rows_ref.ffn_in_ref, bf16[256,1536]{1,0:T(8,128)(2,1)} %get-tuple-element.71.gain_one_ref, ...), custom_call_target="tpu_custom_call" | custom-call | flops 9999999827968 | tf_op jit(solution)/shard_map/pallas_call | solution.py:738
  460.6 3.3 collective-permute-start.9
  464.0 51.3 %all-to-all-done.2 = bf16[64,16,3072]{2,1,0:T(8,128)(2,1)} async-done(((bf16[64,16,3072]{2,1,0:T(8,128)(2,1)}), bf16[64,16,3072]{2,1,0:T(8,128)(2,1)}, u32[]{:S(2)}, u32[]{:S(2)}) %all-to-all-start.2) | async-done | bytes 6291488 | tf_op jit(solution)/shard_map/all_to_all | solution.py:179
  515.3 6.8 %shard_map.292 = bf16[256,1536]{1,0:T(8,128)(2,1)} custom-call(bf16[2,256,1024]{2,1,0:T(8,128)(2,1)} %get-tuple-element.48.turned_ref.refs_2_, bf16[1024,3072]{1,0:T(8,128)(2,1)} %bitcast.14.rows_ref, f32[256,1536]{1,0:T(8,128)} %get-tuple-element.61.base_ref), custom_call_target="tpu_custom_call" | custom-call | flops 9999999827968 | tf_op jit(solution)/shard_map/pallas_call | solution.py:199
  527.2 14.4 %collective-permute-done.10 = bf16[1536,256]{1,0:T(8,128)(2,1)} collective-permute-done((bf16[1536,256]{1,0:T(8,128)(2,1)}, bf16[1536,256]{1,0:T(8,128)(2,1)}, u32[]{:S(2)}, u32[]{:S(2)}) %collective-permute-start.10) | collective-permute-done | bytes 786464 | tf_op jit(solution)/shard_map/ppermute | solution.py:46
  545.8 3.5 collective-permute-start.7
  550.5 7.9 %collective-permute-done.11 = bf16[256,1536]{1,0:T(8,128)(2,1)S(1)} collective-permute-done((bf16[256,1536]{1,0:T(8,128)(2,1)}, bf16[256,1536]{1,0:T(8,128)(2,1)S(1)}, u32[]{:S(2)}, u32[]{:S(2)}) %collective-permute-start.11) | collective-permute-done | bytes 786464 | tf_op jit(solution)/shard_map/ppermute | solution.py:46
  560.5 3.0 collective-permute-done.7
  563.6 19.7 %reduce-scatter.3.cloned.1.call-done = bf16[24,8448]{1,0:T(8,128)(2,1)} async-done(((bf16[768,8448]{1,0:T(8,128)(2,1)}), bf16[24,8448]{1,0:T(8,128)(2,1)}) %reduce-scatter.3.cloned.1.call-update) | async-done | bytes 405520 | tf_op jit(solution)/shard_map/reduce_scatter | solution.py:97
  586.2 2.9 collective-permute-start.4
  590.9 3.4 collective-permute-done.4
  (101 shorter events, 32.6 us)
Async XLA Ops:
  7.2 144.8 %all-gather.5.cloned.1.call-start = ((), (), s32[]{:S(2)}) async-start(), calls=%async_computation.6 | async-start | bytes 13381632 | tf_op jit(solution)/shard_map/all_gather | solution.py:93
  25.9 2.1 copy-start
  25.9 2.1 copy-start.8
  27.0 244.6 %all-gather.7.cloned.1.call-start = ((), (), s32[]{:S(2)}) async-start(), calls=%async_computation.7 | async-start | bytes 9732096 | tf_op jit(solution)/shard_map/all_gather | solution.py:93
  37.7 12.3 %copy-start.3 = (bf16[1,256,1536]{2,1,0:T(8,128)(2,1)S(1)}, bf16[1,256,1536]{2,1,0:T(8,128)(2,1)}, u32[]{:S(2)}) copy-start(bf16[1,256,1536]{2,1,0:T(8,128)(2,1)} %param.33) | copy-start | bytes 2359300
  37.7 134.8 %all-to-all-start.1 = ((bf16[64,16,3200]{2,1,0:T(8,128)(2,1)}), bf16[64,16,3200]{2,1,0:T(8,128)(2,1)}, u32[]{:S(2)}, u32[]{:S(2)}) async-start(bf16[64,16,3200]{2,1,0:T(8,128)(2,1)} %bitcast.32), calls=%async_computation.1 | async-start | bytes 13107200 | tf_op jit(solution)/shard_map/all_to_all | solution.py:179
  46.9 122.1 %collective-permute-start = (bf16[1536,256]{1,0:T(8,128)(2,1)}, bf16[1536,256]{1,0:T(8,128)(2,1)S(1)}, u32[]{:S(2)}, u32[]{:S(2)}) collective-permute-start(bf16[1536,256]{1,0:T(8,128)(2,1)} %bitcast.5.gate_ref), channel_id=1, source_target_pairs={{0,1},{1,0},{2,3},{3,2},{4,5},{5,4},{6,7},{7,6},{8,9},{9,8},{10,11... | collective-permute-start | bytes 2359304 | tf_op jit(solution)/shard_map/ppermute | solution.py:46
  49.9 119.2 %collective-permute-start.1 = (bf16[1536,256]{1,0:T(8,128)(2,1)}, bf16[1536,256]{1,0:T(8,128)(2,1)S(1)}, u32[]{:S(2)}, u32[]{:S(2)}) collective-permute-start(bf16[1536,256]{1,0:T(8,128)(2,1)} %bitcast.6.up_ref), channel_id=1, source_target_pairs={{0,1},{1,0},{2,3},{3,2},{4,5},{5,4},{6,7},{7,6},{8,9},{9,8},{10,11... | collective-permute-start | bytes 2359304 | tf_op jit(solution)/shard_map/ppermute | solution.py:46
  50.0 121.6 %collective-permute-start.2 = (bf16[256,1536]{1,0:T(8,128)(2,1)S(1)}, bf16[256,1536]{1,0:T(8,128)(2,1)S(1)}, u32[]{:S(2)}, u32[]{:S(2)}) collective-permute-start(bf16[256,1536]{1,0:T(8,128)(2,1)S(1)} %bitcast.37), channel_id=1, source_target_pairs={{0,1},{1,0},{2,3},{3,2},{4,5},{5,4},{6,7},{7,6},{8,9},{9,8},{10,11... | collective-permute-start | bytes 2359304 | tf_op jit(solution)/shard_map/ppermute | solution.py:46
  169.1 2.5 copy-start.4
  169.1 2.5 copy-start.5
  171.6 0.9 copy-start.1
  172.5 111.2 %all-to-all-start = ((bf16[64,16,3072]{2,1,0:T(8,128)(2,1)}), bf16[64,16,3072]{2,1,0:T(8,128)(2,1)}, u32[]{:S(2)}, u32[]{:S(2)}) async-start(bf16[64,16,3072]{2,1,0:T(8,128)(2,1)} %bitcast.30), calls=%async_computation | async-start | bytes 12582912 | tf_op jit(solution)/shard_map/all_to_all | solution.py:179
  304.9 115.1 %all-to-all-start.3 = ((bf16[64,16,3200]{2,1,0:T(8,128)(2,1)}), bf16[64,16,3200]{2,1,0:T(8,128)(2,1)}, u32[]{:S(2)}, u32[]{:S(2)}) async-start(bf16[64,16,3200]{2,1,0:T(8,128)(2,1)} %bitcast.34), calls=%async_computation.3 | async-start | bytes 13107200 | tf_op jit(solution)/shard_map/all_to_all | solution.py:179
  317.1 227.0 %reduce-scatter.5.cloned.1.call-start = ((), (), s32[]{:S(2)}) async-start(), calls=%async_computation.9 | async-start | bytes 9732096 | tf_op jit(solution)/shard_map/reduce_scatter | solution.py:97
  420.0 95.3 %all-to-all-start.2 = ((bf16[64,16,3072]{2,1,0:T(8,128)(2,1)}), bf16[64,16,3072]{2,1,0:T(8,128)(2,1)}, u32[]{:S(2)}, u32[]{:S(2)}) async-start(bf16[64,16,3072]{2,1,0:T(8,128)(2,1)} %bitcast.31), calls=%async_computation.2 | async-start | bytes 12582912 | tf_op jit(solution)/shard_map/all_to_all | solution.py:179
  435.4 148.0 %reduce-scatter.3.cloned.1.call-start = ((), (), s32[]{:S(2)}) async-start(), calls=%async_computation.8 | async-start | bytes 13381632 | tf_op jit(solution)/shard_map/reduce_scatter | solution.py:97
  460.6 64.2 %collective-permute-start.9 = (bf16[1536,256]{1,0:T(8,128)(2,1)}, bf16[1536,256]{1,0:T(8,128)(2,1)}, u32[]{:S(2)}, u32[]{:S(2)}) collective-permute-start(bf16[1536,256]{1,0:T(8,128)(2,1)} %shard_map.295), channel_id=1, source_target_pairs={{0,1},{1,0},{2,3},{3,2},{4,5},{5,4},{6,7},{7,6},{8,9},{9,8},{10,11... | collective-permute-start | bytes 2359304 | tf_op jit(solution)/shard_map/ppermute | solution.py:46
  463.9 77.8 %collective-permute-start.10 = (bf16[1536,256]{1,0:T(8,128)(2,1)}, bf16[1536,256]{1,0:T(8,128)(2,1)}, u32[]{:S(2)}, u32[]{:S(2)}) collective-permute-start(bf16[1536,256]{1,0:T(8,128)(2,1)} %shard_map.296), channel_id=1, source_target_pairs={{0,1},{1,0},{2,3},{3,2},{4,5},{5,4},{6,7},{7,6},{8,9},{9,8},{10,11... | collective-permute-start | bytes 2359304 | tf_op jit(solution)/shard_map/ppermute | solution.py:46
  522.1 2.8 copy-start.2
  522.1 19.6 %copy-start.7 = (f32[1536,256]{1,0:T(8,128)S(1)}, f32[1536,256]{1,0:T(8,128)}, u32[]{:S(2)}) copy-start(f32[1536,256]{1,0:T(8,128)} %get-tuple-element.77) | copy-start | bytes 4718596
  522.1 36.3 %collective-permute-start.11 = (bf16[256,1536]{1,0:T(8,128)(2,1)}, bf16[256,1536]{1,0:T(8,128)(2,1)S(1)}, u32[]{:S(2)}, u32[]{:S(2)}) collective-permute-start(bf16[256,1536]{1,0:T(8,128)(2,1)} %shard_map.297), channel_id=1, source_target_pairs={{0,1},{1,0},{2,3},{3,2},{4,5},{5,4},{6,7},{7,6},{8,9},{9,8},{10,11... | collective-permute-start | bytes 2359304 | tf_op jit(solution)/shard_map/ppermute | solution.py:46
  544.2 14.3 %copy-start.6 = (f32[256,1536]{1,0:T(8,128)S(1)}, f32[256,1536]{1,0:T(8,128)}, u32[]{:S(2)}) copy-start(f32[256,1536]{1,0:T(8,128)} %get-tuple-element.79) | copy-start | bytes 4718596
  545.6 14.9 %collective-permute-start.6 = (bf16[12,3072]{1,0:T(8,128)(2,1)S(1)}, bf16[12,3072]{1,0:T(8,128)(2,1)S(1)}, u32[]{:S(2)}, u32[]{:S(2)}) collective-permute-start(bf16[12,3072]{1,0:T(8,128)(2,1)S(1)} %broadcast_select_fusion.9), channel_id=1, source_target_pairs={{0,1},{1,0},{2,3},{3,2},{4,5},{5,4},{6,7},{7,6},{8,9},{9,8},{10,11... | collective-permute-start | bytes 221192 | tf_op jit(solution)/shard_map/ppermute | solution.py:46
  545.8 17.8 %collective-permute-start.7 = (bf16[12,3072]{1,0:T(8,128)(2,1)S(1)}, bf16[12,3072]{1,0:T(8,128)(2,1)S(1)}, u32[]{:S(2)}, u32[]{:S(2)}) collective-permute-start(bf16[12,3072]{1,0:T(8,128)(2,1)S(1)} %get-tuple-element.96), channel_id=1, source_target_pairs={{0,64},{64,0},{1,65},{65,1},{2,66},{66,2},{3,67},{67,3},{4,68},{68... | collective-permute-start | bytes 221192 | tf_op jit(solution)/shard_map/ppermute | solution.py:46
  549.3 14.2 %collective-permute-start.8 = (bf16[12,3072]{1,0:T(8,128)(2,1)S(1)}, bf16[12,3072]{1,0:T(8,128)(2,1)S(1)}, u32[]{:S(2)}, u32[]{:S(2)}) collective-permute-start(bf16[12,3072]{1,0:T(8,128)(2,1)S(1)} %get-tuple-element.97), channel_id=1, source_target_pairs={{0,65},{1,64},{64,1},{65,0},{2,67},{3,66},{66,3},{67,2},{4,69},{5,... | collective-permute-start | bytes 221192 | tf_op jit(solution)/shard_map/ppermute | solution.py:113
  584.5 6.4 %collective-permute-start.3 = (bf16[12,4224]{1,0:T(8,128)(2,1)S(1)}, bf16[12,4224]{1,0:T(8,128)(2,1)S(1)}, u32[]{:S(2)}, u32[]{:S(2)}) collective-permute-start(bf16[12,4224]{1,0:T(8,128)(2,1)S(1)} %broadcast_select_fusion.6), channel_id=1, source_target_pairs={{0,1},{1,0},{2,3},{3,2},{4,5},{5,4},{6,7},{7,6},{8,9},{9,8},{10,11... | collective-permute-start | bytes 304136 | tf_op jit(solution)/shard_map/ppermute | solution.py:46
  586.2 8.2 %collective-permute-start.4 = (bf16[12,4224]{1,0:T(8,128)(2,1)S(1)}, bf16[12,4224]{1,0:T(8,128)(2,1)S(1)}, u32[]{:S(2)}, u32[]{:S(2)}) collective-permute-start(bf16[12,4224]{1,0:T(8,128)(2,1)S(1)} %get-tuple-element.91), channel_id=1, source_target_pairs={{0,64},{64,0},{1,65},{65,1},{2,66},{66,2},{3,67},{67,3},{4,68},{68... | collective-permute-start | bytes 304136 | tf_op jit(solution)/shard_map/ppermute | solution.py:46
  589.0 6.9 %collective-permute-start.5 = (bf16[12,4224]{1,0:T(8,128)(2,1)S(1)}, bf16[12,4224]{1,0:T(8,128)(2,1)S(1)}, u32[]{:S(2)}, u32[]{:S(2)}) collective-permute-start(bf16[12,4224]{1,0:T(8,128)(2,1)S(1)} %get-tuple-element.92), channel_id=1, source_target_pairs={{0,65},{1,64},{64,1},{65,0},{2,67},{3,66},{66,3},{67,2},{4,69},{5,... | collective-permute-start | bytes 304136 | tf_op jit(solution)/shard_map/ppermute | solution.py:113
Sparse Core Ops, SparseCore 0:
  27.1 124.8 all-gather.4
  154.8 116.7 all-gather.6
  324.4 125.1 reduce-scatter.4
  460.7 122.5 reduce-scatter.2

commit v5 on v4

--- a/solution.py
+++ b/solution.py
@@ -158,23 +158,6 @@
     )(rank, out_grad, hits)
 
 
-def dispatch_kernel(deal_ref, rows_ref, out_ref):
-    out_ref[...] = mm(deal_ref[0], rows_ref[...]).astype(BF)
-
-
-def dispatch(deal, rows):
-    return call(
-        dispatch_kernel,
-        (4,),
-        [
-            pl.BlockSpec((1, PAIRS, TOKENS), lambda j: (j // 2, 0, 0)),
-            pl.BlockSpec((TOKENS, 768), lambda j: (0, j % 2)),
-        ],
-        pl.BlockSpec((PAIRS, 768), lambda j: (0, j)),
-        out((PAIRS, 2 * WIDTH), BF),
-    )(deal, rows)
-
-
 def to_experts(rows):
     return lax.all_to_all(
         rows.reshape(EXPERTS, SLOTS // 2, -1), DP, split_axis=0, concat_axis=0, tiled=True
@@ -215,44 +198,49 @@
     return lax.rsqrt(jnp.mean(values * values, axis=-1, keepdims=True) + EPSILON)
 
 
-def forward_kernel(
-    hidden_ref,
-    docs_ref,
-    hits_ref,
-    pack_ref,
-    attn_in_ref,
-    q_ref,
-    kv_ref,
-    probs_ref,
-    attended_ref,
-    middle_ref,
-    ffn_in_ref,
-    gates_ref,
-    gains_ref,
-    small_ref,
-    wq_ref,
-    wkv_ref,
-    wo_ref,
-    sems,
-):
+def forward_kernel(hidden_ref, docs_ref, hits_ref, pack_ref, deal_hbm, *refs):
+    outs, (small_ref, wq_ref, wkv_ref, wo_ref, deal_ref), held = refs[:10], refs[10:15], refs[15:25]
+    sems = refs[25]
+    (
+        attn_in_ref,
+        q_ref,
+        kv_ref,
+        probs_ref,
+        attended_ref,
+        middle_ref,
+        ffn_in_ref,
+        gates_ref,
+        gains_ref,
+        send_ref,
+    ) = held
     copies = [
         fetch(pack_ref.at[:, at : at + ref.shape[1]], ref, sems.at[i])
         for i, (at, ref) in enumerate(
             [(2 * WIDTH + 1024, small_ref), (0, wq_ref), (2 * WIDTH, wkv_ref), (WIDTH, wo_ref)]
         )
     ]
+    copies.append(fetch(deal_hbm, deal_ref, sems.at[4]))
+    sent = []
+
+    def send(i):
+        sent.append(fetch(held[i], outs[i], sems.at[5 + i]))
+
     copies[0].wait()
     gains = jnp.transpose(small_ref[...].astype(F32))
     gains_ref[...] = gains[64:72]
     gain_one, gain_two = gains[64:65], gains[65:66]
     tokens = hidden_ref[...].astype(F32)
     attn_in_ref[...] = (tokens * root_scale(tokens) * gain_one).astype(BF)
+    send(8)
+    send(0)
     copies[1].wait()
     for j in range(0, WIDTH, 512):
         q_ref[:, j : j + 512] = mm(attn_in_ref[...], wq_ref[:, j : j + 512]).astype(BF)
+    send(1)
     copies[2].wait()
     for j in range(0, 1024, 512):
         kv_ref[:, j : j + 512] = mm(attn_in_ref[...], wkv_ref[:, j : j + 512]).astype(BF)
+    send(2)
     first = docs_ref[0, 0]
     second = first + docs_ref[0, 1]
     third = second + docs_ref[0, 2]
@@ -277,6 +265,8 @@
             probs = exponent / jnp.sum(exponent, axis=-1, keepdims=True)
             probs_ref[head] = probs
             attended_ref[:, at] = mm(probs.astype(BF), value).astype(BF)
+    send(3)
+    send(4)
     copies[3].wait()
     for j in range(0, WIDTH, 512):
         at = slice(j, j + 512)
@@ -284,15 +274,26 @@
             attended_ref[...], wo_ref[:, at]
         )
     middle = middle_ref[...]
+    send(5)
     ffn_in_ref[...] = (middle * root_scale(middle) * gain_two).astype(BF)
+    send(6)
+    copies[4].wait()
+    for j in range(4):
+        at = slice(j * 768, (j + 1) * 768)
+        from_at = slice(j % 2 * 768, (j % 2 + 1) * 768)
+        send_ref[:, at] = mm(deal_ref[j // 2], ffn_in_ref[:, from_at]).astype(BF)
+        sent.append(fetch(send_ref.at[:, at], outs[9].at[:, at], sems.at[14 + j]))
     logits = mm(ffn_in_ref[...], small_ref[...])
     hits = hits_ref[...] > 0
     top = jnp.max(jnp.where(hits, logits, NEGATIVE), axis=-1, keepdims=True)
     weight = jnp.where(hits, jnp.exp(jnp.where(hits, logits - top, 0.0)), 0.0)
     gates_ref[...] = weight / jnp.sum(weight, axis=-1, keepdims=True)
-
-
-def forward(hidden, docs, hits, pack):
+    send(7)
+    for copy in sent:
+        copy.wait()
+
+
+def forward(hidden, docs, hits, pack, deal):
     wide = (TOKENS, WIDTH)
     shapes = [
         (wide, BF),
@@ -304,16 +305,19 @@
         (wide, BF),
         ((TOKENS, 128), F32),
         ((8, WIDTH), F32),
+        ((PAIRS, 2 * WIDTH), BF),
     ]
     return call(
         forward_kernel,
         (1,),
-        [full(wide), pl.BlockSpec(memory_space=pltpu.SMEM), full((TOKENS, 128)), ANY],
-        [full(s) for s, _ in shapes],
+        [full(wide), pl.BlockSpec(memory_space=pltpu.SMEM), full((TOKENS, 128)), ANY, ANY],
+        [ANY] * 10,
         [out(s, d) for s, d in shapes],
         [pltpu.VMEM((WIDTH, w), BF) for w in (128, WIDTH, 1024, WIDTH)]
-        + [pltpu.SemaphoreType.DMA((4,))],
-    )(hidden, docs, hits, pack)
+        + [pltpu.VMEM(deal.shape, BF)]
+        + [pltpu.VMEM(s, d) for s, d in shapes]
+        + [pltpu.SemaphoreType.DMA((18,))],
+    )(hidden, docs, hits, pack, deal)
 
 
 def unpaired(ref):
@@ -471,31 +475,32 @@
     )(rows, cot_rows, act, gate_cot, up_cot, after)
 
 
+def unfold_into(down_ref, fold_ref, tail_ref):
+    for j in range(2):
+        at = slice(j * 512, (j + 1) * 512)
+        rows = fold_ref[:, at].astype(F32).reshape(64, 24, 512)
+        down_ref[:, at] = rows[:, :16].reshape(SHARED, 512).astype(BF)
+        tail_ref[:, j * 8 : (j + 1) * 8] = rows[:, 16:]
+    down_ref[:, 1024:] = tail_ref[...].reshape(SHARED, 512).astype(BF)
+
+
 def shared_kernel(
     ffn_in_ref,
     out_grad_ref,
-    middle_ref,
     second_ref,
     _after_ref,
     act_ref,
     pair_cot_ref,
-    sum_ref,
-    cot_ref,
     pair_w_ref,
     fold_ref,
     down_ref,
     tail_ref,
     sems,
 ):
-    pair_copy = fetch(second_ref.at[:, : 2 * SHARED], pair_w_ref, sems.at[0])
-    fold_copy = fetch(second_ref.at[:, 2 * SHARED :], fold_ref, sems.at[1])
+    fold_copy = fetch(second_ref.at[:, 2 * SHARED :], fold_ref, sems.at[0])
+    pair_copy = fetch(second_ref.at[:, : 2 * SHARED], pair_w_ref, sems.at[1])
     fold_copy.wait()
-    for j in range(2):
-        at = slice(j * 512, (j + 1) * 512)
-        rows = fold_ref[:, at].astype(F32).reshape(64, 24, 512)
-        down_ref[:, at] = rows[:, :16].reshape(SHARED, 512).astype(BF)
-        tail_ref[:, j * 8 : (j + 1) * 8] = rows[:, 16:]
-    down_ref[:, 1024:] = tail_ref[...].reshape(SHARED, 512).astype(BF)
+    unfold_into(down_ref, fold_ref, tail_ref)
     pair_copy.wait()
     for j in range(0, SHARED, 256):
         at = slice(j, j + 256)
@@ -508,29 +513,66 @@
         cot = mm_r(out_grad_ref[...], down_ref[at, :])
         pair_cot_ref[:, at] = (cot * upper * (sig * (1.0 + gate * (1.0 - sig)))).astype(BF)
         pair_cot_ref[:, up_at] = (cot * silu).astype(BF)
+
+
+def shared_scratch():
+    return [
+        pltpu.VMEM((WIDTH, 2 * SHARED), BF),
+        pltpu.VMEM((WIDTH, 1024), BF),
+        pltpu.VMEM((SHARED, WIDTH), BF),
+        pltpu.VMEM((64, 16, 512), F32),
+        pltpu.SemaphoreType.DMA((2,)),
+    ]
+
+
+def shared_phase(ffn_in, out_grad, second, after):
+    wide = (TOKENS, WIDTH)
+    shapes = [(TOKENS, SHARED), (TOKENS, 2 * SHARED)]
+    return call(
+        shared_kernel,
+        (1,),
+        [full(wide), full(wide), ANY, ANY],
+        [full(s) for s in shapes],
+        [out(s, BF) for s in shapes],
+        shared_scratch(),
+    )(ffn_in, out_grad, second, after)
+
+
+def shared_end_kernel(
+    act_ref,
+    pair_cot_ref,
+    middle_ref,
+    second_ref,
+    _after_ref,
+    sum_ref,
+    cot_ref,
+    pair_w_ref,
+    fold_ref,
+    down_ref,
+    tail_ref,
+    sems,
+):
+    fold_copy = fetch(second_ref.at[:, 2 * SHARED :], fold_ref, sems.at[0])
+    pair_copy = fetch(second_ref.at[:, : 2 * SHARED], pair_w_ref, sems.at[1])
+    fold_copy.wait()
+    unfold_into(down_ref, fold_ref, tail_ref)
+    pair_copy.wait()
     for j in range(0, WIDTH, 512):
         at = slice(j, j + 512)
         sum_ref[:, at] = middle_ref[:, at] + mm(act_ref[...], down_ref[:, at])
         cot_ref[:, at] = mm_r(pair_cot_ref[...], pair_w_ref[at, :])
 
 
-def shared_phase(ffn_in, out_grad, middle, second, after):
+def shared_end(act, pair_cot, middle, second, after):
     wide = (TOKENS, WIDTH)
-    shapes = [((TOKENS, SHARED), BF), ((TOKENS, 2 * SHARED), BF), (wide, F32), (wide, F32)]
-    return call(
-        shared_kernel,
+    return call(
+        shared_end_kernel,
         (1,),
-        [full(wide), full(wide), full(wide), ANY, ANY],
-        [full(s) for s, _ in shapes],
-        [out(s, d) for s, d in shapes],
-        [
-            pltpu.VMEM((WIDTH, 2 * SHARED), BF),
-            pltpu.VMEM((WIDTH, 1024), BF),
-            pltpu.VMEM((SHARED, WIDTH), BF),
-            pltpu.VMEM((64, 16, 512), F32),
-            pltpu.SemaphoreType.DMA((2,)),
-        ],
-    )(ffn_in, out_grad, middle, second, after)
+        [full(act.shape), full(pair_cot.shape), full(wide), ANY, ANY],
+        [full(wide)] * 2,
+        [out(wide, F32)] * 2,
+        shared_scratch(),
+    )(act, pair_cot, middle, second, after)
 
 
 def shared_grad_kernel(ffn_in_ref, pair_ref, act_ref, cot_ref, _after_ref, out_ref):
@@ -786,23 +828,22 @@
     deal, turned, send_cot = deal_out(rank, out_grad, hits_low)
     cot_rows = to_experts(tie(send_cot, line))
 
-    attn_in, q, kv, probs, attended, middle, ffn_in, gates, gains = forward(
-        hidden_in, doc_lengths, hits_low, pack
+    attn_in, q, kv, probs, attended, middle, ffn_in, gates, gains, send_rows = forward(
+        hidden_in, doc_lengths, hits_low, pack, deal
     )
-    send_rows = tie(dispatch(deal, ffn_in), gate_other, up_other, down_other)
+    send_rows = tie(send_rows, gate_other, up_other, down_other)
     rows = to_experts(send_rows)
 
     act_cot = act_cots(cot_rows, down, down_other, send_rows)
-    shared_low, pair_low, shared_sum, shared_cot = shared_phase(
-        ffn_in, out_grad, middle, second, act_cot
-    )
+    shared_low, pair_low = shared_phase(ffn_in, out_grad, second, act_cot)
 
     weights = (gate, gate_other, up, up_other)
     back, act, gate_cot, up_cot = expert_phase(
-        rows, cot_rows, act_cot, own, pack, weights, shared_cot
+        rows, cot_rows, act_cot, own, pack, weights, pair_low
     )
     shared_grad = shared_grads(ffn_in, pair_low, shared_low, out_grad, act)
-    kept = expert_grads(0, F32, rows, cot_rows, act, gate_cot, up_cot, shared_grad)
+    shared_sum, shared_cot = shared_end(shared_low, pair_low, middle, second, shared_grad)
+    kept = expert_grads(0, F32, rows, cot_rows, act, gate_cot, up_cot, shared_cot)
     shared_grad = scatter_plane(shared_grad)
     sent = expert_grads(1, BF, rows, cot_rows, act, gate_cot, up_cot, kept[0])
     result = expert_outs(act, down, down_other, sent[0])

time: 609 us -> 602 us (0.989)
  waiting for transfers between devices: 344 us -> 325 us
    all_to_all x4, waiting for transfers between devices: 112 us -> 94 us  [to_experts(): lax.all_to_all(rows.reshape(EXPERTS, SLOTS // 2, -1), DP, split_axis=0, c...]
    reduce_scatter x2, waiting for transfers between devices: 19.7 us -> 11.1 us  [scatter_plane(): return lax.psum_scatter(grads, PLANE, scatter_dimension=0, tiled=True)]
    reduce_scatter x2, starting transfers between devices: 0.29 us -> 8.83 us  [scatter_plane(): return lax.psum_scatter(grads, PLANE, scatter_dimension=0, tiled=True)]
  transfers between devices with their start and end apart: 20 -> 20, of which waited for: 14 -> 14; matrix products, arithmetic and copies ran while one was open for 2% -> 2% of each run, Pallas kernels for 20% -> 21%
where the time goes in v5:
time: 602 us; the launch traced here: 594 us
  waiting for transfers between devices  325 us (54%)
  Pallas kernels  144 us (24%)
  starting transfers between devices  73.3 us (12%)
  blocking collectives  15.4 us (3%)
  between operations  14.4 us (2%)
  other arithmetic  11.6 us (2%)
  local copies, waits for them, and re-layouts  9.56 us (2%)
    all_gather x2, waiting for transfers between devices, gather_plane(): lax.all_gather(pairs, PLANE, axis=1, tiled=True).reshape(64 * rows, width)  179 us
    all_to_all x4, waiting for transfers between devices, to_experts(): lax.all_to_all(rows.reshape(EXPERTS, SLOTS // 2, -1), DP, split_axis=0, c...  94 us
    all_to_all x4, starting transfers between devices, to_experts(): lax.all_to_all(rows.reshape(EXPERTS, SLOTS // 2, -1), DP, split_axis=0, c...  47.4 us
    ppermute x10, waiting for transfers between devices, swap(): return lax.ppermute(x, axis, [(0, 1), (1, 0)])  39.6 us
    pallas_call x2, Pallas kernels, expert_grads(): call(expert_grad_kernel, (8,), [pair, pair, tile(HALF, half), tile(HALF,...  26.4 us
    pallas_call x1, Pallas kernels, expert_phase(): call(expert_kernel, (8,), [pair(2 * WIDTH), pair(128, 24), tile(512), ful...  21.2 us
    pallas_call x1, Pallas kernels, backward(): call(backward_kernel, (1,), [ANY] * 13, [full(s) for s, _ in shapes], [ou...  15.6 us
    all_gather x1, blocking collectives, body(): lax.all_gather(jnp.concatenate(parts, axis=1), ('zh', 'zl'), axis=0, tile...  15.4 us
  transfers between devices with their start and end apart: 20, of which 14 were waited for; matrix products, arithmetic and copies ran while one was open for 2% of the time, Pallas kernels for 21%

profile of v5, /device:TPU:0, one launch (start us, length us, event | category | flops | bytes accessed | tf_op | source)
XLA Modules:
  0.0 593.6 jit_solution(8273966657133139012)
XLA Ops:
  10.5 15.4 %all-gather.1.refs_1_ = bf16[4,12,7296]{2,1,0:T(8,128)(2,1)S(1)} all-gather(bf16[1,12,7296]{2,1,0:T(8,128)(2,1)S(1)} %bitcast.39), channel_id=2, replica_groups=mesh['zh'=2,'x'=4,'y'=4,'c'=2,'zl'=2] {'zh','zl'}, dimensions={0}, use_global_device_ids=true | all-gather | bytes 875520 | tf_op jit(solution)/shard_map/all_gather | solution.py:812
  29.9 7.7 %shard_map.280 = (bf16[2,1024,256]{2,1,0:T(8,128)(2,1)}, bf16[2,256,1024]{2,1,0:T(8,128)(2,1)}, bf16[1024,3200]{1,0:T(8,128)(2,1)}) custom-call(f32[64,256]{1,0:T(8,128)} %slice_select_fusion.rank_ref, bf16[256,1536]{1,0:T(8,128)(2,1)} %refs_7_.1, bf16[256,128]{1,0:T(8,128)(2,1)} %convert.hits_ref), custom_call_target="tpu_custom_call" | custom-call | tf_op jit(solution)/shard_map/pallas_call | solution.py:144
  37.6 9.2 %all-to-all-start.1 = ((bf16[64,16,3200]{2,1,0:T(8,128)(2,1)}), bf16[64,16,3200]{2,1,0:T(8,128)(2,1)}, u32[]{:S(2)}, u32[]{:S(2)}) async-start(bf16[64,16,3200]{2,1,0:T(8,128)(2,1)} %bitcast.34), calls=%async_computation.1 | async-start | bytes 13107200 | tf_op jit(solution)/shard_map/all_to_all | solution.py:162
  46.8 3.0 collective-permute-start
  51.9 101.0 %all-gather.5.cloned.1.call-done = bf16[2,768,4224]{2,1,0:T(8,128)(2,1)} async-done(((bf16[2,24,4224]{2,1,0:T(8,128)(2,1)}), bf16[2,768,4224]{2,1,0:T(8,128)(2,1)}) %all-gather.5.cloned.1.call-update) | async-done | bytes 12976144 | tf_op jit(solution)/shard_map/all_gather | solution.py:93
  152.9 13.1 %shard_map.281 = (bf16[256,1536]{1,0:T(8,128)(2,1)}, bf16[256,1536]{1,0:T(8,128)(2,1)}, bf16[256,1024]{1,0:T(8,128)(2,1)}, f32[12,256,256]{2,1,0:T(8,128)}, bf16...) custom-call(bf16[256,1536]{1,0:T(8,128)(2,1)} %refs_11_.1, ...), custom_call_target="tpu_custom_call" | custom-call | tf_op jit(solution)/shard_map/pallas_call | solution.py:310
  166.0 5.5 collective-permute-done.2.refs_3_.other_ref
  172.4 11.2 %all-to-all-start = ((bf16[64,16,3072]{2,1,0:T(8,128)(2,1)}), bf16[64,16,3072]{2,1,0:T(8,128)(2,1)}, u32[]{:S(2)}, u32[]{:S(2)}) async-start(bf16[64,16,3072]{2,1,0:T(8,128)(2,1)} %bitcast.31), calls=%async_computation | async-start | bytes 12582912 | tf_op jit(solution)/shard_map/all_to_all | solution.py:162
  184.2 9.6 %shard_map.284._after_ref.act_cot_ref = f32[2048,512]{1,0:T(8,128)} custom-call(bf16[1024,3200]{1,0:T(8,128)(2,1)} %bitcast.11.cot_ref.marks_ref, bf16[256,1536]{1,0:T(8,128)(2,1)} %bitcast.36, bf16[256,1536]{1,0:T(8,128)(2,1)} %copy-done.1, bf16[1024,3072]{1,0:T(8,128)(2,1)} %shard_map.282._after_ref), custom_call_target="tpu_custom_call" | custom-call | tf_op jit(solution)/shard_map/pallas_call | solution.py:334
  193.8 77.8 %all-gather.7.cloned.1.call-done = bf16[2,768,3072]{2,1,0:T(8,128)(2,1)} async-done(((bf16[2,24,3072]{2,1,0:T(8,128)(2,1)}), bf16[2,768,3072]{2,1,0:T(8,128)(2,1)}) %all-gather.7.cloned.1.call-update) | async-done | bytes 9437200 | tf_op jit(solution)/shard_map/all_gather | solution.py:93
  271.6 9.0 %shard_map.285 = (bf16[256,1024]{1,0:T(8,128)(2,1)}, bf16[256,2048]{1,0:T(8,128)(2,1)}) custom-call(bf16[256,1536]{1,0:T(8,128)(2,1)} %get-tuple-element.53.ffn_in_ref, bf16[256,1536]{1,0:T(8,128)(2,1)} %refs_7_.1, bf16[1536,3072]{1,0:T(8,128)(2,1)} %bitcast.32, f32[2048,512]{1,0:T(8,128)} %shard_map.284._after_ref.act_cot_ref), custom_call_target="tpu_custom_call" | custom-call | tf_op jit(solution)/shard_map/pallas_call | solution.py:531
  280.6 21.2 %shard_map.286 = (bf16[1024,3200]{1,0:T(8,128)(2,1)}, bf16[2048,512]{1,0:T(8,128)(2,1)}, bf16[2048,512]{1,0:T(8,128)(2,1)}, bf16[2048,512]{1,0:T(8,128)(2,1)}) custom-call(bf16[1024,3072]{1,0:T(8,128)(2,1)} %bitcast.9.rows_ref, bf16[1024,3200]{1,0:T(8,128)(2,1)} %bitcast.11.cot_ref.marks_ref, f32[2048,512]{1,0:T(8,128)} %shard_map.284._after_ref.act_cot_ref, ...), custom_call_target="tpu_custom_call" | custom-call | tf_op jit(solution)/shard_map/pallas_call | solution.py:409
  301.8 12.1 %all-to-all-start.3 = ((bf16[64,16,3200]{2,1,0:T(8,128)(2,1)}), bf16[64,16,3200]{2,1,0:T(8,128)(2,1)}, u32[]{:S(2)}, u32[]{:S(2)}) async-start(bf16[64,16,3200]{2,1,0:T(8,128)(2,1)} %bitcast.35), calls=%async_computation.3 | async-start | bytes 13107200 | tf_op jit(solution)/shard_map/all_to_all | solution.py:162
  314.0 7.1 %shard_map.287._after_ref = bf16[768,6144]{1,0:T(8,128)(2,1)} custom-call(bf16[256,1536]{1,0:T(8,128)(2,1)} %get-tuple-element.53.ffn_in_ref, bf16[256,2048]{1,0:T(8,128)(2,1)} %get-tuple-element.54._after_ref.pair_ref.pair_cot_ref, bf16[256,1024]{1,0:T(8,128)(2,1)} %get-tuple-element.58.act_ref, bf16[256,1536]{1,0:T(8,128)(2,1)} %refs_7_.1, ...), custom_call_target="tpu_custom_call" | custom-call | tf_op jit(solution)/shard_map/pallas_call | solution.py:591
  321.1 9.4 %shard_map.288 = (f32[256,1536]{1,0:T(8,128)}, f32[256,1536]{1,0:T(8,128)}) custom-call(bf16[256,1024]{1,0:T(8,128)(2,1)} %get-tuple-element.58.act_ref, bf16[256,2048]{1,0:T(8,128)(2,1)} %get-tuple-element.54._after_ref.pair_ref.pair_cot_ref, f32[256,1536]{1,0:T(8,128)} %get-tuple-element.59.middle_ref.refs_5_, bf16[1536,3072]{1,0:T(8,128)(2,1)} %bitcast.33, ...), custom_call_target="tpu_custom_call" | custom-call | tf_op jit(solution)/shard_map/pallas_call | solution.py:568
  330.5 13.6 %shard_map.289 = (f32[1536,256]{1,0:T(8,128)}, f32[1536,256]{1,0:T(8,128)}, f32[256,1536]{1,0:T(8,128)}) custom-call(bf16[1024,3072]{1,0:T(8,128)(2,1)} %bitcast.9.rows_ref, bf16[1024,3200]{1,0:T(8,128)(2,1)} %bitcast.11.cot_ref.marks_ref, bf16[2048,512]{1,0:T(8,128)(2,1)} %get-tuple-element.55._after_ref.act_ref, ...), custom_call_target="tpu_custom_call" | custom-call | tf_op jit(solution)/shard_map/pallas_call | solution.py:468
  344.1 12.8 %shard_map.290 = (bf16[1536,256]{1,0:T(8,128)(2,1)}, bf16[1536,256]{1,0:T(8,128)(2,1)}, bf16[256,1536]{1,0:T(8,128)(2,1)}) custom-call(bf16[1024,3072]{1,0:T(8,128)(2,1)} %bitcast.9.rows_ref, bf16[1024,3200]{1,0:T(8,128)(2,1)} %bitcast.11.cot_ref.marks_ref, bf16[2048,512]{1,0:T(8,128)(2,1)} %get-tuple-element.55._after_ref.act_ref, ...), custom_call_target="tpu_custom_call" | custom-call | tf_op jit(solution)/shard_map/pallas_call | solution.py:468
  356.9 9.2 %shard_map.291.refs_12_ = bf16[1024,3072]{1,0:T(8,128)(2,1)} custom-call(bf16[2048,512]{1,0:T(8,128)(2,1)} %get-tuple-element.55._after_ref.act_ref, bf16[256,1536]{1,0:T(8,128)(2,1)} %bitcast.37, bf16[256,1536]{1,0:T(8,128)(2,1)} %copy-done.1, bf16[1536,256]{1,0:T(8,128)(2,1)} %get-tuple-element.62._after_ref.refs_0_), custom_call_target="tpu_custom_call" | custom-call | tf_op jit(solution)/shard_map/pallas_call | solution.py:427
  366.1 50.7 %all-to-all-done.3 = bf16[64,16,3200]{2,1,0:T(8,128)(2,1)} async-done(((bf16[64,16,3200]{2,1,0:T(8,128)(2,1)}), bf16[64,16,3200]{2,1,0:T(8,128)(2,1)}, u32[]{:S(2)}, u32[]{:S(2)}) %all-to-all-start.3) | async-done | bytes 6553632 | tf_op jit(solution)/shard_map/all_to_all | solution.py:162
  416.8 14.9 %all-to-all-start.2 = ((bf16[64,16,3072]{2,1,0:T(8,128)(2,1)}), bf16[64,16,3072]{2,1,0:T(8,128)(2,1)}, u32[]{:S(2)}, u32[]{:S(2)}) async-start(bf16[64,16,3072]{2,1,0:T(8,128)(2,1)} %bitcast.30), calls=%async_computation.2 | async-start | bytes 12582912 | tf_op jit(solution)/shard_map/all_to_all | solution.py:162
  431.7 8.8 %reduce-scatter.3.cloned.1.call-start = ((), (), s32[]{:S(2)}) async-start(), calls=%async_computation.8 | async-start | bytes 13381632 | tf_op jit(solution)/shard_map/reduce_scatter | solution.py:97
  440.5 15.6 %shard_map.293 = (bf16[256,1536]{1,0:T(8,128)(2,1)}, bf16[256,1536]{1,0:T(8,128)(2,1)}, bf16[256,1024]{1,0:T(8,128)(2,1)}, f32[256,1536]{1,0:T(8,128)}, bf16[256...) custom-call(bf16[1024,3200]{1,0:T(8,128)(2,1)} %bitcast.16.refs_0_, ...), custom_call_target="tpu_custom_call" | custom-call | tf_op jit(solution)/shard_map/pallas_call | solution.py:722
  456.1 9.1 %shard_map.294.refs_1_ = bf16[768,8448]{1,0:T(8,128)(2,1)} custom-call(bf16[256,1536]{1,0:T(8,128)(2,1)} %get-tuple-element.71.attn_in_ref, bf16[256,1536]{1,0:T(8,128)(2,1)} %get-tuple-element.72.attended_ref, bf16[256,1536]{1,0:T(8,128)(2,1)} %get-tuple-element.53.ffn_in_ref, bf16[256,1536]{1,0:T(8,128)(2,1)} %get-tuple-element.73.gain_one_ref, ...), custom_call_target="tpu_custom_call" | custom-call | flops 9999999827968 | tf_op jit(solution)/shard_map/pallas_call | solution.py:780
  467.4 43.3 %all-to-all-done.2 = bf16[64,16,3072]{2,1,0:T(8,128)(2,1)} async-done(((bf16[64,16,3072]{2,1,0:T(8,128)(2,1)}), bf16[64,16,3072]{2,1,0:T(8,128)(2,1)}, u32[]{:S(2)}, u32[]{:S(2)}) %all-to-all-start.2) | async-done | bytes 6291488 | tf_op jit(solution)/shard_map/all_to_all | solution.py:162
  510.7 6.4 %shard_map.292 = bf16[256,1536]{1,0:T(8,128)(2,1)} custom-call(bf16[2,256,1024]{2,1,0:T(8,128)(2,1)} %get-tuple-element.49.turned_ref.refs_2_, bf16[1024,3072]{1,0:T(8,128)(2,1)} %bitcast.14.rows_ref, f32[256,1536]{1,0:T(8,128)} %get-tuple-element.63.base_ref), custom_call_target="tpu_custom_call" | custom-call | flops 9999999827968 | tf_op jit(solution)/shard_map/pallas_call | solution.py:182
  517.3 4.4 collective-permute-done.9
  524.2 14.4 %collective-permute-done.10 = bf16[1536,256]{1,0:T(8,128)(2,1)} collective-permute-done((bf16[1536,256]{1,0:T(8,128)(2,1)}, bf16[1536,256]{1,0:T(8,128)(2,1)}, u32[]{:S(2)}, u32[]{:S(2)}) %collective-permute-start.10) | collective-permute-done | bytes 786464 | tf_op jit(solution)/shard_map/ppermute | solution.py:46
  542.7 3.5 collective-permute-start.7
  547.5 7.9 %collective-permute-done.11 = bf16[256,1536]{1,0:T(8,128)(2,1)S(1)} collective-permute-done((bf16[256,1536]{1,0:T(8,128)(2,1)}, bf16[256,1536]{1,0:T(8,128)(2,1)S(1)}, u32[]{:S(2)}, u32[]{:S(2)}) %collective-permute-start.11) | collective-permute-done | bytes 786464 | tf_op jit(solution)/shard_map/ppermute | solution.py:46
  560.4 11.1 %reduce-scatter.3.cloned.1.call-done = bf16[24,8448]{1,0:T(8,128)(2,1)} async-done(((bf16[768,8448]{1,0:T(8,128)(2,1)}), bf16[24,8448]{1,0:T(8,128)(2,1)}) %reduce-scatter.3.cloned.1.call-update) | async-done | bytes 405520 | tf_op jit(solution)/shard_map/reduce_scatter | solution.py:97
  574.3 2.9 collective-permute-start.4
  579.1 3.4 collective-permute-done.4
  (101 shorter events, 34.8 us)
Async XLA Ops:
  7.2 145.7 %all-gather.5.cloned.1.call-start = ((), (), s32[]{:S(2)}) async-start(), calls=%async_computation.6 | async-start | bytes 13381632 | tf_op jit(solution)/shard_map/all_gather | solution.py:93
  25.9 2.0 copy-start
  25.9 2.0 copy-start.8
  27.0 244.6 %all-gather.7.cloned.1.call-start = ((), (), s32[]{:S(2)}) async-start(), calls=%async_computation.7 | async-start | bytes 9732096 | tf_op jit(solution)/shard_map/all_gather | solution.py:93
  37.6 12.3 %copy-start.3 = (bf16[1,256,1536]{2,1,0:T(8,128)(2,1)S(1)}, bf16[1,256,1536]{2,1,0:T(8,128)(2,1)}, u32[]{:S(2)}) copy-start(bf16[1,256,1536]{2,1,0:T(8,128)(2,1)} %param.33) | copy-start | bytes 2359300
  37.6 134.8 %all-to-all-start.1 = ((bf16[64,16,3200]{2,1,0:T(8,128)(2,1)}), bf16[64,16,3200]{2,1,0:T(8,128)(2,1)}, u32[]{:S(2)}, u32[]{:S(2)}) async-start(bf16[64,16,3200]{2,1,0:T(8,128)(2,1)} %bitcast.34), calls=%async_computation.1 | async-start | bytes 13107200 | tf_op jit(solution)/shard_map/all_to_all | solution.py:162
  46.8 119.1 %collective-permute-start = (bf16[1536,256]{1,0:T(8,128)(2,1)}, bf16[1536,256]{1,0:T(8,128)(2,1)S(1)}, u32[]{:S(2)}, u32[]{:S(2)}) collective-permute-start(bf16[1536,256]{1,0:T(8,128)(2,1)} %bitcast.5.gate_ref), channel_id=1, source_target_pairs={{0,1},{1,0},{2,3},{3,2},{4,5},{5,4},{6,7},{7,6},{8,9},{9,8},{10,11... | collective-permute-start | bytes 2359304 | tf_op jit(solution)/shard_map/ppermute | solution.py:46
  49.8 116.2 %collective-permute-start.1 = (bf16[1536,256]{1,0:T(8,128)(2,1)}, bf16[1536,256]{1,0:T(8,128)(2,1)S(1)}, u32[]{:S(2)}, u32[]{:S(2)}) collective-permute-start(bf16[1536,256]{1,0:T(8,128)(2,1)} %bitcast.6.up_ref), channel_id=1, source_target_pairs={{0,1},{1,0},{2,3},{3,2},{4,5},{5,4},{6,7},{7,6},{8,9},{9,8},{10,11... | collective-permute-start | bytes 2359304 | tf_op jit(solution)/shard_map/ppermute | solution.py:46
  49.9 121.6 %collective-permute-start.2 = (bf16[256,1536]{1,0:T(8,128)(2,1)S(1)}, bf16[256,1536]{1,0:T(8,128)(2,1)S(1)}, u32[]{:S(2)}, u32[]{:S(2)}) collective-permute-start(bf16[256,1536]{1,0:T(8,128)(2,1)S(1)} %bitcast.38), channel_id=1, source_target_pairs={{0,1},{1,0},{2,3},{3,2},{4,5},{5,4},{6,7},{7,6},{8,9},{9,8},{10,11... | collective-permute-start | bytes 2359304 | tf_op jit(solution)/shard_map/ppermute | solution.py:46
  166.0 5.5 copy-start.4
  166.0 5.5 copy-start.5
  171.5 0.9 copy-start.1
  172.4 108.1 %all-to-all-start = ((bf16[64,16,3072]{2,1,0:T(8,128)(2,1)}), bf16[64,16,3072]{2,1,0:T(8,128)(2,1)}, u32[]{:S(2)}, u32[]{:S(2)}) async-start(bf16[64,16,3072]{2,1,0:T(8,128)(2,1)} %bitcast.31), calls=%async_computation | async-start | bytes 12582912 | tf_op jit(solution)/shard_map/all_to_all | solution.py:162
  301.8 115.0 %all-to-all-start.3 = ((bf16[64,16,3200]{2,1,0:T(8,128)(2,1)}), bf16[64,16,3200]{2,1,0:T(8,128)(2,1)}, u32[]{:S(2)}, u32[]{:S(2)}) async-start(bf16[64,16,3200]{2,1,0:T(8,128)(2,1)} %bitcast.35), calls=%async_computation.3 | async-start | bytes 13107200 | tf_op jit(solution)/shard_map/all_to_all | solution.py:162
  313.9 227.1 %reduce-scatter.5.cloned.1.call-start = ((), (), s32[]{:S(2)}) async-start(), calls=%async_computation.9 | async-start | bytes 9732096 | tf_op jit(solution)/shard_map/reduce_scatter | solution.py:97
  416.8 93.9 %all-to-all-start.2 = ((bf16[64,16,3072]{2,1,0:T(8,128)(2,1)}), bf16[64,16,3072]{2,1,0:T(8,128)(2,1)}, u32[]{:S(2)}, u32[]{:S(2)}) async-start(bf16[64,16,3072]{2,1,0:T(8,128)(2,1)} %bitcast.30), calls=%async_computation.2 | async-start | bytes 12582912 | tf_op jit(solution)/shard_map/all_to_all | solution.py:162
  431.7 139.8 %reduce-scatter.3.cloned.1.call-start = ((), (), s32[]{:S(2)}) async-start(), calls=%async_computation.8 | async-start | bytes 13381632 | tf_op jit(solution)/shard_map/reduce_scatter | solution.py:97
  465.3 56.5 %collective-permute-start.9 = (bf16[1536,256]{1,0:T(8,128)(2,1)}, bf16[1536,256]{1,0:T(8,128)(2,1)}, u32[]{:S(2)}, u32[]{:S(2)}) collective-permute-start(bf16[1536,256]{1,0:T(8,128)(2,1)} %shard_map.295), channel_id=1, source_target_pairs={{0,1},{1,0},{2,3},{3,2},{4,5},{5,4},{6,7},{7,6},{8,9},{9,8},{10,11... | collective-permute-start | bytes 2359304 | tf_op jit(solution)/shard_map/ppermute | solution.py:46
  465.8 72.8 %collective-permute-start.10 = (bf16[1536,256]{1,0:T(8,128)(2,1)}, bf16[1536,256]{1,0:T(8,128)(2,1)}, u32[]{:S(2)}, u32[]{:S(2)}) collective-permute-start(bf16[1536,256]{1,0:T(8,128)(2,1)} %shard_map.296), channel_id=1, source_target_pairs={{0,1},{1,0},{2,3},{3,2},{4,5},{5,4},{6,7},{7,6},{8,9},{9,8},{10,11... | collective-permute-start | bytes 2359304 | tf_op jit(solution)/shard_map/ppermute | solution.py:46
  517.1 4.6 copy-start.2
  517.1 21.5 %copy-start.7 = (f32[1536,256]{1,0:T(8,128)S(1)}, f32[1536,256]{1,0:T(8,128)}, u32[]{:S(2)}) copy-start(f32[1536,256]{1,0:T(8,128)} %get-tuple-element.79) | copy-start | bytes 4718596
  517.1 38.2 %collective-permute-start.11 = (bf16[256,1536]{1,0:T(8,128)(2,1)}, bf16[256,1536]{1,0:T(8,128)(2,1)S(1)}, u32[]{:S(2)}, u32[]{:S(2)}) collective-permute-start(bf16[256,1536]{1,0:T(8,128)(2,1)} %shard_map.297), channel_id=1, source_target_pairs={{0,1},{1,0},{2,3},{3,2},{4,5},{5,4},{6,7},{7,6},{8,9},{9,8},{10,11... | collective-permute-start | bytes 2359304 | tf_op jit(solution)/shard_map/ppermute | solution.py:46
  541.1 14.3 %copy-start.6 = (f32[256,1536]{1,0:T(8,128)S(1)}, f32[256,1536]{1,0:T(8,128)}, u32[]{:S(2)}) copy-start(f32[256,1536]{1,0:T(8,128)} %get-tuple-element.81) | copy-start | bytes 4718596
  542.5 14.9 %collective-permute-start.6 = (bf16[12,3072]{1,0:T(8,128)(2,1)S(1)}, bf16[12,3072]{1,0:T(8,128)(2,1)S(1)}, u32[]{:S(2)}, u32[]{:S(2)}) collective-permute-start(bf16[12,3072]{1,0:T(8,128)(2,1)S(1)} %broadcast_select_fusion.9), channel_id=1, source_target_pairs={{0,1},{1,0},{2,3},{3,2},{4,5},{5,4},{6,7},{7,6},{8,9},{9,8},{10,11... | collective-permute-start | bytes 221192 | tf_op jit(solution)/shard_map/ppermute | solution.py:46
  542.7 17.6 %collective-permute-start.7 = (bf16[12,3072]{1,0:T(8,128)(2,1)S(1)}, bf16[12,3072]{1,0:T(8,128)(2,1)S(1)}, u32[]{:S(2)}, u32[]{:S(2)}) collective-permute-start(bf16[12,3072]{1,0:T(8,128)(2,1)S(1)} %get-tuple-element.98), channel_id=1, source_target_pairs={{0,64},{64,0},{1,65},{65,1},{2,66},{66,2},{3,67},{67,3},{4,68},{68... | collective-permute-start | bytes 221192 | tf_op jit(solution)/shard_map/ppermute | solution.py:46
  546.2 14.2 %collective-permute-start.8 = (bf16[12,3072]{1,0:T(8,128)(2,1)S(1)}, bf16[12,3072]{1,0:T(8,128)(2,1)S(1)}, u32[]{:S(2)}, u32[]{:S(2)}) collective-permute-start(bf16[12,3072]{1,0:T(8,128)(2,1)S(1)} %get-tuple-element.99), channel_id=1, source_target_pairs={{0,65},{1,64},{64,1},{65,0},{2,67},{3,66},{66,3},{67,2},{4,69},{5,... | collective-permute-start | bytes 221192 | tf_op jit(solution)/shard_map/ppermute | solution.py:113
  572.7 6.4 %collective-permute-start.3 = (bf16[12,4224]{1,0:T(8,128)(2,1)S(1)}, bf16[12,4224]{1,0:T(8,128)(2,1)S(1)}, u32[]{:S(2)}, u32[]{:S(2)}) collective-permute-start(bf16[12,4224]{1,0:T(8,128)(2,1)S(1)} %broadcast_select_fusion.6), channel_id=1, source_target_pairs={{0,1},{1,0},{2,3},{3,2},{4,5},{5,4},{6,7},{7,6},{8,9},{9,8},{10,11... | collective-permute-start | bytes 304136 | tf_op jit(solution)/shard_map/ppermute | solution.py:46
  574.3 8.2 %collective-permute-start.4 = (bf16[12,4224]{1,0:T(8,128)(2,1)S(1)}, bf16[12,4224]{1,0:T(8,128)(2,1)S(1)}, u32[]{:S(2)}, u32[]{:S(2)}) collective-permute-start(bf16[12,4224]{1,0:T(8,128)(2,1)S(1)} %get-tuple-element.93), channel_id=1, source_target_pairs={{0,64},{64,0},{1,65},{65,1},{2,66},{66,2},{3,67},{67,3},{4,68},{68... | collective-permute-start | bytes 304136 | tf_op jit(solution)/shard_map/ppermute | solution.py:46
  577.2 6.9 %collective-permute-start.5 = (bf16[12,4224]{1,0:T(8,128)(2,1)S(1)}, bf16[12,4224]{1,0:T(8,128)(2,1)S(1)}, u32[]{:S(2)}, u32[]{:S(2)}) collective-permute-start(bf16[12,4224]{1,0:T(8,128)(2,1)S(1)} %get-tuple-element.94), channel_id=1, source_target_pairs={{0,65},{1,64},{64,1},{65,0},{2,67},{3,66},{66,3},{67,2},{4,69},{5,... | collective-permute-start | bytes 304136 | tf_op jit(solution)/shard_map/ppermute | solution.py:113
Sparse Core Ops, SparseCore 0:
  27.1 125.7 all-gather.4
  155.7 115.8 all-gather.6
  321.2 119.9 reduce-scatter.4
  465.4 106.0 reduce-scatter.2

commit v6 on v5

--- a/solution.py
+++ b/solution.py
@@ -610,10 +610,11 @@
 
 
 def backward_kernel(*refs):
-    n_in, n_out = 13, 8
+    n_in, n_out = 13, 7
     sources, outs, scratch = refs[:n_in], refs[n_in : n_in + n_out], refs[n_in + n_out :]
     back_hbm, pack_hbm = sources[:2]
-    middle_low_ref, dq_ref, dkv_ref, grad_in_ref, logit_ref, one_ref, two_ref, cot_ref = outs
+    results, scratch = scratch[:8], scratch[8:]
+    middle_low_ref, dq_ref, dkv_ref, grad_in_ref, logit_ref, one_ref, two_ref, cot_ref = results
     back_ref, wo_ref, wq_ref, wkv_ref, small_ref, acc, sems = scratch[:7]
     held = scratch[7:]
     loads = [(back_hbm.at[:512], back_ref.at[:512]), (back_hbm.at[512:], back_ref.at[512:])]
@@ -631,6 +632,12 @@
     out_grad_ref, q_ref, kv_ref, probs_ref, hidden_ref = held[5:]
     loads = [loads[2], loads[0], loads[1]] + loads[3:]
     copies = [fetch(a, b, sems.at[i]) for i, (a, b) in enumerate(loads)]
+    sent = []
+
+    def send(*which):
+        for i in which:
+            sent.append(fetch(results[i], outs[i], sems.at[16 + i]))
+
     for i in (0, 1):
         copies[i].wait()
     lane = lax.broadcasted_iota(jnp.int32, (512, 128), 1)
@@ -662,6 +669,7 @@
     total = out_grad_ref[...].astype(F32) + norm_back(middle, scale, gains_ref[1:2], cot)
     grad_in_ref[...] = total
     middle_low_ref[...] = total.astype(BF)
+    send(0, 4, 6)
     for j in range(0, WIDTH, 512):
         at = slice(j, j + 512)
         cot_ref[:, at] = mm_r(middle_low_ref[...], wo_ref[at, :]).astype(BF)
@@ -685,6 +693,7 @@
             dk += mm_l(dscores, q_ref[:, at])
         dkv_ref[:, key_at] = (dk * SCALING).astype(BF)
         dkv_ref[:, value_at] = dv.astype(BF)
+    send(1, 2)
     for i in range(14, 16):
         copies[i].wait()
     for j in range(0, WIDTH, 512):
@@ -694,7 +703,11 @@
     scale = root_scale(tokens)
     cot = acc[...]
     one_ref[...] = (cot * tokens * scale).astype(BF)
+    send(5)
     grad_in_ref[...] += norm_back(tokens, scale, gains_ref[0:1], cot)
+    send(3)
+    for copy in sent:
+        copy.wait()
 
 
 def backward(back, pack, turned, shared_cot, gates, middle, gains, out_grad, q, kv, probs, hidden, after):
@@ -717,32 +730,39 @@
         pltpu.VMEM((WIDTH, 1024), BF),
         pltpu.VMEM((WIDTH, 128), BF),
         pltpu.VMEM((TOKENS, WIDTH), F32),
-        pltpu.SemaphoreType.DMA((16,)),
+        pltpu.SemaphoreType.DMA((23,)),
     ] + [pltpu.VMEM(a.shape, a.dtype) for a in held]
+    scratch = [pltpu.VMEM(s, d) for s, d in shapes] + scratch
     return call(
         backward_kernel,
         (1,),
         [ANY] * 13,
-        [full(s) for s, _ in shapes],
-        [out(s, d) for s, d in shapes],
+        [ANY] * 7,
+        [out(s, d) for s, d in shapes[:7]],
         scratch,
     )(back, pack, *held, after)
 
 
-def dense_grad_kernel(
-    attn_in_ref,
-    attended_ref,
-    ffn_in_ref,
-    gain_one_ref,
-    gain_two_ref,
-    dq_ref,
-    middle_ref,
-    dkv_ref,
-    logit_ref,
-    out_ref,
-    held,
-    sems,
-):
+def dense_grad_kernel(*refs):
+    out_ref, held, sems = refs[9], refs[10], refs[20]
+    (
+        attn_in_ref,
+        attended_ref,
+        ffn_in_ref,
+        gain_one_ref,
+        gain_two_ref,
+        dq_ref,
+        middle_ref,
+        dkv_ref,
+        logit_ref,
+    ) = refs[11:20]
+    loads = {i: fetch(refs[i], refs[11 + i], sems.at[6 + i]) for i in (1, 6, 0, 5, 7, 2, 8, 3, 4)}
+
+    def need(*which):
+        for i in which:
+            if i in loads:
+                loads.pop(i).wait()
+
     copies = []
 
     def send(at, width):
@@ -752,20 +772,24 @@
     for half in range(2):
         rows = slice(half * 768, (half + 1) * 768)
         base = half * PACK
+        need(1, 6)
         attended = attended_ref[:, rows]
         for j in range(0, WIDTH, 512):
             at = base + WIDTH + j
             held[:, at : at + 512] = mm_l(attended, middle_ref[:, j : j + 512]).astype(BF)
         send(base + WIDTH, WIDTH)
+        need(0, 5)
         attn_in = attn_in_ref[:, rows]
         for j in range(0, WIDTH, 512):
             at = base + j
             held[:, at : at + 512] = mm_l(attn_in, dq_ref[:, j : j + 512]).astype(BF)
         send(base, WIDTH)
+        need(7)
         for j in range(0, 1024, 512):
             at = base + 2 * WIDTH + j
             held[:, at : at + 512] = mm_l(attn_in, dkv_ref[:, j : j + 512]).astype(BF)
         lane = lax.broadcasted_iota(jnp.int32, (TOKENS, 128), 1)
+        need(2, 8, 3, 4)
         small = mm_l(ffn_in_ref[:, rows], logit_ref[...])
         small += mm_l(gain_one_ref[:, rows], jnp.where(lane == 64, 1.0, 0.0).astype(BF))
         small += mm_l(gain_two_ref[:, rows], jnp.where(lane == 65, 1.0, 0.0).astype(BF))
@@ -780,10 +804,12 @@
     return call(
         dense_grad_kernel,
         (1,),
-        [full(a.shape) for a in ins],
+        [ANY] * 9,
         ANY,
         out((768, 2 * PACK), BF),
-        [pltpu.VMEM((768, 2 * PACK), BF), pltpu.SemaphoreType.DMA((6,))],
+        [pltpu.VMEM((768, 2 * PACK), BF)]
+        + [pltpu.VMEM(a.shape, a.dtype) for a in ins]
+        + [pltpu.SemaphoreType.DMA((15,))],
         flops=10**13,
     )(*ins)
 
@@ -849,7 +875,7 @@
     result = expert_outs(act, down, down_other, sent[0])
     back = to_experts(back)
 
-    middle_low, dq, dkv, grad_in, logit, one_rows, two_rows, _ = backward(
+    middle_low, dq, dkv, grad_in, logit, one_rows, two_rows = backward(
         back, pack, turned, shared_cot, gates, middle, gains, out_grad, q, kv, probs, hidden_in, result
     )
     result = to_experts(result)

time: 602 us -> 601 us (level)
  no operation moved by 1% of the time
where the time goes in v6:
time: 601 us; the launch traced here: 592 us
  waiting for transfers between devices  325 us (54%)
  Pallas kernels  143 us (24%)
  starting transfers between devices  73.3 us (12%)
  blocking collectives  15.4 us (3%)
  between operations  14.4 us (2%)
  other arithmetic  11.6 us (2%)
  local copies, waits for them, and re-layouts  9.56 us (2%)
    all_gather x2, waiting for transfers between devices, gather_plane(): lax.all_gather(pairs, PLANE, axis=1, tiled=True).reshape(64 * rows, width)  179 us
    all_to_all x4, waiting for transfers between devices, to_experts(): lax.all_to_all(rows.reshape(EXPERTS, SLOTS // 2, -1), DP, split_axis=0, c...  95.2 us
    all_to_all x4, starting transfers between devices, to_experts(): lax.all_to_all(rows.reshape(EXPERTS, SLOTS // 2, -1), DP, split_axis=0, c...  47.4 us
    ppermute x10, waiting for transfers between devices, swap(): return lax.ppermute(x, axis, [(0, 1), (1, 0)])  39.2 us
    pallas_call x2, Pallas kernels, expert_grads(): call(expert_grad_kernel, (8,), [pair, pair, tile(HALF, half), tile(HALF,...  26.4 us
    pallas_call x1, Pallas kernels, expert_phase(): call(expert_kernel, (8,), [pair(2 * WIDTH), pair(128, 24), tile(512), ful...  21.2 us
    ppermute x10, starting transfers between devices, swap(): return lax.ppermute(x, axis, [(0, 1), (1, 0)])  15.5 us
    all_gather x1, blocking collectives, body(): lax.all_gather(jnp.concatenate(parts, axis=1), ('zh', 'zl'), axis=0, tile...  15.4 us
  transfers between devices with their start and end apart: 20, of which 14 were waited for; matrix products, arithmetic and copies ran while one was open for 2% of the time, Pallas kernels for 21%

profile of v6, /device:TPU:0, one launch (start us, length us, event | category | flops | bytes accessed | tf_op | source)
XLA Modules:
  0.0 592.0 jit_solution(16898380924424214588)
XLA Ops:
  10.5 15.4 %all-gather.1.refs_1_ = bf16[4,12,7296]{2,1,0:T(8,128)(2,1)S(1)} all-gather(bf16[1,12,7296]{2,1,0:T(8,128)(2,1)S(1)} %bitcast.39), channel_id=2, replica_groups=mesh['zh'=2,'x'=4,'y'=4,'c'=2,'zl'=2] {'zh','zl'}, dimensions={0}, use_global_device_ids=true | all-gather | bytes 875520 | tf_op jit(solution)/shard_map/all_gather | solution.py:838
  29.9 7.7 %shard_map.280 = (bf16[2,1024,256]{2,1,0:T(8,128)(2,1)}, bf16[2,256,1024]{2,1,0:T(8,128)(2,1)}, bf16[1024,3200]{1,0:T(8,128)(2,1)}) custom-call(f32[64,256]{1,0:T(8,128)} %slice_select_fusion.rank_ref, bf16[256,1536]{1,0:T(8,128)(2,1)} %refs_7_.1, bf16[256,128]{1,0:T(8,128)(2,1)} %convert.hits_ref), custom_call_target="tpu_custom_call" | custom-call | tf_op jit(solution)/shard_map/pallas_call | solution.py:144
  37.6 9.2 %all-to-all-start.1 = ((bf16[64,16,3200]{2,1,0:T(8,128)(2,1)}), bf16[64,16,3200]{2,1,0:T(8,128)(2,1)}, u32[]{:S(2)}, u32[]{:S(2)}) async-start(bf16[64,16,3200]{2,1,0:T(8,128)(2,1)} %bitcast.34), calls=%async_computation.1 | async-start | bytes 13107200 | tf_op jit(solution)/shard_map/all_to_all | solution.py:162
  46.8 3.0 collective-permute-start
  51.9 101.0 %all-gather.5.cloned.1.call-done = bf16[2,768,4224]{2,1,0:T(8,128)(2,1)} async-done(((bf16[2,24,4224]{2,1,0:T(8,128)(2,1)}), bf16[2,768,4224]{2,1,0:T(8,128)(2,1)}) %all-gather.5.cloned.1.call-update) | async-done | bytes 12976144 | tf_op jit(solution)/shard_map/all_gather | solution.py:93
  152.9 13.1 %shard_map.281 = (bf16[256,1536]{1,0:T(8,128)(2,1)}, bf16[256,1536]{1,0:T(8,128)(2,1)}, bf16[256,1024]{1,0:T(8,128)(2,1)}, f32[12,256,256]{2,1,0:T(8,128)}, bf16...) custom-call(bf16[256,1536]{1,0:T(8,128)(2,1)} %refs_11_.1, ...), custom_call_target="tpu_custom_call" | custom-call | tf_op jit(solution)/shard_map/pallas_call | solution.py:310
  166.0 5.5 collective-permute-done.2.refs_3_.other_ref
  172.4 11.2 %all-to-all-start = ((bf16[64,16,3072]{2,1,0:T(8,128)(2,1)}), bf16[64,16,3072]{2,1,0:T(8,128)(2,1)}, u32[]{:S(2)}, u32[]{:S(2)}) async-start(bf16[64,16,3072]{2,1,0:T(8,128)(2,1)} %bitcast.31), calls=%async_computation | async-start | bytes 12582912 | tf_op jit(solution)/shard_map/all_to_all | solution.py:162
  184.2 9.6 %shard_map.284._after_ref.act_cot_ref = f32[2048,512]{1,0:T(8,128)} custom-call(bf16[1024,3200]{1,0:T(8,128)(2,1)} %bitcast.11.cot_ref.marks_ref, bf16[256,1536]{1,0:T(8,128)(2,1)} %bitcast.36, bf16[256,1536]{1,0:T(8,128)(2,1)} %copy-done.1, bf16[1024,3072]{1,0:T(8,128)(2,1)} %shard_map.282._after_ref), custom_call_target="tpu_custom_call" | custom-call | tf_op jit(solution)/shard_map/pallas_call | solution.py:334
  193.8 77.8 %all-gather.7.cloned.1.call-done = bf16[2,768,3072]{2,1,0:T(8,128)(2,1)} async-done(((bf16[2,24,3072]{2,1,0:T(8,128)(2,1)}), bf16[2,768,3072]{2,1,0:T(8,128)(2,1)}) %all-gather.7.cloned.1.call-update) | async-done | bytes 9437200 | tf_op jit(solution)/shard_map/all_gather | solution.py:93
  271.6 9.0 %shard_map.285 = (bf16[256,1024]{1,0:T(8,128)(2,1)}, bf16[256,2048]{1,0:T(8,128)(2,1)}) custom-call(bf16[256,1536]{1,0:T(8,128)(2,1)} %get-tuple-element.53.ffn_in_ref.refs_2_, bf16[256,1536]{1,0:T(8,128)(2,1)} %refs_7_.1, bf16[1536,3072]{1,0:T(8,128)(2,1)} %bitcast.32, f32[2048,512]{1,0:T(8,128)} %shard_map.284._after_ref.act_cot_ref), custom_call_target="tpu_custom_call" | custom-call | tf_op jit(solution)/shard_map/pallas_call | solution.py:531
  280.6 21.2 %shard_map.286 = (bf16[1024,3200]{1,0:T(8,128)(2,1)}, bf16[2048,512]{1,0:T(8,128)(2,1)}, bf16[2048,512]{1,0:T(8,128)(2,1)}, bf16[2048,512]{1,0:T(8,128)(2,1)}) custom-call(bf16[1024,3072]{1,0:T(8,128)(2,1)} %bitcast.9.rows_ref, bf16[1024,3200]{1,0:T(8,128)(2,1)} %bitcast.11.cot_ref.marks_ref, f32[2048,512]{1,0:T(8,128)} %shard_map.284._after_ref.act_cot_ref, ...), custom_call_target="tpu_custom_call" | custom-call | tf_op jit(solution)/shard_map/pallas_call | solution.py:409
  301.8 12.1 %all-to-all-start.3 = ((bf16[64,16,3200]{2,1,0:T(8,128)(2,1)}), bf16[64,16,3200]{2,1,0:T(8,128)(2,1)}, u32[]{:S(2)}, u32[]{:S(2)}) async-start(bf16[64,16,3200]{2,1,0:T(8,128)(2,1)} %bitcast.35), calls=%async_computation.3 | async-start | bytes 13107200 | tf_op jit(solution)/shard_map/all_to_all | solution.py:162
  314.0 7.1 %shard_map.287._after_ref = bf16[768,6144]{1,0:T(8,128)(2,1)} custom-call(bf16[256,1536]{1,0:T(8,128)(2,1)} %get-tuple-element.53.ffn_in_ref.refs_2_, bf16[256,2048]{1,0:T(8,128)(2,1)} %get-tuple-element.54._after_ref.pair_ref.pair_cot_ref, bf16[256,1024]{1,0:T(8,128)(2,1)} %get-tuple-element.58.act_ref, bf16[256,1536]{1,0:T(8,128)(2,1)} %refs_7_.1, ...), custom_call_target="tpu_custom_call" | custom-call | tf_op jit(solution)/shard_map/pallas_call | solution.py:591
  321.1 9.4 %shard_map.288 = (f32[256,1536]{1,0:T(8,128)}, f32[256,1536]{1,0:T(8,128)}) custom-call(bf16[256,1024]{1,0:T(8,128)(2,1)} %get-tuple-element.58.act_ref, bf16[256,2048]{1,0:T(8,128)(2,1)} %get-tuple-element.54._after_ref.pair_ref.pair_cot_ref, f32[256,1536]{1,0:T(8,128)} %get-tuple-element.59.middle_ref.refs_5_, bf16[1536,3072]{1,0:T(8,128)(2,1)} %bitcast.33, ...), custom_call_target="tpu_custom_call" | custom-call | tf_op jit(solution)/shard_map/pallas_call | solution.py:568
  330.5 13.6 %shard_map.289 = (f32[1536,256]{1,0:T(8,128)}, f32[1536,256]{1,0:T(8,128)}, f32[256,1536]{1,0:T(8,128)}) custom-call(bf16[1024,3072]{1,0:T(8,128)(2,1)} %bitcast.9.rows_ref, bf16[1024,3200]{1,0:T(8,128)(2,1)} %bitcast.11.cot_ref.marks_ref, bf16[2048,512]{1,0:T(8,128)(2,1)} %get-tuple-element.55._after_ref.act_ref, ...), custom_call_target="tpu_custom_call" | custom-call | tf_op jit(solution)/shard_map/pallas_call | solution.py:468
  344.1 12.8 %shard_map.290 = (bf16[1536,256]{1,0:T(8,128)(2,1)}, bf16[1536,256]{1,0:T(8,128)(2,1)}, bf16[256,1536]{1,0:T(8,128)(2,1)}) custom-call(bf16[1024,3072]{1,0:T(8,128)(2,1)} %bitcast.9.rows_ref, bf16[1024,3200]{1,0:T(8,128)(2,1)} %bitcast.11.cot_ref.marks_ref, bf16[2048,512]{1,0:T(8,128)(2,1)} %get-tuple-element.55._after_ref.act_ref, ...), custom_call_target="tpu_custom_call" | custom-call | tf_op jit(solution)/shard_map/pallas_call | solution.py:468
  356.9 9.2 %shard_map.291.refs_12_ = bf16[1024,3072]{1,0:T(8,128)(2,1)} custom-call(bf16[2048,512]{1,0:T(8,128)(2,1)} %get-tuple-element.55._after_ref.act_ref, bf16[256,1536]{1,0:T(8,128)(2,1)} %bitcast.37, bf16[256,1536]{1,0:T(8,128)(2,1)} %copy-done.1, bf16[1536,256]{1,0:T(8,128)(2,1)} %get-tuple-element.62._after_ref.refs_0_), custom_call_target="tpu_custom_call" | custom-call | tf_op jit(solution)/shard_map/pallas_call | solution.py:427
  366.1 50.7 %all-to-all-done.3 = bf16[64,16,3200]{2,1,0:T(8,128)(2,1)} async-done(((bf16[64,16,3200]{2,1,0:T(8,128)(2,1)}), bf16[64,16,3200]{2,1,0:T(8,128)(2,1)}, u32[]{:S(2)}, u32[]{:S(2)}) %all-to-all-start.3) | async-done | bytes 6553632 | tf_op jit(solution)/shard_map/all_to_all | solution.py:162
  416.8 14.9 %all-to-all-start.2 = ((bf16[64,16,3072]{2,1,0:T(8,128)(2,1)}), bf16[64,16,3072]{2,1,0:T(8,128)(2,1)}, u32[]{:S(2)}, u32[]{:S(2)}) async-start(bf16[64,16,3072]{2,1,0:T(8,128)(2,1)} %bitcast.30), calls=%async_computation.2 | async-start | bytes 12582912 | tf_op jit(solution)/shard_map/all_to_all | solution.py:162
  431.7 8.8 %reduce-scatter.3.cloned.1.call-start = ((), (), s32[]{:S(2)}) async-start(), calls=%async_computation.8 | async-start | bytes 13381632 | tf_op jit(solution)/shard_map/reduce_scatter | solution.py:97
  440.5 15.2 %shard_map.293 = (bf16[256,1536]{1,0:T(8,128)(2,1)}, bf16[256,1536]{1,0:T(8,128)(2,1)}, bf16[256,1024]{1,0:T(8,128)(2,1)}, f32[256,1536]{1,0:T(8,128)}, bf16[256...) custom-call(bf16[1024,3200]{1,0:T(8,128)(2,1)} %bitcast.16.refs_0_, ...), custom_call_target="tpu_custom_call" | custom-call | tf_op jit(solution)/shard_map/pallas_call | solution.py:736
  455.7 8.3 %shard_map.294.refs_1_ = bf16[768,8448]{1,0:T(8,128)(2,1)} custom-call(bf16[256,1536]{1,0:T(8,128)(2,1)} %get-tuple-element.71.refs_0_, bf16[256,1536]{1,0:T(8,128)(2,1)} %get-tuple-element.72.refs_1_, bf16[256,1536]{1,0:T(8,128)(2,1)} %get-tuple-element.53.ffn_in_ref.refs_2_, bf16[256,1536]{1,0:T(8,128)(2,1)} %get-tuple-element.73.refs_3_, ...), custom_call_target="tpu_custom_call" | custom-call | flops 9999999827968 | tf_op jit(solution)/shard_map/pallas_call | solution.py:804
  466.2 44.5 %all-to-all-done.2 = bf16[64,16,3072]{2,1,0:T(8,128)(2,1)} async-done(((bf16[64,16,3072]{2,1,0:T(8,128)(2,1)}), bf16[64,16,3072]{2,1,0:T(8,128)(2,1)}, u32[]{:S(2)}, u32[]{:S(2)}) %all-to-all-start.2) | async-done | bytes 6291488 | tf_op jit(solution)/shard_map/all_to_all | solution.py:162
  510.7 6.4 %shard_map.292 = bf16[256,1536]{1,0:T(8,128)(2,1)} custom-call(bf16[2,256,1024]{2,1,0:T(8,128)(2,1)} %get-tuple-element.49.turned_ref.refs_2_, bf16[1024,3072]{1,0:T(8,128)(2,1)} %bitcast.14.rows_ref, f32[256,1536]{1,0:T(8,128)} %get-tuple-element.63.base_ref), custom_call_target="tpu_custom_call" | custom-call | flops 9999999827968 | tf_op jit(solution)/shard_map/pallas_call | solution.py:182
  517.3 3.5 collective-permute-done.9
  523.2 14.4 %collective-permute-done.10 = bf16[1536,256]{1,0:T(8,128)(2,1)} collective-permute-done((bf16[1536,256]{1,0:T(8,128)(2,1)}, bf16[1536,256]{1,0:T(8,128)(2,1)}, u32[]{:S(2)}, u32[]{:S(2)}) %collective-permute-start.10) | collective-permute-done | bytes 786464 | tf_op jit(solution)/shard_map/ppermute | solution.py:46
  541.9 3.5 collective-permute-start.7
  546.5 7.9 %collective-permute-done.11 = bf16[256,1536]{1,0:T(8,128)(2,1)S(1)} collective-permute-done((bf16[256,1536]{1,0:T(8,128)(2,1)}, bf16[256,1536]{1,0:T(8,128)(2,1)S(1)}, u32[]{:S(2)}, u32[]{:S(2)}) %collective-permute-start.11) | collective-permute-done | bytes 786464 | tf_op jit(solution)/shard_map/ppermute | solution.py:46
  556.5 3.5 collective-permute-done.7
  560.1 10.1 %reduce-scatter.3.cloned.1.call-done = bf16[24,8448]{1,0:T(8,128)(2,1)} async-done(((bf16[768,8448]{1,0:T(8,128)(2,1)}), bf16[24,8448]{1,0:T(8,128)(2,1)}) %reduce-scatter.3.cloned.1.call-update) | async-done | bytes 405520 | tf_op jit(solution)/shard_map/reduce_scatter | solution.py:97
  577.7 3.3 collective-permute-done.4
  (101 shorter events, 34.7 us)
Async XLA Ops:
  7.2 145.7 %all-gather.5.cloned.1.call-start = ((), (), s32[]{:S(2)}) async-start(), calls=%async_computation.6 | async-start | bytes 13381632 | tf_op jit(solution)/shard_map/all_gather | solution.py:93
  25.9 2.0 copy-start
  25.9 2.0 copy-start.8
  27.0 244.6 %all-gather.7.cloned.1.call-start = ((), (), s32[]{:S(2)}) async-start(), calls=%async_computation.7 | async-start | bytes 9732096 | tf_op jit(solution)/shard_map/all_gather | solution.py:93
  37.6 12.3 %copy-start.3 = (bf16[1,256,1536]{2,1,0:T(8,128)(2,1)S(1)}, bf16[1,256,1536]{2,1,0:T(8,128)(2,1)}, u32[]{:S(2)}) copy-start(bf16[1,256,1536]{2,1,0:T(8,128)(2,1)} %param.33) | copy-start | bytes 2359300
  37.6 134.8 %all-to-all-start.1 = ((bf16[64,16,3200]{2,1,0:T(8,128)(2,1)}), bf16[64,16,3200]{2,1,0:T(8,128)(2,1)}, u32[]{:S(2)}, u32[]{:S(2)}) async-start(bf16[64,16,3200]{2,1,0:T(8,128)(2,1)} %bitcast.34), calls=%async_computation.1 | async-start | bytes 13107200 | tf_op jit(solution)/shard_map/all_to_all | solution.py:162
  46.8 119.1 %collective-permute-start = (bf16[1536,256]{1,0:T(8,128)(2,1)}, bf16[1536,256]{1,0:T(8,128)(2,1)S(1)}, u32[]{:S(2)}, u32[]{:S(2)}) collective-permute-start(bf16[1536,256]{1,0:T(8,128)(2,1)} %bitcast.5.gate_ref), channel_id=1, source_target_pairs={{0,1},{1,0},{2,3},{3,2},{4,5},{5,4},{6,7},{7,6},{8,9},{9,8},{10,11... | collective-permute-start | bytes 2359304 | tf_op jit(solution)/shard_map/ppermute | solution.py:46
  49.8 116.2 %collective-permute-start.1 = (bf16[1536,256]{1,0:T(8,128)(2,1)}, bf16[1536,256]{1,0:T(8,128)(2,1)S(1)}, u32[]{:S(2)}, u32[]{:S(2)}) collective-permute-start(bf16[1536,256]{1,0:T(8,128)(2,1)} %bitcast.6.up_ref), channel_id=1, source_target_pairs={{0,1},{1,0},{2,3},{3,2},{4,5},{5,4},{6,7},{7,6},{8,9},{9,8},{10,11... | collective-permute-start | bytes 2359304 | tf_op jit(solution)/shard_map/ppermute | solution.py:46
  49.9 121.6 %collective-permute-start.2 = (bf16[256,1536]{1,0:T(8,128)(2,1)S(1)}, bf16[256,1536]{1,0:T(8,128)(2,1)S(1)}, u32[]{:S(2)}, u32[]{:S(2)}) collective-permute-start(bf16[256,1536]{1,0:T(8,128)(2,1)S(1)} %bitcast.38), channel_id=1, source_target_pairs={{0,1},{1,0},{2,3},{3,2},{4,5},{5,4},{6,7},{7,6},{8,9},{9,8},{10,11... | collective-permute-start | bytes 2359304 | tf_op jit(solution)/shard_map/ppermute | solution.py:46
  166.0 5.5 copy-start.4
  166.0 5.5 copy-start.5
  171.5 0.9 copy-start.1
  172.4 108.1 %all-to-all-start = ((bf16[64,16,3072]{2,1,0:T(8,128)(2,1)}), bf16[64,16,3072]{2,1,0:T(8,128)(2,1)}, u32[]{:S(2)}, u32[]{:S(2)}) async-start(bf16[64,16,3072]{2,1,0:T(8,128)(2,1)} %bitcast.31), calls=%async_computation | async-start | bytes 12582912 | tf_op jit(solution)/shard_map/all_to_all | solution.py:162
  301.8 115.0 %all-to-all-start.3 = ((bf16[64,16,3200]{2,1,0:T(8,128)(2,1)}), bf16[64,16,3200]{2,1,0:T(8,128)(2,1)}, u32[]{:S(2)}, u32[]{:S(2)}) async-start(bf16[64,16,3200]{2,1,0:T(8,128)(2,1)} %bitcast.35), calls=%async_computation.3 | async-start | bytes 13107200 | tf_op jit(solution)/shard_map/all_to_all | solution.py:162
  313.9 226.2 %reduce-scatter.5.cloned.1.call-start = ((), (), s32[]{:S(2)}) async-start(), calls=%async_computation.9 | async-start | bytes 9732096 | tf_op jit(solution)/shard_map/reduce_scatter | solution.py:97
  416.8 93.9 %all-to-all-start.2 = ((bf16[64,16,3072]{2,1,0:T(8,128)(2,1)}), bf16[64,16,3072]{2,1,0:T(8,128)(2,1)}, u32[]{:S(2)}, u32[]{:S(2)}) async-start(bf16[64,16,3072]{2,1,0:T(8,128)(2,1)} %bitcast.30), calls=%async_computation.2 | async-start | bytes 12582912 | tf_op jit(solution)/shard_map/all_to_all | solution.py:162
  431.7 138.5 %reduce-scatter.3.cloned.1.call-start = ((), (), s32[]{:S(2)}) async-start(), calls=%async_computation.8 | async-start | bytes 13381632 | tf_op jit(solution)/shard_map/reduce_scatter | solution.py:97
  464.1 56.7 %collective-permute-start.9 = (bf16[1536,256]{1,0:T(8,128)(2,1)}, bf16[1536,256]{1,0:T(8,128)(2,1)}, u32[]{:S(2)}, u32[]{:S(2)}) collective-permute-start(bf16[1536,256]{1,0:T(8,128)(2,1)} %shard_map.295), channel_id=1, source_target_pairs={{0,1},{1,0},{2,3},{3,2},{4,5},{5,4},{6,7},{7,6},{8,9},{9,8},{10,11... | collective-permute-start | bytes 2359304 | tf_op jit(solution)/shard_map/ppermute | solution.py:46
  464.6 73.1 %collective-permute-start.10 = (bf16[1536,256]{1,0:T(8,128)(2,1)}, bf16[1536,256]{1,0:T(8,128)(2,1)}, u32[]{:S(2)}, u32[]{:S(2)}) collective-permute-start(bf16[1536,256]{1,0:T(8,128)(2,1)} %shard_map.296), channel_id=1, source_target_pairs={{0,1},{1,0},{2,3},{3,2},{4,5},{5,4},{6,7},{7,6},{8,9},{9,8},{10,11... | collective-permute-start | bytes 2359304 | tf_op jit(solution)/shard_map/ppermute | solution.py:46
  517.1 3.7 copy-start.2
  517.1 20.5 %copy-start.7 = (f32[1536,256]{1,0:T(8,128)S(1)}, f32[1536,256]{1,0:T(8,128)}, u32[]{:S(2)}) copy-start(f32[1536,256]{1,0:T(8,128)} %get-tuple-element.79) | copy-start | bytes 4718596
  517.1 37.3 %collective-permute-start.11 = (bf16[256,1536]{1,0:T(8,128)(2,1)}, bf16[256,1536]{1,0:T(8,128)(2,1)S(1)}, u32[]{:S(2)}, u32[]{:S(2)}) collective-permute-start(bf16[256,1536]{1,0:T(8,128)(2,1)} %shard_map.297), channel_id=1, source_target_pairs={{0,1},{1,0},{2,3},{3,2},{4,5},{5,4},{6,7},{7,6},{8,9},{9,8},{10,11... | collective-permute-start | bytes 2359304 | tf_op jit(solution)/shard_map/ppermute | solution.py:46
  540.1 14.3 %copy-start.6 = (f32[256,1536]{1,0:T(8,128)S(1)}, f32[256,1536]{1,0:T(8,128)}, u32[]{:S(2)}) copy-start(f32[256,1536]{1,0:T(8,128)} %get-tuple-element.81) | copy-start | bytes 4718596
  541.6 14.9 %collective-permute-start.6 = (bf16[12,3072]{1,0:T(8,128)(2,1)S(1)}, bf16[12,3072]{1,0:T(8,128)(2,1)S(1)}, u32[]{:S(2)}, u32[]{:S(2)}) collective-permute-start(bf16[12,3072]{1,0:T(8,128)(2,1)S(1)} %broadcast_select_fusion.9), channel_id=1, source_target_pairs={{0,1},{1,0},{2,3},{3,2},{4,5},{5,4},{6,7},{7,6},{8,9},{9,8},{10,11... | collective-permute-start | bytes 221192 | tf_op jit(solution)/shard_map/ppermute | solution.py:46
  541.9 18.1 %collective-permute-start.7 = (bf16[12,3072]{1,0:T(8,128)(2,1)S(1)}, bf16[12,3072]{1,0:T(8,128)(2,1)S(1)}, u32[]{:S(2)}, u32[]{:S(2)}) collective-permute-start(bf16[12,3072]{1,0:T(8,128)(2,1)S(1)} %get-tuple-element.98), channel_id=1, source_target_pairs={{0,64},{64,0},{1,65},{65,1},{2,66},{66,2},{3,67},{67,3},{4,68},{68... | collective-permute-start | bytes 221192 | tf_op jit(solution)/shard_map/ppermute | solution.py:46
  545.4 14.6 %collective-permute-start.8 = (bf16[12,3072]{1,0:T(8,128)(2,1)S(1)}, bf16[12,3072]{1,0:T(8,128)(2,1)S(1)}, u32[]{:S(2)}, u32[]{:S(2)}) collective-permute-start(bf16[12,3072]{1,0:T(8,128)(2,1)S(1)} %get-tuple-element.99), channel_id=1, source_target_pairs={{0,65},{1,64},{64,1},{65,0},{2,67},{3,66},{66,3},{67,2},{4,69},{5,... | collective-permute-start | bytes 221192 | tf_op jit(solution)/shard_map/ppermute | solution.py:113
  571.3 6.4 %collective-permute-start.3 = (bf16[12,4224]{1,0:T(8,128)(2,1)S(1)}, bf16[12,4224]{1,0:T(8,128)(2,1)S(1)}, u32[]{:S(2)}, u32[]{:S(2)}) collective-permute-start(bf16[12,4224]{1,0:T(8,128)(2,1)S(1)} %broadcast_select_fusion.6), channel_id=1, source_target_pairs={{0,1},{1,0},{2,3},{3,2},{4,5},{5,4},{6,7},{7,6},{8,9},{9,8},{10,11... | collective-permute-start | bytes 304136 | tf_op jit(solution)/shard_map/ppermute | solution.py:46
  573.0 8.1 %collective-permute-start.4 = (bf16[12,4224]{1,0:T(8,128)(2,1)S(1)}, bf16[12,4224]{1,0:T(8,128)(2,1)S(1)}, u32[]{:S(2)}, u32[]{:S(2)}) collective-permute-start(bf16[12,4224]{1,0:T(8,128)(2,1)S(1)} %get-tuple-element.93), channel_id=1, source_target_pairs={{0,64},{64,0},{1,65},{65,1},{2,66},{66,2},{3,67},{67,3},{4,68},{68... | collective-permute-start | bytes 304136 | tf_op jit(solution)/shard_map/ppermute | solution.py:46
  575.8 6.8 %collective-permute-start.5 = (bf16[12,4224]{1,0:T(8,128)(2,1)S(1)}, bf16[12,4224]{1,0:T(8,128)(2,1)S(1)}, u32[]{:S(2)}, u32[]{:S(2)}) collective-permute-start(bf16[12,4224]{1,0:T(8,128)(2,1)S(1)} %get-tuple-element.94), channel_id=1, source_target_pairs={{0,65},{1,64},{64,1},{65,0},{2,67},{3,66},{66,3},{67,2},{4,69},{5,... | collective-permute-start | bytes 304136 | tf_op jit(solution)/shard_map/ppermute | solution.py:113
Sparse Core Ops, SparseCore 0:
  27.1 125.7 all-gather.4
  155.7 115.8 all-gather.6
  321.2 119.9 reduce-scatter.4
  464.2 105.8 reduce-scatter.2
